TPU v7x, 32 devices: a whole 2x2x4 slice. The times are simulated.
32 devices in a mesh: region: 16 (over z, y, x), rays: 2 (over core).
Axes of the slice: x: 2, y: 2, z: 4, core: 2. Of those that a mesh axis runs over, the one named last changes fastest.
Arguments:
- ray_codes: bfloat16 [2, 1024, 128], P(None, 'rays'), may hold values from -6 to 6
- target: bfloat16 [1024, 384], P('rays'), may hold values from -0.19921875 to 1
- direction: int32 [1024], P('rays'), may hold values from 0 to 1
- entries: int32 [16, 1024], P('region', 'rays'), may hold values from 0 to 4
- exits: int32 [16, 1024], P('region', 'rays'), may hold values from 4 to 8
- depth_bins: int32 [16, 8, 1024], P('region', None, 'rays'), may hold values from 0 to 63, as said below
- in_layer: float32 [3, 16, 128, 256], P(None, 'region', 'rays'), as said below
- mid_layer: float32 [3, 16, 256, 256], P(None, 'region', 'rays'), as said below
- feat_layer: float32 [3, 16, 256, 384], P(None, 'region', 'rays'), as said below
- vectors: float32 [3, 16, 1152], P(None, 'region', 'rays'), as said below
Outputs:
- new_in_layer: float32 [3, 16, 128, 256], P(None, 'region', 'rays')
- new_mid_layer: float32 [3, 16, 256, 256], P(None, 'region', 'rays')
- new_feat_layer: float32 [3, 16, 256, 384], P(None, 'region', 'rays')
- new_vectors: float32 [3, 16, 1152], P(None, 'region', 'rays')
- depth_grad: float32 [16, 1024], P('region', 'rays')
Inputs may be any that keep to these rules, and one draw needn't show every extreme that they name: `direction`: 0: the ray meets the regions in increasing index order; 1: in decreasing order. A ray's samples inside a region are the slots j with entries <= j < exits. `depth_bins`: slot j lies in bins j * (8) to (j + 1) * 8 - 1. `in_layer`: the second moments (index 2 of the first dimension) are positive. `mid_layer`: the second moments (index 2 of the first dimension) are positive. `feat_layer`: the second moments (index 2 of the first dimension) are positive. `vectors`: the second moments (index 2 of the first dimension) are positive.
All inputs are finite; a program needn't handle non-finite values.
Results may differ from a plain program's by a relative error of at most 0.0025.
The roundings to bfloat16 on the way count: a program that leaves them out, or rounds other values in their place, can miss the bound.
Values may be sent and summed in bfloat16 or wider, within the bound.
No kernel may reach another device: no remote copies, remote signals or barrier semaphores. Data moves between devices by JAX's collectives and lax.ppermute only.
A program may use at most 64 MiB of HBM per device.

v0:
```python
import jax
import jax.numpy as jnp
from jax import lax
from jax.sharding import PartitionSpec as P

BINS = 64


depth_scale = 4.0
beta_one = 0.9
beta_two = 0.999
learn_rate = 0.001
epsilon = 1e-08
first_fix = 1.0 - 0.9**10
second_fix = 1.0 - 0.999**10


def forward(ray_codes, depth_bins, entry_row, exit_row, weights, unit_length):
    in_weight, mid_weight, feat_weight, vec_weight = weights
    hidden_width = in_weight.shape[1]
    bias_one = vec_weight[:hidden_width].astype(jnp.float32)
    bias_two = vec_weight[hidden_width : 2 * hidden_width].astype(jnp.float32)
    density_weight = vec_weight[2 * hidden_width : 3 * hidden_width]
    bias_feat = vec_weight[3 * hidden_width :].astype(jnp.float32)
    samples, ray_count = depth_bins.shape
    bin_float = depth_bins.astype(jnp.float32)
    following = jnp.concatenate(
        [bin_float[1:], jnp.full((1, ray_count), float(BINS), jnp.float32)], 0
    )
    spacing = (following - bin_float) * unit_length
    position = (bin_float + 0.5) / BINS
    sample_slot = lax.broadcasted_iota(jnp.int32, (samples, ray_count), 0)
    inside = ((sample_slot >= entry_row[None, :]) & (sample_slot < exit_row[None, :])).astype(
        jnp.float32
    )
    codes_float = ray_codes.astype(jnp.float32)
    encoded = (codes_float[0][None] + position[:, :, None] * codes_float[1][None]).astype(
        jnp.bfloat16
    )
    encoded = encoded.reshape(samples * ray_count, codes_float.shape[2])
    hidden_one = jnp.maximum(
        jnp.dot(encoded, in_weight, preferred_element_type=jnp.float32) + bias_one, 0.0
    ).astype(jnp.bfloat16)
    hidden_two = jnp.maximum(
        jnp.dot(hidden_one, mid_weight, preferred_element_type=jnp.float32) + bias_two, 0.0
    ).astype(jnp.bfloat16)
    density_raw = jnp.dot(hidden_two, density_weight, preferred_element_type=jnp.float32).reshape(
        samples, ray_count
    )
    colour = jax.nn.sigmoid(
        jnp.dot(hidden_two, feat_weight, preferred_element_type=jnp.float32) + bias_feat
    )
    colour = colour.reshape(samples, ray_count, feat_weight.shape[1])
    optical = jax.nn.softplus(density_raw) * spacing * inside
    optical_before = jnp.cumsum(optical, 0) - optical
    local_weight = jnp.exp(-optical_before) * -jnp.expm1(-optical)
    return (
        encoded,
        hidden_one,
        hidden_two,
        density_raw,
        colour,
        optical,
        optical_before,
        local_weight,
        spacing,
        inside,
    )


def backward(found, weights, entry_trans, after_sum, feature_grad):
    (
        encoded,
        hidden_one,
        hidden_two,
        density_raw,
        colour,
        optical,
        optical_before,
        local_weight,
        spacing,
        inside,
    ) = found
    in_weight, mid_weight, feat_weight, vec_weight = weights
    hidden_width = in_weight.shape[1]
    density_weight = vec_weight[2 * hidden_width : 3 * hidden_width]
    grad_float = feature_grad.astype(jnp.float32)
    sample_grad = jnp.sum(colour * grad_float[None], -1)
    weighted = local_weight * sample_grad
    later_local = jnp.cumsum(weighted[::-1], 0)[::-1] - weighted
    optical_grad = (
        entry_trans[None] * (jnp.exp(-(optical_before + optical)) * sample_grad - later_local)
        - after_sum[None]
    )
    density_grad = (
        (optical_grad * spacing * inside * jax.nn.sigmoid(density_raw))
        .astype(jnp.bfloat16)
        .reshape(-1)
    )
    colour_grad = (
        (entry_trans[None] * local_weight)[:, :, None] * grad_float[None] * colour * (1.0 - colour)
    ).astype(jnp.bfloat16)
    colour_grad = colour_grad.reshape(-1, colour.shape[2])
    hidden_grad = jnp.dot(colour_grad, feat_weight.T, preferred_element_type=jnp.float32)
    hidden_grad = (
        hidden_grad
        + density_grad.astype(jnp.float32)[:, None] * density_weight.astype(jnp.float32)[None, :]
    )
    second_grad = (hidden_grad * (hidden_two > 0)).astype(jnp.bfloat16)
    first_grad = (
        jnp.dot(second_grad, mid_weight.T, preferred_element_type=jnp.float32) * (hidden_one > 0)
    ).astype(jnp.bfloat16)
    in_grad = jnp.dot(encoded.T, first_grad, preferred_element_type=jnp.float32)
    mid_grad = jnp.dot(hidden_one.T, second_grad, preferred_element_type=jnp.float32)
    feat_grad = jnp.dot(hidden_two.T, colour_grad, preferred_element_type=jnp.float32)
    density_sum = jnp.dot(density_grad, hidden_two, preferred_element_type=jnp.float32)
    vec_grad = jnp.concatenate(
        [
            jnp.sum(first_grad, 0, dtype=jnp.float32),
            jnp.sum(second_grad, 0, dtype=jnp.float32),
            density_sum,
            jnp.sum(colour_grad, 0, dtype=jnp.float32),
        ]
    )
    return (in_grad, mid_grad, feat_grad, vec_grad)


def adam_update(stacked, gradient):
    first_moment = beta_one * stacked[1] + (1.0 - beta_one) * gradient
    second = beta_two * stacked[2] + (1.0 - beta_two) * gradient * gradient
    update_step = first_moment / first_fix / (jnp.sqrt(second / second_fix) + epsilon)
    return jnp.stack([stacked[0] - learn_rate * update_step, first_moment, second])


def side_sums(all_values, own_index):
    region_order = lax.broadcasted_iota(jnp.int32, all_values.shape, 0)
    below_sum = jnp.sum(jnp.where(region_order < own_index, all_values, 0.0), 0)
    above_sum = jnp.sum(jnp.where(region_order > own_index, all_values, 0.0), 0)
    return (below_sum, above_sum)


def per_device(
    ray_codes,
    target,
    direction,
    entries,
    exits,
    depth_bins,
    in_layer,
    mid_layer,
    feat_layer,
    vectors,
):
    pieces = (
        in_layer[0, 0].astype(jnp.bfloat16),
        mid_layer[0, 0].astype(jnp.bfloat16),
        feat_layer[0, 0].astype(jnp.bfloat16),
        vectors[0, 0].astype(jnp.bfloat16),
    )
    weights = (
        lax.all_gather(pieces[0], "rays", axis=0, tiled=True),
        lax.all_gather(pieces[1], "rays", axis=0, tiled=True),
        lax.all_gather(pieces[2], "rays", axis=0, tiled=True),
        lax.all_gather(pieces[3], "rays", axis=0, tiled=True),
    )
    regions = lax.axis_size("region")
    found = forward(
        ray_codes, depth_bins[0], entries[0], exits[0], weights, depth_scale / (regions * BINS)
    )
    colour, optical, local_weight = (found[4], found[5], found[7])
    depth = jnp.sum(optical, 0)
    local_partial = jnp.sum(local_weight[:, :, None] * colour, 0)
    onward = direction == 0
    all_depth = lax.all_gather(depth[None], "region", axis=0, tiled=True)
    below_depth, above_depth = side_sums(all_depth, lax.axis_index("region"))
    entry_trans = jnp.exp(-jnp.where(onward, below_depth, above_depth))
    contribution = entry_trans[:, None] * local_partial
    rendered = lax.psum(contribution, "region")
    feature_grad = (rendered - target.astype(jnp.float32)).astype(jnp.bfloat16)
    region_grad = entry_trans * jnp.sum(feature_grad.astype(jnp.float32) * local_partial, -1)
    all_grad = lax.all_gather(region_grad[None], "region", axis=0, tiled=True)
    below_grad, above_grad = side_sums(all_grad, lax.axis_index("region"))
    after_sum = jnp.where(onward, above_grad, below_grad)
    in_grad, mid_grad, feat_grad, vec_grad = backward(
        found, weights, entry_trans, after_sum, feature_grad
    )
    in_share, mid_share, feat_share, vec_share = (
        lax.psum_scatter(in_grad, "rays", scatter_dimension=0, tiled=True),
        lax.psum_scatter(mid_grad, "rays", scatter_dimension=0, tiled=True),
        lax.psum_scatter(feat_grad, "rays", scatter_dimension=0, tiled=True),
        lax.psum_scatter(vec_grad, "rays", scatter_dimension=0, tiled=True),
    )
    return (
        adam_update(in_layer[:, 0], in_share)[:, None],
        adam_update(mid_layer[:, 0], mid_share)[:, None],
        adam_update(feat_layer[:, 0], feat_share)[:, None],
        adam_update(vectors[:, 0], vec_share)[:, None],
        (-after_sum)[None],
    )


def solution(mesh):
    placed = (
        P(None, "rays", None),
        P("rays", None),
        P("rays"),
        P("region", "rays"),
        P("region", "rays"),
        P("region", None, "rays"),
        P(None, "region", "rays", None),
        P(None, "region", "rays", None),
        P(None, "region", "rays", None),
        P(None, "region", "rays"),
    )
    return jax.shard_map(
        per_device,
        mesh=mesh,
        in_specs=placed,
        out_specs=(
            P(None, "region", "rays", None),
            P(None, "region", "rays", None),
            P(None, "region", "rays", None),
            P(None, "region", "rays"),
            P("region", "rays"),
        ),
        check_vma=False,
    )
```

profile of v0, /device:TPU:0, one launch (start us, length us, event | category | flops | bytes accessed | tf_op | source)
XLA Modules:
  0.0 273.6 jit_solution(1729665506876578495)
XLA Ops:
  7.2 1.3 multiply_reduce_fusion.3
  8.6 1.3 fusion.41
  10.8 2.6 all-reduce.1
  13.4 0.5 slice_convert_fusion.3
  13.9 0.7 multiply_bitcast_fusion.1
  14.6 0.7 convert_element_type.91
  15.4 0.8 bitcast_convert_fusion.2
  16.3 1.8 all_gather.18
  18.1 0.9 bitcast_convert_fusion.1
  19.0 1.9 all_gather.20
  20.9 1.0 bitcast_convert_fusion
  21.9 1.9 all_gather.22
  23.9 1.0 convert_element_type.90
  24.9 0.7 fusion.12
  25.6 0.7 fusion.8
  26.6 0.7 fusion.10
  27.4 0.6 copy-done.29
  27.9 0.6 fusion.42
  28.6 42.4 %all-gather.2 = f32[16,1,512]{2,1,0:T(1,128)S(1)} all-gather(f32[1,1,512]{2,1,0:T(1,128)S(1)} %bitcast.185), channel_id=2, replica_groups=mesh['region'=16,'rays'=2] {'region'}, dimensions={0}, use_global_device_ids=true | all-gather | bytes 34816 | tf_op jit(solution)/shard_map/all_gather | solution.py:174
  71.2 0.6 negate_exponential_fusion
  71.8 0.6 multiply_bitcast_fusion
  72.4 1.8 add_divide_fusion
  74.3 0.8 multiply_reduce_fusion
  75.1 1.8 copy-done
  76.9 1.0 broadcast_multiply_fusion
  78.0 1.3 copy.24
  80.0 104.3 %all-reduce.5.cloned.1.call-done = f32[512,384]{1,0:T(8,128)} async-done(((f32[512,384]{1,0:T(8,128)}), f32[512,384]{1,0:T(8,128)}) %all-reduce.5.cloned.1.call-update) | async-done | bytes 786448 | tf_op jit(solution)/shard_map/psum | solution.py:178
  184.3 1.3 multiply_reduce_fusion.1
  185.6 0.7 mul.299
  186.3 5.0 %convert_reduce_fusion = (f32[384]{0:T(512)S(1)}, bf16[4096,384]{1,0:T(8,128)(2,1)}, f32[4096]{0:T(1024)S(1)}) fusion(f32[4096,384]{1,0:T(8,128)} %copy-done, f32[512,384]{1,0:T(8,128)S(1)} %get-tuple-element.30, f32[4096]{0:T(1024)} %bitcast.175), kind=kLoop, calls=%fused_computation.6 | loop fusion | flops 14151296 | bytes 10257920 | tf_op jit(solution)/shard_map/reduce_sum | solution.py:122
  191.6 38.8 %all-gather.3 = f32[16,1,512]{2,1,0:T(1,128)S(1)} all-gather(f32[1,1,512]{2,1,0:T(1,128)S(1)} %bitcast.184), channel_id=3, replica_groups=mesh['region'=16,'rays'=2] {'region'}, dimensions={0}, use_global_device_ids=true | all-gather | bytes 34816 | tf_op jit(solution)/shard_map/all_gather | solution.py:181
  230.5 0.6 fusion.35
  231.6 3.3 %convert_reduce_fusion.1 = (f32[256]{0:T(256)S(1)}, bf16[4096,256]{1,0:T(8,128)(2,1)S(1)}) fusion(f32[256]{0:T(256)S(1)} %copy-done.28, f32[4096]{0:T(1024)S(1)} %convert_element_type.108, bf16[4096,384]{1,0:T(8,128)(2,1)} %get-tuple-element.28, bf16[256,384]{1,0:T(8,128)(2,1)S(1)} %all_gather.22, bf16[4096,256]{1,0:T(8,128)(2,1)S(1)} %fusion.10), kind=kOutput, calls=%fused_computation.20 | convolution fusion | flops 812646144 | bytes 7555072 | tf_op jit(solution)/shard_map/dot_general | solution.py:104
  235.0 1.0 convert_reduce_fusion.2
  236.3 0.7 copy-done.2
  237.0 1.2 fusion.43
  238.2 2.5 all-reduce.2
  240.7 3.7 %fusion.44 = f32[256,256]{1,0:T(8,128)} fusion(bf16[4096,256]{1,0:T(8,128)(2,1)} %copy-done.29, bf16[4096,256]{1,0:T(8,128)(2,1)} %copy-done.31), kind=kOutput, calls=%fused_computation.101 | convolution fusion | flops 536870912 | bytes 4456448 | tf_op jit(solution)/shard_map/dot_general | solution.py:114
  244.7 4.0 %fusion.45 = f32[256,384]{1,0:T(8,128)} fusion(bf16[4096,256]{1,0:T(8,128)(2,1)S(1)} %fusion.10, bf16[4096,384]{1,0:T(8,128)(2,1)} %get-tuple-element.28), kind=kOutput, calls=%fused_computation.102 | convolution fusion | flops 805306368 | bytes 5636096 | tf_op jit(solution)/shard_map/dot_general | solution.py:115
  248.7 0.6 broadcast_in_dim.49
  249.3 0.9 fusion.19
  250.2 0.7 maximum_bitcast_fusion.2
  250.9 2.5 reduce-scatter.6.cloned.1.call-done
  253.4 1.0 fusion.17
  254.4 0.8 maximum_bitcast_fusion.1
  255.2 10.0 %reduce-scatter.8.cloned.1.call-done = f32[128,384]{1,0:T(8,128)} async-done(((f32[256,384]{1,0:T(8,128)}), f32[128,384]{1,0:T(8,128)}) %reduce-scatter.8.cloned.1.call-update) | async-done | bytes 196624 | tf_op jit(solution)/shard_map/reduce_scatter | solution.py:190
  265.1 1.1 fusion.15
  266.2 0.9 maximum_bitcast_fusion
  (100 shorter events, 2.3 us)
Async XLA Ops:
  7.2 177.1 %all-reduce.5.cloned.1.call-start = ((), (), s32[]{:S(2)}) async-start(), calls=%async_computation.3 | async-start | bytes 1572864 | tf_op jit(solution)/shard_map/psum | solution.py:178
  8.6 6.8 %copy-start.14 = (f32[576]{0:T(1024)}, f32[576]{0:T(1024)S(1)}, u32[]{:S(2)}) copy-start(f32[576]{0:T(1024)S(1)} %get-tuple-element.20) | copy-start | bytes 6916
  15.4 55.7 %copy-start.22 = (pred[16]{0:T(512)(128)(4,1)}, pred[16]{0:T(512)(128)(4,1)S(1)}, u32[]{:S(2)}) copy-start(pred[16]{0:T(512)(128)(4,1)S(1)} %get-tuple-element.59) | copy-start | bytes 52
  15.4 55.7 %copy-start.24 = (pred[16]{0:T(512)(128)(4,1)}, pred[16]{0:T(512)(128)(4,1)S(1)}, u32[]{:S(2)}) copy-start(pred[16]{0:T(512)(128)(4,1)S(1)} %get-tuple-element.60) | copy-start | bytes 52
  20.9 5.7 %copy-start.10 = (bf16[256,256]{1,0:T(8,128)(2,1)}, bf16[256,256]{1,0:T(8,128)(2,1)S(1)}, u32[]{:S(2)}) copy-start(bf16[256,256]{1,0:T(8,128)(2,1)S(1)} %all_gather.20) | copy-start | bytes 393220
  25.6 1.0 copy-start.1
  26.6 1.3 copy-start.29
  26.6 2.0 copy-start.7
  26.6 2.0 copy-start.18
  26.6 2.0 copy-start.20
  26.6 44.6 %copy-start.26 = (s32[512]{0:T(512)S(1)}, s32[512]{0:T(512)}, u32[]{:S(2)}) copy-start(s32[512]{0:T(512)} %param.12) | copy-start | bytes 6148
  71.1 3.1 %copy-start.8 = (f32[8,512]{1,0:T(8,128)}, f32[8,512]{1,0:T(8,128)S(1)}, u32[]{:S(2)}) copy-start(f32[8,512]{1,0:T(8,128)S(1)} %reduce_window_sum.17) | copy-start | bytes 49156
  71.8 3.2 %copy-start.12 = (f32[512]{0:T(512)}, f32[512]{0:T(512)S(1)}, u32[]{:S(2)}) copy-start(f32[512]{0:T(512)S(1)} %get-tuple-element.33) | copy-start | bytes 6148
  74.2 2.7 copy-start
  74.3 110.0 %copy-start.5 = (bf16[512,384]{1,0:T(8,128)(2,1)S(1)}, bf16[512,384]{1,0:T(8,128)(2,1)}, u32[]{:S(2)}) copy-start(bf16[512,384]{1,0:T(8,128)(2,1)} %param.11) | copy-start | bytes 1179652
  77.9 171.4 %reduce-scatter.4.cloned.1.call-start = ((), (), s32[]{:S(2)}) async-start(), calls=%async_computation.4 | async-start | bytes 196608 | tf_op jit(solution)/shard_map/reduce_scatter | solution.py:188
  186.3 44.1 %copy-start.23 = (pred[16]{0:T(512)(128)(4,1)S(1)}, pred[16]{0:T(512)(128)(4,1)}, u32[]{:S(2)}) copy-start(pred[16]{0:T(512)(128)(4,1)} %copy-done.22) | copy-start | bytes 52
  186.3 44.1 %copy-start.25 = (pred[16]{0:T(512)(128)(4,1)S(1)}, pred[16]{0:T(512)(128)(4,1)}, u32[]{:S(2)}) copy-start(pred[16]{0:T(512)(128)(4,1)} %copy-done.24) | copy-start | bytes 52
  186.3 44.2 %copy-start.27 = (pred[512]{0:T(512)(128)(4,1)S(1)}, pred[512]{0:T(512)(128)(4,1)}, u32[]{:S(2)}) copy-start(pred[512]{0:T(512)(128)(4,1)} %get-tuple-element.34) | copy-start | bytes 1540
  186.3 44.8 %copy-start.9 = (f32[8,512]{1,0:T(8,128)S(1)}, f32[8,512]{1,0:T(8,128)}, u32[]{:S(2)}) copy-start(f32[8,512]{1,0:T(8,128)} %copy-done.8) | copy-start | bytes 49156
  186.3 44.8 %copy-start.13 = (f32[512]{0:T(512)S(1)}, f32[512]{0:T(512)}, u32[]{:S(2)}) copy-start(f32[512]{0:T(512)} %copy-done.12) | copy-start | bytes 6148
  186.3 44.8 %copy-start.19 = (s32[1,512]{1,0:T(1,128)S(1)}, s32[1,512]{1,0:T(1,128)}, u32[]{:S(2)}) copy-start(s32[1,512]{1,0:T(1,128)} %param.14) | copy-start | bytes 6148
  186.3 44.8 %copy-start.21 = (s32[1,512]{1,0:T(1,128)S(1)}, s32[1,512]{1,0:T(1,128)}, u32[]{:S(2)}) copy-start(s32[1,512]{1,0:T(1,128)} %param.13) | copy-start | bytes 6148
  186.3 45.3 %copy-start.28 = (f32[256]{0:T(256)S(1)}, f32[256]{0:T(256)}, u32[]{:S(2)}) copy-start(f32[256]{0:T(256)} %get-tuple-element.49) | copy-start | bytes 3076
  231.6 3.4 %copy-start.11 = (bf16[256,256]{1,0:T(8,128)(2,1)S(1)}, bf16[256,256]{1,0:T(8,128)(2,1)}, u32[]{:S(2)}) copy-start(bf16[256,256]{1,0:T(8,128)(2,1)} %copy-done.10) | copy-start | bytes 393220
  231.6 3.4 %copy-start.30 = (bf16[4096,256]{1,0:T(8,128)(2,1)S(1)}, bf16[4096,256]{1,0:T(8,128)(2,1)}, u32[]{:S(2)}) copy-start(bf16[4096,256]{1,0:T(8,128)(2,1)} %copy-done.29) | copy-start | bytes 6291460
  235.0 1.4 copy-start.31
  235.0 2.0 copy-start.2
  238.1 6.4 %copy-start.15 = (f32[576]{0:T(1024)S(1)}, f32[576]{0:T(1024)}, u32[]{:S(2)}) copy-start(f32[576]{0:T(1024)} %copy-done.14) | copy-start | bytes 6916
  238.1 6.4 %copy-start.16 = (f32[576]{0:T(1024)S(1)}, f32[576]{0:T(1024)}, u32[]{:S(2)}) copy-start(f32[576]{0:T(1024)} %get-tuple-element.19) | copy-start | bytes 6916
  238.1 6.4 %copy-start.17 = (f32[576]{0:T(1024)S(1)}, f32[576]{0:T(1024)}, u32[]{:S(2)}) copy-start(f32[576]{0:T(1024)} %get-tuple-element.21) | copy-start | bytes 6916
  238.2 15.2 %reduce-scatter.6.cloned.1.call-start = ((), (), s32[]{:S(2)}) async-start(), calls=%async_computation.5 | async-start | bytes 393216 | tf_op jit(solution)/shard_map/reduce_scatter | solution.py:189
  244.4 20.7 %reduce-scatter.8.cloned.1.call-start = ((), (), s32[]{:S(2)}) async-start(), calls=%async_computation.6 | async-start | bytes 589824 | tf_op jit(solution)/shard_map/reduce_scatter | solution.py:190
  244.6 4.7 %copy-start.6 = (f32[3,1,64,256]{3,2,1,0:T(8,128)S(1)}, f32[3,1,64,256]{3,2,1,0:T(8,128)}, u32[]{:S(2)}) copy-start(f32[3,1,64,256]{3,2,1,0:T(8,128)} %param.16) | copy-start | bytes 589828
  244.7 8.7 %copy-start.4 = (f32[3,1,128,256]{3,2,1,0:T(8,128)S(1)}, f32[3,1,128,256]{3,2,1,0:T(8,128)}, u32[]{:S(2)}) copy-start(f32[3,1,128,256]{3,2,1,0:T(8,128)} %param.17) | copy-start | bytes 1179652
  248.7 16.5 %copy-start.3 = (f32[3,1,128,384]{3,2,1,0:T(8,128)S(1)}, f32[3,1,128,384]{3,2,1,0:T(8,128)}, u32[]{:S(2)}) copy-start(f32[3,1,128,384]{3,2,1,0:T(8,128)} %param.18) | copy-start | bytes 1769476
Sparse Core Ops, SparseCore 0:
  78.1 106.1 all-reduce.4
  238.3 3.3 reduce-scatter.3
  244.6 8.7 reduce-scatter.5
  256.1 8.9 reduce-scatter.7
where the time goes:
time: 274 us
  waiting for transfers between devices  117 us (43%)
  blocking collectives  92 us (34%)
  other arithmetic  21.4 us (8%)
  matrix products  17.4 us (6%)
  between operations  15.5 us (6%)
  local copies, waits for them, and re-layouts  10.3 us (4%)
    psum x1, waiting for transfers between devices, per_device(): rendered = lax.psum(contribution, 'region')  104 us
    all_gather x1, blocking collectives, per_device(): all_depth = lax.all_gather(depth[None], 'region', axis=0, tiled=True)  42.4 us
    all_gather x1, blocking collectives, per_device(): all_grad = lax.all_gather(region_grad[None], 'region', axis=0, tiled=True)  38.8 us
    reduce_scatter x1, waiting for transfers between devices, per_device(): lax.psum_scatter(feat_grad, 'rays', scatter_dimension=0, tiled=True)  9.95 us
    unnamed x71, local copies, waits for them, and re-layouts  6.67 us
  transfers between devices with their start and end apart: 4, of which 3 were waited for; matrix products, arithmetic and copies ran while one was open for 5% of the time, Pallas kernels for 0%

commit v1 on v0

v1 whole, which is shorter than its diff:
```python
import functools

import jax
import jax.numpy as jnp
from jax import lax
from jax.experimental import pallas as pl
from jax.experimental.pallas import tpu as pltpu
from jax.sharding import PartitionSpec as P

BINS = 64
LANES = 128

depth_scale = 4.0
beta_one = 0.9
beta_two = 0.999
learn_rate = 0.001
epsilon = 1e-08
first_fix = 1.0 - 0.9**10
second_fix = 1.0 - 0.999**10

f32 = jnp.float32
bf16 = jnp.bfloat16
LIMIT = 48 * 1024 * 1024


def whole():
    return pl.BlockSpec(memory_space=pltpu.VMEM)


def call(body, out_shape, n_in, scratch=(), limit=LIMIT, flops=1000000, moved=1000000):
    many = isinstance(out_shape, (tuple, list))
    return pl.pallas_call(
        body,
        out_shape=out_shape,
        in_specs=[whole()] * n_in,
        out_specs=tuple(whole() for _ in out_shape) if many else whole(),
        scratch_shapes=list(scratch),
        compiler_params=pltpu.CompilerParams(vmem_limit_bytes=limit),
        cost_estimate=pl.CostEstimate(flops=flops, bytes_accessed=moved, transcendentals=0),
    )


def blocks(width):
    return [slice(LANES * k, LANES * (k + 1)) for k in range(width // LANES)]


def wide_rows(count):
    return -(-count // LANES)


def row_block(row, rows):
    width = row.shape[1]
    padded = wide_rows(width) * LANES
    if padded != width:
        row = jnp.concatenate([row, jnp.zeros((1, padded - width), f32)], 1)
    place = lax.broadcasted_iota(jnp.int32, (rows, LANES), 0)
    out = jnp.zeros((rows, LANES), f32)
    for k, cut in enumerate(blocks(padded)):
        out = jnp.where(place == k, jnp.broadcast_to(row[:, cut], (rows, LANES)), out)
    return out


def block_row(block, count):
    return jnp.concatenate([block[k : k + 1] for k in range(count)], 1)


def split3(value):
    high = value.astype(bf16).astype(f32)
    rest = value - high
    mid = rest.astype(bf16).astype(f32)
    return (high, mid, rest - mid)


def lanes_of(shape):
    return lax.broadcasted_iota(jnp.int32, shape, 1)


def turned(rows, ray_count):
    fill = LANES - rows.shape[0]
    return jnp.concatenate([rows, jnp.zeros((fill, ray_count), f32)], 0).T


def fold(extra, own_rows, regions):
    fold_rows = min(own_rows, 16)
    groups = own_rows // fold_rows
    extra = extra.reshape(regions, own_rows, LANES)
    out = extra[:, :fold_rows]
    for g in range(1, groups):
        piece = extra[:, fold_rows * g : fold_rows * (g + 1)].reshape(regions * fold_rows, LANES)
        piece = pltpu.roll(piece, (LANES // groups) * g, 1)
        out = out + piece.reshape(regions, fold_rows, LANES)
    return out


def unfold(folded, own_rows, used):
    regions, fold_rows, _ = folded.shape
    groups = own_rows // fold_rows
    flat = folded.reshape(regions * fold_rows, LANES)
    keep = lanes_of(flat.shape) < used
    parts = []
    for g in range(groups):
        piece = flat if g == 0 else pltpu.roll(flat, LANES - (LANES // groups) * g, 1)
        parts.append(jnp.where(keep, piece, 0.0).reshape(regions, fold_rows, LANES))
    return jnp.concatenate(parts, 1) if groups > 1 else parts[0]


def pack_body(in_ref, mid_ref, feat_ref, vec_ref, out_ref):
    spot = 0
    for ref in (in_ref, mid_ref, feat_ref):
        rows, width = ref.shape[2:]
        for cut in blocks(width):
            out_ref[spot : spot + rows, :] = ref[0, 0, :, cut].astype(bf16)
            spot += rows
    out_ref[spot : spot + 16, :] = row_block(vec_ref[0], 16).astype(bf16)


def forward_body(
    pack_ref,
    codes_ref,
    bins_ref,
    entry_ref,
    exit_ref,
    send_ref,
    enc_ref,
    one_ref,
    two_ref,
    colour_ref,
    scalar_ref,
    mid_ref,
    head_ref,
    *,
    shapes,
    vec_share,
    regions,
):
    shards = pack_ref.shape[0]
    samples, ray_count = bins_ref.shape
    own_rows = ray_count // regions
    in_rows, hidden = shapes[0]
    mid_rows = shapes[1][0]
    feat_rows, feat = shapes[2]
    spot = 0
    mats = []
    for rows, width in shapes:
        pieces = []
        for cut in blocks(width):
            pieces.append(
                jnp.concatenate([pack_ref[s, spot : spot + rows, :] for s in range(shards)], 0)
            )
            spot += rows
        mats.append(jnp.concatenate(pieces, 1))
    in_weight, mid_weight, feat_weight = mats
    vec_total = vec_share * shards
    vec = jnp.zeros((1, vec_total), f32)
    for s in range(shards):
        block = pack_ref[s, spot : spot + 16, :].astype(f32)
        count = wide_rows(vec_share)
        row = block_row(block, count)
        fill = vec_total - count * LANES
        if fill:
            row = jnp.concatenate([row, jnp.zeros((1, fill), f32)], 1)
        if s:
            row = pltpu.roll(row, vec_share * s, 1)
        vec = vec + row
    bias_one = vec[:, :hidden]
    bias_two = vec[:, hidden : 2 * hidden]
    density_row = vec[:, 2 * hidden : 3 * hidden]
    bias_feat = vec[:, 3 * hidden :]
    density_cols = jnp.broadcast_to(density_row, (LANES, hidden)).T
    mid_ref[...] = mid_weight
    head_ref[...] = jnp.concatenate([feat_weight, density_cols.astype(bf16)], 1)

    bins = bins_ref[...].astype(f32)
    slot = lax.broadcasted_iota(jnp.int32, bins.shape, 0)
    following = jnp.where(slot == samples - 1, float(BINS), pltpu.roll(bins, samples - 1, 0))
    spacing = (following - bins) * (depth_scale / (regions * BINS))
    inside = ((slot >= entry_ref[...]) & (slot < exit_ref[...])).astype(f32)
    position = turned((bins + 0.5) / BINS, ray_count)
    code_zero = codes_ref[0].astype(f32)
    code_one = codes_ref[1].astype(f32)
    density = jnp.zeros((ray_count, LANES), f32)
    lane = lanes_of((hidden, LANES))
    for j in range(samples):
        rows = slice(ray_count * j, ray_count * (j + 1))
        encoded = (code_zero + position[:, j : j + 1] * code_one).astype(bf16)
        enc_ref[rows, :] = encoded
        one = jnp.dot(encoded, in_weight, preferred_element_type=f32) + bias_one
        one = jnp.maximum(one, 0.0).astype(bf16)
        one_ref[rows, :] = one
        two = jnp.dot(one, mid_weight, preferred_element_type=f32) + bias_two
        two = jnp.maximum(two, 0.0).astype(bf16)
        two_ref[rows, :] = two
        head = jnp.concatenate(
            [feat_weight, jnp.where(lane == j, density_cols, 0.0).astype(bf16)], 1
        )
        raw = jnp.dot(two, head, preferred_element_type=f32)
        density = density + raw[:, feat:]
        colour_ref[rows, :] = 0.5 * jnp.tanh(0.5 * (raw[:, :feat] + bias_feat)) + 0.5
    density = density.T[:samples]
    soft = jnp.maximum(density, 0.0) + jnp.log1p(jnp.exp(-jnp.abs(density)))
    optical = soft * spacing * inside
    before = [jnp.zeros((1, ray_count), f32)]
    for j in range(samples):
        before.append(before[-1] + optical[j : j + 1])
    depth = before.pop()
    optical_before = jnp.concatenate(before, 0)
    local_weight = jnp.exp(-optical_before) * (jnp.tanh(0.5 * optical) * (1.0 + jnp.exp(-optical)))
    sig = 0.5 * jnp.tanh(0.5 * density) + 0.5
    scalar_ref[0] = local_weight
    scalar_ref[1] = jnp.exp(-(optical_before + optical))
    scalar_ref[2] = spacing * inside * sig
    columns = turned(jnp.concatenate([*split3(depth), local_weight], 0), ray_count)
    total = jnp.zeros((ray_count, feat), f32)
    for j in range(samples):
        rows = slice(ray_count * j, ray_count * (j + 1))
        total = total + columns[:, 3 + j : 4 + j] * colour_ref[rows, :]
    extra = jnp.where(lanes_of(columns.shape) < 3, columns, 0.0)
    parts = [total[:, cut].reshape(regions, own_rows, LANES) for cut in blocks(feat)]
    parts.append(fold(extra, own_rows, regions))
    send_ref[...] = jnp.concatenate(parts, 1).astype(bf16)


def owner_body(got_ref, target_ref, direction_ref, out_ref):
    regions = got_ref.shape[0]
    own_rows, feat = target_ref.shape
    cuts = blocks(feat)
    got = got_ref[...].astype(f32)
    extra = unfold(got[:, own_rows * len(cuts) :], own_rows, 3)
    depth = [jnp.sum(extra[q], 1, keepdims=True) for q in range(regions)]
    onward = direction_ref[...] == 0

    def side(values):
        below, above = ([jnp.zeros_like(values[0])], [jnp.zeros_like(values[0])])
        for q in range(regions - 1):
            below.append(below[-1] + values[q])
            above.append(above[-1] + values[regions - 1 - q])
        return (below, above[::-1])

    below, above = side(depth)
    trans = [jnp.exp(-jnp.where(onward, below[q], above[q])) for q in range(regions)]

    def part(q, k):
        return got[q, own_rows * k : own_rows * (k + 1)]

    grads = []
    for k, cut in enumerate(cuts):
        rendered = trans[0] * part(0, k)
        for q in range(1, regions):
            rendered = rendered + trans[q] * part(q, k)
        grads.append((rendered - target_ref[:, cut].astype(f32)).astype(bf16).astype(f32))
    region_grad = []
    for q in range(regions):
        product = grads[0] * part(q, 0)
        for k in range(1, len(cuts)):
            product = product + grads[k] * part(q, k)
        region_grad.append(trans[q] * jnp.sum(product, 1, keepdims=True))
    below, above = side(region_grad)
    lane = lanes_of((own_rows, LANES))
    for q in range(regions):
        after = jnp.where(onward, above[q], below[q])
        extra = jnp.zeros((own_rows, LANES), f32)
        for i, piece in enumerate((*split3(trans[q]), *split3(after))):
            extra = jnp.where(lane == i, piece, extra)
        out_ref[q] = jnp.concatenate([*grads, fold(extra, own_rows, 1)[0]], 0).astype(bf16)


def over_rows(left, right):
    return lax.dot_general(left, right, (((0,), (0,)), ((), ())), preferred_element_type=f32)


def across(left, right):
    return lax.dot_general(left, right, (((1,), (1,)), ((), ())), preferred_element_type=f32)


def backward_body(
    got_ref,
    enc_ref,
    one_ref,
    two_ref,
    colour_ref,
    scalar_ref,
    mid_ref,
    head_ref,
    out_ref,
    depth_ref,
    head_grad_ref,
    second_ref,
    first_ref,
    *,
    shapes,
    vec_share,
    shards,
):
    regions = got_ref.shape[0]
    samples, ray_count = scalar_ref.shape[1:]
    own_rows = ray_count // regions
    hidden = mid_ref.shape[0]
    feat = colour_ref.shape[1]
    cuts = blocks(feat)
    got = got_ref[...].astype(f32)
    grad = jnp.concatenate(
        [
            got[:, own_rows * k : own_rows * (k + 1)].reshape(ray_count, LANES)
            for k in range(len(cuts))
        ],
        1,
    )
    extra = unfold(got[:, own_rows * len(cuts) :], own_rows, 6).reshape(ray_count, LANES).T
    trans = extra[0:1] + extra[1:2] + extra[2:3]
    after = extra[3:4] + extra[4:5] + extra[5:6]
    depth_ref[...] = -after
    lane = lanes_of((ray_count, LANES))
    sample_grad = jnp.zeros((ray_count, LANES), f32)
    for j in range(samples):
        rows = slice(ray_count * j, ray_count * (j + 1))
        product = jnp.sum(colour_ref[rows, :] * grad, 1, keepdims=True)
        sample_grad = jnp.where(lane == j, product, sample_grad)
    sample_grad = sample_grad.T[:samples]
    local_weight = scalar_ref[0]
    weighted = local_weight * sample_grad
    later = [jnp.zeros((1, ray_count), f32)]
    for j in range(samples - 1, 0, -1):
        later.append(later[-1] + weighted[j : j + 1])
    later = jnp.concatenate(later[::-1], 0)
    optical_grad = trans * (scalar_ref[1] * sample_grad - later) - after
    density_grad = optical_grad * scalar_ref[2]
    columns = turned(jnp.concatenate([trans * local_weight, density_grad], 0), ray_count)
    first_sum = jnp.zeros((1, hidden), f32)
    second_sum = jnp.zeros((1, hidden), f32)
    colour_sum = jnp.zeros((1, feat), f32)
    for j in range(samples):
        rows = slice(ray_count * j, ray_count * (j + 1))
        colour = colour_ref[rows, :]
        colour_grad = (columns[:, j : j + 1] * grad * colour * (1.0 - colour)).astype(bf16)
        density_part = jnp.where(lane == samples + j, columns, 0.0).astype(bf16)
        head_grad = jnp.concatenate([colour_grad, density_part], 1)
        head_grad_ref[rows, :] = head_grad
        hidden_grad = across(head_grad, head_ref[...])
        second = jnp.where(two_ref[rows, :].astype(f32) > 0, hidden_grad, 0.0).astype(bf16)
        second_ref[rows, :] = second
        below = across(second, mid_ref[...])
        first = jnp.where(one_ref[rows, :].astype(f32) > 0, below, 0.0).astype(bf16)
        first_ref[rows, :] = first
        colour_sum = colour_sum + jnp.sum(colour_grad.astype(f32), 0, keepdims=True)
        second_sum = second_sum + jnp.sum(second.astype(f32), 0, keepdims=True)
        first_sum = first_sum + jnp.sum(first.astype(f32), 0, keepdims=True)
    in_grad = over_rows(enc_ref[...], first_ref[...])
    mid_grad = over_rows(one_ref[...], second_ref[...])
    head_grad = over_rows(two_ref[...], head_grad_ref[...])
    density_sum = jnp.sum(head_grad[:, feat:].T, 0, keepdims=True)
    vec = jnp.concatenate([first_sum, second_sum, density_sum, colour_sum], 1)
    spot = 0
    for (rows, width), value in zip(shapes, (in_grad, mid_grad, head_grad)):
        for cut in blocks(width):
            for s in range(shards):
                out_ref[s, spot : spot + rows, :] = value[rows * s : rows * (s + 1), cut]
            spot += rows
    total = vec.shape[1]
    for s in range(shards):
        row = pltpu.roll(vec, total - vec_share * s, 1) if s else vec
        out_ref[s, spot : spot + 16, :] = row_block(row[:, : wide_rows(vec_share) * LANES], 16)


def adam_body(grad_ref, *refs):
    state_refs, out_refs = (refs[:4], refs[4:])

    def update(stacked, gradient):
        first_moment = beta_one * stacked[1] + (1.0 - beta_one) * gradient
        second = beta_two * stacked[2] + (1.0 - beta_two) * gradient * gradient
        step = first_moment / first_fix / (jnp.sqrt(second / second_fix) + epsilon)
        return (stacked[0] - learn_rate * step, first_moment, second)

    shards = grad_ref.shape[0]
    spot = 0
    for ref, out in zip(state_refs[:3], out_refs[:3]):
        rows, width = ref.shape[2:]
        for cut in blocks(width):
            gradient = grad_ref[0, spot : spot + rows, :]
            for s in range(1, shards):
                gradient = gradient + grad_ref[s, spot : spot + rows, :]
            spot += rows
            new = update([ref[i, 0, :, cut] for i in range(3)], gradient)
            for i in range(3):
                out[i, 0, :, cut] = new[i]
    ref, out = (state_refs[3], out_refs[3])
    share = ref.shape[2]
    block = grad_ref[0, spot : spot + 16, :]
    for s in range(1, shards):
        block = block + grad_ref[s, spot : spot + 16, :]
    gradient = block_row(block, wide_rows(share))[:, :share]
    new = update([ref[i] for i in range(3)], gradient)
    for i in range(3):
        out[i] = new[i]


def shaped(shape, dtype):
    return jax.ShapeDtypeStruct(shape, dtype)


def per_device(
    ray_codes,
    target,
    direction,
    entries,
    exits,
    depth_bins,
    in_layer,
    mid_layer,
    feat_layer,
    vectors,
):
    regions = lax.axis_size("region")
    shards = lax.axis_size("rays")
    region = lax.axis_index("region")
    samples, ray_count = depth_bins.shape[1:]
    own_rows = ray_count // regions
    layers = (in_layer, mid_layer, feat_layer)
    shapes = tuple(layer.shape[2:] for layer in layers)
    vec_share = vectors.shape[2]
    hidden = shapes[0][1]
    feat = shapes[2][1]
    code_width = ray_codes.shape[2]
    pack_rows = sum(rows * (width // LANES) for rows, width in shapes) + 16
    block_rows = own_rows * (feat // LANES) + min(own_rows, 16)
    total = samples * ray_count

    pack = call(pack_body, shaped((pack_rows, LANES), bf16), 4)(*layers, vectors)
    packs = lax.all_gather(pack, "rays", axis=0)
    send, encoded, one, two, colour, scalars, mid_weight, head_weight = call(
        functools.partial(forward_body, shapes=shapes, vec_share=vec_share, regions=regions),
        (
            shaped((regions, block_rows, LANES), bf16),
            shaped((total, code_width), bf16),
            shaped((total, hidden), bf16),
            shaped((total, hidden), bf16),
            shaped((total, feat), f32),
            shaped((3, samples, ray_count), f32),
            shaped((hidden, hidden), bf16),
            shaped((hidden, feat + LANES), bf16),
        ),
        5,
    )(packs, ray_codes, depth_bins[0], entries, exits)
    got = lax.all_to_all(send, "region", 0, 0)
    own_target = lax.dynamic_slice_in_dim(target, region * own_rows, own_rows, 0)
    own_direction = lax.dynamic_slice_in_dim(direction, region * own_rows, own_rows, 0)
    reply = call(owner_body, shaped((regions, block_rows, LANES), bf16), 3)(
        got, own_target, own_direction[:, None]
    )
    answer = lax.all_to_all(reply, "region", 0, 0)
    grads, depth_grad = call(
        functools.partial(
            backward_body, shapes=shapes, vec_share=vec_share, shards=shards
        ),
        (shaped((shards, pack_rows, LANES), f32), shaped((1, ray_count), f32)),
        8,
        scratch=(
            pltpu.VMEM((total, feat + LANES), bf16),
            pltpu.VMEM((total, hidden), bf16),
            pltpu.VMEM((total, hidden), bf16),
        ),
    )(answer, encoded, one, two, colour, scalars, mid_weight, head_weight)
    if shards == 2:
        mine = lax.axis_index("rays")
        other = lax.dynamic_index_in_dim(grads, 1 - mine, 0, keepdims=False)
        keep = lax.dynamic_index_in_dim(grads, mine, 0, keepdims=False)
        other = lax.ppermute(other, "rays", [(0, 1), (1, 0)])
        shares = jnp.stack([keep, other])
    else:
        shares = lax.all_to_all(grads, "rays", 0, 0)
    states = (*layers, vectors)
    new = call(adam_body, tuple(shaped(s.shape, f32) for s in states), 5)(shares, *states)
    return (*new, depth_grad)


def solution(mesh):
    placed = (
        P(None, "rays", None),
        P("rays", None),
        P("rays"),
        P("region", "rays"),
        P("region", "rays"),
        P("region", None, "rays"),
        P(None, "region", "rays", None),
        P(None, "region", "rays", None),
        P(None, "region", "rays", None),
        P(None, "region", "rays"),
    )
    return jax.shard_map(
        per_device,
        mesh=mesh,
        in_specs=placed,
        out_specs=(
            P(None, "region", "rays", None),
            P(None, "region", "rays", None),
            P(None, "region", "rays", None),
            P(None, "region", "rays"),
            P("region", "rays"),
        ),
        check_vma=False,
    )
```

time: 274 us -> 74.8 us (0.27)
  blocking collectives: 92 us -> 2.31 us
  waiting for transfers between devices: 117 us -> 28.2 us
  Pallas kernels: 0 us -> 21.7 us
  other arithmetic: 21.4 us -> 0.05 us
  matrix products: 17.4 us -> 0 us
  between operations: 15.5 us -> 0.79 us
  starting transfers between devices: 0.16 us -> 12.1 us
    psum x1 -> x0, waiting for transfers between devices: 104 us -> none  [per_device(): rendered = lax.psum(contribution, 'region')]
    all_gather x5 -> x1, blocking collectives: 86.9 us -> 2.31 us  [per_device(): packs = lax.all_gather(pack, 'rays', axis=0)]
    all_to_all x0 -> x2, waiting for transfers between devices: none -> 26.5 us  [the longest x1 13.3 us: per_device(): got = lax.all_to_all(send, 'region', 0, 0)]
    pallas_call x0 -> x5, Pallas kernels: none -> 21.7 us  [the longest x1 10.9 us: per_device(): call(functools.partial(backward_body, shapes=shapes, vec_share=vec_share,...]
    dot_general x10 -> x0, matrix products: 17.4 us -> none  [the longest x1 3.99 us: backward(): jnp.dot(hidden_two.T, colour_grad, preferred_element_type=jnp.float32)]
    reduce_scatter x3 -> x0, waiting for transfers between devices: 12.4 us -> none  [the longest x1 9.95 us: per_device(): lax.psum_scatter(feat_grad, 'rays', scatter_dimension=0, tiled=True)]
    all_to_all x0 -> x2, starting transfers between devices: none -> 12 us  [the longest x1 8.23 us: per_device(): got = lax.all_to_all(send, 'region', 0, 0)]
    reduce_sum x6 -> x0, other arithmetic: 7.33 us -> none  [the longest x1 5.02 us: backward(): jnp.sum(colour_grad, 0, dtype=jnp.float32)]
  transfers between devices with their start and end apart: 4 -> 3, of which waited for: 3 -> 3; matrix products, arithmetic and copies ran while one was open for 5% -> 1% of each run, Pallas kernels for 0% -> 0%
where the time goes in v1:
time: 74.8 us; the launch traced here: 74.2 us
  waiting for transfers between devices  28.2 us (38%)
  Pallas kernels  21.7 us (29%)
  starting transfers between devices  12.1 us (16%)
  local copies, waits for them, and re-layouts  9.03 us (12%)
  blocking collectives  2.31 us (3%)
  between operations  0.79 us (1%)
    all_to_all x1, waiting for transfers between devices, per_device(): got = lax.all_to_all(send, 'region', 0, 0)  13.3 us
    all_to_all x1, waiting for transfers between devices, per_device(): answer = lax.all_to_all(reply, 'region', 0, 0)  13.2 us
    pallas_call x1, Pallas kernels, per_device(): call(functools.partial(backward_body, shapes=shapes, vec_share=vec_share,...  10.9 us
    all_to_all x1, starting transfers between devices, per_device(): got = lax.all_to_all(send, 'region', 0, 0)  8.23 us
    unnamed x30, local copies, waits for them, and re-layouts  8.12 us
    pallas_call x1, Pallas kernels, per_device(): call(functools.partial(forward_body, shapes=shapes, vec_share=vec_share,...  7.47 us
    all_to_all x1, starting transfers between devices, per_device(): answer = lax.all_to_all(reply, 'region', 0, 0)  3.79 us
    all_gather x1, blocking collectives, per_device(): packs = lax.all_gather(pack, 'rays', axis=0)  2.31 us
  transfers between devices with their start and end apart: 3, of which 3 were waited for; matrix products, arithmetic and copies ran while one was open for 1% of the time, Pallas kernels for 0%

profile of v1, /device:TPU:0, one launch (start us, length us, event | category | flops | bytes accessed | tf_op | source)
XLA Modules:
  0.0 74.2 jit_solution(4060169665519377546)
XLA Ops:
  0.6 0.0 copy-start
  0.6 0.0 copy-start.1
  0.7 1.1 %copy-done.1 = f32[3,1,128,384]{3,2,1,0:T(8,128)S(1)} copy-done((f32[3,1,128,384]{3,2,1,0:T(8,128)S(1)}, f32[3,1,128,384]{3,2,1,0:T(8,128)}, u32[]{:S(2)}) %copy-start.1) | copy-done | bytes 589848
  1.8 0.0 copy-start.3
  1.8 1.0 %copy-done.3 = f32[3,1,128,256]{3,2,1,0:T(8,128)S(1)} copy-done((f32[3,1,128,256]{3,2,1,0:T(8,128)S(1)}, f32[3,1,128,256]{3,2,1,0:T(8,128)}, u32[]{:S(2)}) %copy-start.3) | copy-done | bytes 393240
  2.8 0.0 copy-start.7
  2.8 0.9 %copy-done.7 = f32[3,1,64,256]{3,2,1,0:T(8,128)S(1)} copy-done((f32[3,1,64,256]{3,2,1,0:T(8,128)S(1)}, f32[3,1,64,256]{3,2,1,0:T(8,128)}, u32[]{:S(2)}) %copy-start.7) | copy-done | bytes 196632
  3.7 0.0 copy-start.10
  3.7 0.7 copy-done.10
  4.4 0.0 copy-start.9
  4.4 2.3 %all-gather = bf16[1568,128]{1,0:T(8,128)(2,1)S(1)} all-gather(bf16[784,128]{1,0:T(8,128)(2,1)S(1)} %shard_map.137), channel_id=2, replica_groups=mesh['region'=16,'rays'=2] {'rays'}, dimensions={0}, use_global_device_ids=true | all-gather | bytes 602112 | tf_op jit(solution)/shard_map/all_gather | solution.py:428
  6.7 0.0 copy-done.9
  6.7 0.0 copy-start.12
  6.7 0.7 copy-done.12
  7.4 0.0 copy-start.13
  7.4 0.7 copy-done.13
  8.1 0.0 copy-start.14
  8.1 0.7 copy-done.14
  8.8 7.5 %shard_map.138 = (bf16[16,112,128]{2,1,0:T(8,128)(2,1)}, bf16[4096,128]{1,0:T(8,128)(2,1)S(1)}, bf16[4096,256]{1,0:T(8,128)(2,1)S(1)}, bf16[4096,256]{1,0:T(8,12...) custom-call(bf16[2,784,128]{2,1,0:T(8,128)(2,1)S(1)} %bitcast.7, ...), custom_call_target="tpu_custom_call" | custom-call | flops 1000000 | bytes 1000000 | tf_op jit(solution)/shard_map/pallas_call | solution.py:429
  16.3 0.0 copy-start.5
  16.3 1.1 %copy-done.5 = bf16[4096,128]{1,0:T(8,128)(2,1)} copy-done((bf16[4096,128]{1,0:T(8,128)(2,1)}, bf16[4096,128]{1,0:T(8,128)(2,1)S(1)}, u32[]{:S(2)}) %copy-start.5) | copy-done | bytes 1048600
  17.3 8.2 %all-to-all-start = ((bf16[16,112,128]{2,1,0:T(8,128)(2,1)}), bf16[16,112,128]{2,1,0:T(8,128)(2,1)S(1)}, u32[]{:S(2)}, u32[]{:S(2)}) async-start(bf16[16,112,128]{2,1,0:T(8,128)(2,1)} %get-tuple-element.19), calls=%async_computation | async-start | bytes 917504 | tf_op jit(solution)/shard_map/all_to_all | solution.py:443
  25.6 0.8 %dynamic-slice_bitcast_fusion.1 = s32[32,1]{0,1:T(1,128)S(1)} fusion(s32[512]{0:T(512)} %param.12, s32[]{:T(128)S(6)} %select_n.11), kind=kLoop, calls=%fused_computation.4 | loop fusion | bytes 260 | tf_op jit(solution)/shard_map/broadcast_in_dim | solution.py:447
  26.3 0.1 copy.15.direction_ref
  26.4 0.0 copy-done
  26.4 13.3 %all-to-all-done.got_ref = bf16[16,112,128]{2,1,0:T(8,128)(2,1)S(1)} async-done(((bf16[16,112,128]{2,1,0:T(8,128)(2,1)}), bf16[16,112,128]{2,1,0:T(8,128)(2,1)S(1)}, u32[]{:S(2)}, u32[]{:S(2)}) %all-to-all-start) | async-done | bytes 458784 | tf_op jit(solution)/shard_map/all_to_all | solution.py:443
  39.7 2.2 %shard_map.139 = bf16[16,112,128]{2,1,0:T(8,128)(2,1)} custom-call(bf16[16,112,128]{2,1,0:T(8,128)(2,1)S(1)} %all-to-all-done.got_ref, bf16[32,384]{1,0:T(8,128)(2,1)S(1)} %constant_dynamic-slice_fusion.1.target_ref, s32[32,1]{1,0:T(8,128)S(1)} %copy.15.direction_ref), custom_call_target="tpu_custom_call" | custom-call | flops 1000000 | bytes 1000000 | tf_op jit(solution)/shard_map/pallas_call | solution.py:446
  42.0 3.8 %all-to-all-start.1 = ((bf16[16,112,128]{2,1,0:T(8,128)(2,1)}), bf16[16,112,128]{2,1,0:T(8,128)(2,1)S(1)}, u32[]{:S(2)}, u32[]{:S(2)}) async-start(bf16[16,112,128]{2,1,0:T(8,128)(2,1)} %shard_map.139), calls=%async_computation.1 | async-start | bytes 917504 | tf_op jit(solution)/shard_map/all_to_all | solution.py:449
  45.8 13.2 %all-to-all-done.1.got_ref = bf16[16,112,128]{2,1,0:T(8,128)(2,1)S(1)} async-done(((bf16[16,112,128]{2,1,0:T(8,128)(2,1)}), bf16[16,112,128]{2,1,0:T(8,128)(2,1)S(1)}, u32[]{:S(2)}, u32[]{:S(2)}) %all-to-all-start.1) | async-done | bytes 458784 | tf_op jit(solution)/shard_map/all_to_all | solution.py:449
  59.0 0.0 copy-start.6
  59.0 1.2 %copy-done.6 = bf16[4096,128]{1,0:T(8,128)(2,1)S(1)} copy-done((bf16[4096,128]{1,0:T(8,128)(2,1)S(1)}, bf16[4096,128]{1,0:T(8,128)(2,1)}, u32[]{:S(2)}) %copy-start.6) | copy-done | bytes 1048600
  60.2 10.9 %shard_map.140 = (f32[2,784,128]{2,1,0:T(8,128)S(1)}, f32[1,512]{1,0:T(1,128)}) custom-call(bf16[16,112,128]{2,1,0:T(8,128)(2,1)S(1)} %all-to-all-done.1.got_ref, bf16[4096,128]{1,0:T(8,128)(2,1)S(1)} %copy-done.6, bf16[4096,256]{1,0:T(8,128)(2,1)S(1)} %get-tuple-element.21.one_ref, bf16[4096,256]{1,0:T(8,128)(2,1)} %get-tuple-element.22.two_ref, ...), custom_call_target="tpu_custom_call" | custom-call | flops 1000000 | bytes 1000000 | tf_op jit(solution)/shard_map/pallas_call | solution.py:450
  71.1 0.0 copy-start.2
  71.1 0.0 copy-start.4
  71.1 0.0 copy-start.8
  71.1 0.0 copy-start.11
  71.1 0.1 constant_dynamic-slice_fusion
  71.2 0.1 collective-permute-start
  71.3 1.7 %collective-permute-done = f32[784,128]{1,0:T(8,128)S(1)} collective-permute-done((f32[784,128]{1,0:T(8,128)S(1)}, f32[784,128]{1,0:T(8,128)S(1)}, u32[]{:S(2)}, u32[]{:S(2)}) %collective-permute-start) | collective-permute-done | bytes 401440 | tf_op jit(solution)/shard_map/ppermute | solution.py:466
  73.0 0.1 pad_maximum_fusion.grad_ref
  73.1 0.0 copy-done.2
  73.1 0.0 copy-done.4
  73.1 0.0 copy-done.8
  73.1 0.0 copy-done.11
  73.1 1.1 %shard_map.141 = (f32[3,1,64,256]{3,2,1,0:T(8,128)}, f32[3,1,128,256]{3,2,1,0:T(8,128)}, f32[3,1,128,384]{3,2,1,0:T(8,128)}, f32[3,1,576]{2,1,0:T(1,128)}) custom-call(f32[2,784,128]{2,1,0:T(8,128)S(1)} %pad_maximum_fusion.grad_ref, f32[3,1,64,256]{3,2,1,0:T(8,128)S(1)} %copy-done.8, f32[3,1,128,256]{3,2,1,0:T(8,128)S(1)} %copy-done.4, ...), custom_call_target="tpu_custom_call" | custom-call | flops 1000000 | bytes 1000000 | tf_op jit(solution)/shard_map/pallas_call | solution.py:471
  (2 shorter events, 0.0 us)
Async XLA Ops:
  0.6 25.8 %copy-start = (bf16[512,384]{1,0:T(8,128)(2,1)S(1)}, bf16[512,384]{1,0:T(8,128)(2,1)}, u32[]{:S(2)}) copy-start(bf16[512,384]{1,0:T(8,128)(2,1)} %param.11) | copy-start | bytes 1179652
  0.6 1.1 %copy-start.1 = (f32[3,1,128,384]{3,2,1,0:T(8,128)S(1)}, f32[3,1,128,384]{3,2,1,0:T(8,128)}, u32[]{:S(2)}) copy-start(f32[3,1,128,384]{3,2,1,0:T(8,128)} %refs_2_.1) | copy-start | bytes 1769476
  1.8 1.0 %copy-start.3 = (f32[3,1,128,256]{3,2,1,0:T(8,128)S(1)}, f32[3,1,128,256]{3,2,1,0:T(8,128)}, u32[]{:S(2)}) copy-start(f32[3,1,128,256]{3,2,1,0:T(8,128)} %refs_1_.1) | copy-start | bytes 1179652
  2.8 0.9 %copy-start.7 = (f32[3,1,64,256]{3,2,1,0:T(8,128)S(1)}, f32[3,1,64,256]{3,2,1,0:T(8,128)}, u32[]{:S(2)}) copy-start(f32[3,1,64,256]{3,2,1,0:T(8,128)} %refs_0_.1) | copy-start | bytes 589828
  3.7 0.7 copy-start.10
  4.4 2.3 %copy-start.9 = (bf16[2,512,128]{2,1,0:T(8,128)(2,1)S(1)}, bf16[2,512,128]{2,1,0:T(8,128)(2,1)}, u32[]{:S(2)}) copy-start(bf16[2,512,128]{2,1,0:T(8,128)(2,1)} %codes_ref.1) | copy-start | bytes 786436
  6.7 0.7 copy-start.12
  7.4 0.7 copy-start.13
  8.1 0.7 copy-start.14
  16.3 1.1 %copy-start.5 = (bf16[4096,128]{1,0:T(8,128)(2,1)}, bf16[4096,128]{1,0:T(8,128)(2,1)S(1)}, u32[]{:S(2)}) copy-start(bf16[4096,128]{1,0:T(8,128)(2,1)S(1)} %get-tuple-element.20.enc_ref) | copy-start | bytes 3145732
  17.3 22.4 %all-to-all-start = ((bf16[16,112,128]{2,1,0:T(8,128)(2,1)}), bf16[16,112,128]{2,1,0:T(8,128)(2,1)S(1)}, u32[]{:S(2)}, u32[]{:S(2)}) async-start(bf16[16,112,128]{2,1,0:T(8,128)(2,1)} %get-tuple-element.19), calls=%async_computation | async-start | bytes 917504 | tf_op jit(solution)/shard_map/all_to_all | solution.py:443
  42.0 17.0 %all-to-all-start.1 = ((bf16[16,112,128]{2,1,0:T(8,128)(2,1)}), bf16[16,112,128]{2,1,0:T(8,128)(2,1)S(1)}, u32[]{:S(2)}, u32[]{:S(2)}) async-start(bf16[16,112,128]{2,1,0:T(8,128)(2,1)} %shard_map.139), calls=%async_computation.1 | async-start | bytes 917504 | tf_op jit(solution)/shard_map/all_to_all | solution.py:449
  59.0 1.2 %copy-start.6 = (bf16[4096,128]{1,0:T(8,128)(2,1)S(1)}, bf16[4096,128]{1,0:T(8,128)(2,1)}, u32[]{:S(2)}) copy-start(bf16[4096,128]{1,0:T(8,128)(2,1)} %copy-done.5) | copy-start | bytes 3145732
  71.1 2.0 %copy-start.2 = (f32[3,1,128,384]{3,2,1,0:T(8,128)S(1)}, f32[3,1,128,384]{3,2,1,0:T(8,128)}, u32[]{:S(2)}) copy-start(f32[3,1,128,384]{3,2,1,0:T(8,128)} %refs_2_.1) | copy-start | bytes 1769476
  71.1 2.0 %copy-start.4 = (f32[3,1,128,256]{3,2,1,0:T(8,128)S(1)}, f32[3,1,128,256]{3,2,1,0:T(8,128)}, u32[]{:S(2)}) copy-start(f32[3,1,128,256]{3,2,1,0:T(8,128)} %refs_1_.1) | copy-start | bytes 1179652
  71.1 2.0 %copy-start.8 = (f32[3,1,64,256]{3,2,1,0:T(8,128)S(1)}, f32[3,1,64,256]{3,2,1,0:T(8,128)}, u32[]{:S(2)}) copy-start(f32[3,1,64,256]{3,2,1,0:T(8,128)} %refs_0_.1) | copy-start | bytes 589828
  71.1 2.0 %copy-start.11 = (f32[3,1,576]{2,1,0:T(1,128)S(1)}, f32[3,1,576]{2,1,0:T(1,128)}, u32[]{:S(2)}) copy-start(f32[3,1,576]{2,1,0:T(1,128)} %refs_3_.1) | copy-start | bytes 20740
  71.2 1.8 %collective-permute-start = (f32[784,128]{1,0:T(8,128)S(1)}, f32[784,128]{1,0:T(8,128)S(1)}, u32[]{:S(2)}, u32[]{:S(2)}) collective-permute-start(f32[784,128]{1,0:T(8,128)S(1)} %get-tuple-element.34), channel_id=1, source_target_pairs={{0,1},{1,0},{2,3},{3,2},{4,5},{5,4},{6,7},{7,6},{8,9},{9,8},{10,11... | collective-permute-start | bytes 1204232 | tf_op jit(solution)/shard_map/ppermute | solution.py:466

commit v2 on v1

v2 whole, which is shorter than its diff:
```python
import functools

import jax
import jax.numpy as jnp
from jax import lax
from jax.experimental import pallas as pl
from jax.experimental.pallas import tpu as pltpu
from jax.sharding import PartitionSpec as P

BINS = 64
LANES = 128

depth_scale = 4.0
beta_one = 0.9
beta_two = 0.999
learn_rate = 0.001
epsilon = 1e-08
first_fix = 1.0 - 0.9**10
second_fix = 1.0 - 0.999**10

f32 = jnp.float32
bf16 = jnp.bfloat16


def in_vmem(value):
    return pltpu.with_memory_space_constraint(value, pltpu.VMEM)


def in_hbm(value):
    return pltpu.with_memory_space_constraint(value, pltpu.HBM)


def call(body, out_shape, inputs, limit, scratch=(), specs=None, flops=1000000, moved=1000000):
    many = isinstance(out_shape, (tuple, list))
    spec = pl.BlockSpec(memory_space=pltpu.VMEM)
    return pl.pallas_call(
        body,
        out_shape=out_shape,
        in_specs=specs or [spec] * len(inputs),
        out_specs=tuple(spec for _ in out_shape) if many else spec,
        scratch_shapes=list(scratch),
        compiler_params=pltpu.CompilerParams(vmem_limit_bytes=limit * 1024 * 1024),
        cost_estimate=pl.CostEstimate(flops=flops, bytes_accessed=moved, transcendentals=0),
    )(*inputs)


def blocks(width):
    return [slice(LANES * k, LANES * (k + 1)) for k in range(width // LANES)]


def wide_rows(count):
    return -(-count // LANES)


def row_block(row, rows):
    width = row.shape[1]
    padded = wide_rows(width) * LANES
    if padded != width:
        row = jnp.concatenate([row, jnp.zeros((1, padded - width), f32)], 1)
    place = lax.broadcasted_iota(jnp.int32, (rows, LANES), 0)
    out = jnp.zeros((rows, LANES), f32)
    for k, cut in enumerate(blocks(padded)):
        out = jnp.where(place == k, jnp.broadcast_to(row[:, cut], (rows, LANES)), out)
    return out


def block_row(block, count):
    return jnp.concatenate([block[k : k + 1] for k in range(count)], 1)


def split3(value):
    high = value.astype(bf16).astype(f32)
    rest = value - high
    mid = rest.astype(bf16).astype(f32)
    return (high, mid, rest - mid)


def lanes_of(shape):
    return lax.broadcasted_iota(jnp.int32, shape, 1)


def turned(rows, ray_count):
    fill = LANES - rows.shape[0]
    return jnp.concatenate([rows, jnp.zeros((fill, ray_count), f32)], 0).T


def fold(extra, own_rows, regions):
    fold_rows = 8
    groups = own_rows // fold_rows
    extra = extra.reshape(regions, own_rows, LANES)
    out = extra[:, :fold_rows]
    for g in range(1, groups):
        piece = extra[:, fold_rows * g : fold_rows * (g + 1)].reshape(regions * fold_rows, LANES)
        piece = pltpu.roll(piece, (LANES // groups) * g, 1)
        out = out + piece.reshape(regions, fold_rows, LANES)
    return out


def unfold(folded, own_rows, used):
    regions, fold_rows, _ = folded.shape
    groups = own_rows // fold_rows
    flat = folded.reshape(regions * fold_rows, LANES)
    keep = lanes_of(flat.shape) < used
    parts = []
    for g in range(groups):
        piece = flat if g == 0 else pltpu.roll(flat, LANES - (LANES // groups) * g, 1)
        parts.append(jnp.where(keep, piece, 0.0).reshape(regions, fold_rows, LANES))
    return jnp.concatenate(parts, 1) if groups > 1 else parts[0]


def prepare_body(*refs, unit_length, own_rows):
    ins, refs = (refs[:10], refs[10:])
    pack_ref, enc_ref, geometry_ref, *refs = refs
    target_ref = refs.pop(0) if own_rows else None
    held, sems = (refs[:-1], refs[-1])
    copies = []

    def fetch(source, place):
        copies.append(pltpu.make_async_copy(source, place, sems.at[len(copies)]))
        copies[-1].start()

    for ref, hold in zip(ins[:4], held[:4]):
        fetch(ref.at[0], hold)
    for ref, hold in zip(ins[4:9], held[4:9]):
        fetch(ref, hold)
    if own_rows:
        first = pl.multiple_of(lax.axis_index("region") * own_rows, 16)
        fetch(ins[9].at[pl.ds(first, own_rows)], target_ref)
    spot = 0
    for copy, hold in zip(copies[:3], held[:3]):
        copy.wait()
        rows, width = hold.shape[1:]
        for cut in blocks(width):
            pack_ref[spot : spot + rows, :] = hold[0, :, cut].astype(bf16)
            spot += rows
    for copy in copies[3:]:
        copy.wait()
    pack_ref[spot : spot + 16, :] = row_block(held[3][...], 16).astype(bf16)
    codes, bins, entry, exit_, direction = held[4:9]
    bins = bins[0].astype(f32)
    samples, ray_count = bins.shape
    slot = lax.broadcasted_iota(jnp.int32, bins.shape, 0)
    following = jnp.where(slot == samples - 1, float(BINS), pltpu.roll(bins, samples - 1, 0))
    inside = ((slot >= entry[...]) & (slot < exit_[...])).astype(f32)
    geometry_ref[:samples] = (following - bins) * unit_length * inside
    geometry_ref[samples : samples + 1] = direction[...].astype(f32)
    position = turned((bins + 0.5) / BINS, ray_count)
    code_zero = codes[0].astype(f32)
    code_one = codes[1].astype(f32)
    for j in range(samples):
        encoded = code_zero + position[:, j : j + 1] * code_one
        enc_ref[ray_count * j : ray_count * (j + 1), :] = encoded.astype(bf16)


def assemble(packs, shapes, vec_share):
    shards = len(packs)
    spot = 0
    mats = []
    for rows, width in shapes:
        pieces = []
        for cut in blocks(width):
            pieces.append(jnp.concatenate([p[spot : spot + rows, :] for p in packs], 0))
            spot += rows
        mats.append(jnp.concatenate(pieces, 1))
    vec_total = vec_share * shards
    vec = jnp.zeros((1, vec_total), f32)
    for s, p in enumerate(packs):
        block = p[spot : spot + 16, :].astype(f32)
        count = wide_rows(vec_share)
        row = block_row(block, count)
        fill = vec_total - count * LANES
        if fill:
            row = jnp.concatenate([row, jnp.zeros((1, fill), f32)], 1)
        if s:
            row = pltpu.roll(row, vec_share * s, 1)
        vec = vec + row
    return (*mats, vec)


def forward_body(*refs, shapes, vec_share, regions, pair):
    both = None
    if pair:
        own_ref, other_ref, *refs, both = refs
        mine = lax.axis_index("rays")
        both[mine] = own_ref[...]
        both[1 - mine] = other_ref[...]
        packs = [both.at[0], both.at[1]]
    else:
        packs_ref, *refs = refs
        packs = [packs_ref.at[s] for s in range(packs_ref.shape[0])]
    enc_ref, geometry_ref, send_ref, one_ref, two_ref, colour_ref, scalar_ref, *refs = refs
    mid_ref, head_ref = refs
    samples, ray_count = scalar_ref.shape[1:]
    own_rows = ray_count // regions
    hidden = mid_ref.shape[0]
    feat = colour_ref.shape[1]
    in_weight, mid_weight, feat_weight, vec = assemble(packs, shapes, vec_share)
    bias_one = vec[:, :hidden]
    bias_two = vec[:, hidden : 2 * hidden]
    density_row = vec[:, 2 * hidden : 3 * hidden]
    bias_feat = vec[:, 3 * hidden :]
    density_cols = jnp.broadcast_to(density_row, (LANES, hidden)).T
    mid_ref[...] = mid_weight
    head_ref[...] = jnp.concatenate([feat_weight, density_cols.astype(bf16)], 1)
    geometry = geometry_ref[:samples]
    density = jnp.zeros((ray_count, LANES), f32)
    lane = lanes_of((ray_count, LANES))
    for j in range(samples):
        rows = slice(ray_count * j, ray_count * (j + 1))
        one = jnp.dot(enc_ref[rows, :], in_weight, preferred_element_type=f32) + bias_one
        one = jnp.maximum(one, 0.0).astype(bf16)
        one_ref[rows, :] = one
        two = jnp.dot(one, mid_weight, preferred_element_type=f32) + bias_two
        two = jnp.maximum(two, 0.0).astype(bf16)
        two_ref[rows, :] = two
        raw = jnp.dot(two, head_ref[...], preferred_element_type=f32)
        density = jnp.where(lane == j, raw[:, feat:], density)
        colour_ref[rows, :] = 0.5 * jnp.tanh(0.5 * (raw[:, :feat] + bias_feat)) + 0.5
    density = density.T[:samples]
    soft = jnp.maximum(density, 0.0) + jnp.log1p(jnp.exp(-jnp.abs(density)))
    optical = soft * geometry
    before = [jnp.zeros((1, ray_count), f32)]
    for j in range(samples):
        before.append(before[-1] + optical[j : j + 1])
    depth = before.pop()
    optical_before = jnp.concatenate(before, 0)
    local_weight = jnp.exp(-optical_before) * (jnp.tanh(0.5 * optical) * (1.0 + jnp.exp(-optical)))
    sig = 0.5 * jnp.tanh(0.5 * density) + 0.5
    scalar_ref[0] = local_weight
    scalar_ref[1] = jnp.exp(-(optical_before + optical))
    scalar_ref[2] = geometry * sig
    direction = geometry_ref[samples : samples + 1]
    columns = turned(
        jnp.concatenate([*split3(depth), direction, local_weight], 0), ray_count
    )
    total = jnp.zeros((ray_count, feat), f32)
    for j in range(samples):
        rows = slice(ray_count * j, ray_count * (j + 1))
        total = total + columns[:, 4 + j : 5 + j] * colour_ref[rows, :]
    extra = jnp.where(lane < 4, columns, 0.0)
    parts = [total[:, cut].reshape(regions, own_rows, LANES) for cut in blocks(feat)]
    parts.append(fold(extra, own_rows, regions))
    send_ref[...] = jnp.concatenate(parts, 1).astype(bf16)


def owner_body(got_ref, target_ref, out_ref):
    regions = got_ref.shape[0]
    own_rows, feat = target_ref.shape
    cuts = blocks(feat)
    got = got_ref[...].astype(f32)
    extra = unfold(got[:, own_rows * len(cuts) :], own_rows, 4)
    lane = lanes_of((own_rows, LANES))
    depth = [
        jnp.sum(jnp.where(lane < 3, extra[q], 0.0), 1, keepdims=True) for q in range(regions)
    ]
    onward = extra[0][:, 3:4] < 0.5

    def side(values):
        below, above = ([jnp.zeros_like(values[0])], [jnp.zeros_like(values[0])])
        for q in range(regions - 1):
            below.append(below[-1] + values[q])
            above.append(above[-1] + values[regions - 1 - q])
        return (below, above[::-1])

    below, above = side(depth)
    trans = [jnp.exp(-jnp.where(onward, below[q], above[q])) for q in range(regions)]

    def part(q, k):
        return got[q, own_rows * k : own_rows * (k + 1)]

    grads = []
    for k, cut in enumerate(cuts):
        rendered = trans[0] * part(0, k)
        for q in range(1, regions):
            rendered = rendered + trans[q] * part(q, k)
        grads.append((rendered - target_ref[:, cut].astype(f32)).astype(bf16).astype(f32))
    region_grad = []
    for q in range(regions):
        product = grads[0] * part(q, 0)
        for k in range(1, len(cuts)):
            product = product + grads[k] * part(q, k)
        region_grad.append(trans[q] * jnp.sum(product, 1, keepdims=True))
    below, above = side(region_grad)
    for q in range(regions):
        after = jnp.where(onward, above[q], below[q])
        extra = jnp.zeros((own_rows, LANES), f32)
        for i, piece in enumerate((*split3(trans[q]), *split3(after))):
            extra = jnp.where(lane == i, piece, extra)
        out_ref[q] = jnp.concatenate([*grads, fold(extra, own_rows, 1)[0]], 0).astype(bf16)


def over_rows(left, right):
    return lax.dot_general(left, right, (((0,), (0,)), ((), ())), preferred_element_type=f32)


def across(left, right):
    return lax.dot_general(left, right, (((1,), (1,)), ((), ())), preferred_element_type=f32)


def backward_body(
    got_ref,
    enc_ref,
    one_ref,
    two_ref,
    colour_ref,
    scalar_ref,
    mid_ref,
    head_ref,
    depth_ref,
    *refs,
    shapes,
    vec_share,
    shards,
):
    *outs, head_grad_ref, second_ref, first_ref, shares = refs
    regions = got_ref.shape[0]
    samples, ray_count = scalar_ref.shape[1:]
    own_rows = ray_count // regions
    hidden = mid_ref.shape[0]
    feat = colour_ref.shape[1]
    cuts = blocks(feat)
    got = got_ref[...].astype(f32)
    grad = jnp.concatenate(
        [
            got[:, own_rows * k : own_rows * (k + 1)].reshape(ray_count, LANES)
            for k in range(len(cuts))
        ],
        1,
    )
    extra = unfold(got[:, own_rows * len(cuts) :], own_rows, 6).reshape(ray_count, LANES).T
    trans = extra[0:1] + extra[1:2] + extra[2:3]
    after = extra[3:4] + extra[4:5] + extra[5:6]
    depth_ref[...] = -after
    lane = lanes_of((ray_count, LANES))
    sample_grad = jnp.zeros((ray_count, LANES), f32)
    for j in range(samples):
        rows = slice(ray_count * j, ray_count * (j + 1))
        product = jnp.sum(colour_ref[rows, :] * grad, 1, keepdims=True)
        sample_grad = jnp.where(lane == j, product, sample_grad)
    sample_grad = sample_grad.T[:samples]
    local_weight = scalar_ref[0]
    weighted = local_weight * sample_grad
    later = [jnp.zeros((1, ray_count), f32)]
    for j in range(samples - 1, 0, -1):
        later.append(later[-1] + weighted[j : j + 1])
    later = jnp.concatenate(later[::-1], 0)
    optical_grad = trans * (scalar_ref[1] * sample_grad - later) - after
    density_grad = optical_grad * scalar_ref[2]
    columns = turned(jnp.concatenate([trans * local_weight, density_grad], 0), ray_count)
    first_sum = jnp.zeros((1, hidden), f32)
    second_sum = jnp.zeros((1, hidden), f32)
    colour_sum = jnp.zeros((1, feat), f32)
    for j in range(samples):
        rows = slice(ray_count * j, ray_count * (j + 1))
        colour = colour_ref[rows, :]
        colour_grad = (columns[:, j : j + 1] * grad * colour * (1.0 - colour)).astype(bf16)
        density_part = jnp.where(lane == samples + j, columns, 0.0).astype(bf16)
        head_grad_ref[rows, :] = jnp.concatenate([colour_grad, density_part], 1)
        colour_sum = colour_sum + jnp.sum(colour_grad.astype(f32), 0, keepdims=True)
    hidden_grad = across(head_grad_ref[...], head_ref[...])
    second = jnp.where(two_ref[...].astype(f32) > 0, hidden_grad, 0.0).astype(bf16)
    second_ref[...] = second
    second_sum = jnp.sum(second.astype(f32), 0, keepdims=True)
    below = across(second_ref[...], mid_ref[...])
    first = jnp.where(one_ref[...].astype(f32) > 0, below, 0.0).astype(bf16)
    first_ref[...] = first
    first_sum = jnp.sum(first.astype(f32), 0, keepdims=True)
    in_grad = over_rows(enc_ref[...], first_ref[...])
    mid_grad = over_rows(one_ref[...], second_ref[...])
    head_grad = over_rows(two_ref[...], head_grad_ref[...])
    density_sum = jnp.sum(head_grad[:, feat:].T, 0, keepdims=True)
    vec = jnp.concatenate([first_sum, second_sum, density_sum, colour_sum], 1)
    values = [in_grad, mid_grad, head_grad[:, :feat]]
    shares = refs[-1]
    mine = lax.axis_index("rays")
    total = vec.shape[1]
    for s in range(shards):
        place = lax.rem(s + shards - mine, shards) if shards == 2 else s
        spot = 0
        for (rows, width), value in zip(shapes, values):
            for cut in blocks(width):
                shares[place, spot : spot + rows, :] = value[rows * s : rows * (s + 1), cut]
                spot += rows
        row = pltpu.roll(vec, total - vec_share * s, 1) if s else vec
        shares[place, spot : spot + 16, :] = row_block(row[:, : wide_rows(vec_share) * LANES], 16)
    if shards == 2:
        outs[0][...] = shares[0]
        outs[1][...] = shares[1]
    else:
        outs[0][...] = shares[...]


def adam_body(*refs, shards):
    grad_refs = refs[:shards]
    state_refs, out_refs = (refs[shards : shards + 4], refs[shards + 4 :])

    def update(stacked, gradient):
        first_moment = beta_one * stacked[1] + (1.0 - beta_one) * gradient
        second = beta_two * stacked[2] + (1.0 - beta_two) * gradient * gradient
        step = first_moment / first_fix / (jnp.sqrt(second / second_fix) + epsilon)
        return (stacked[0] - learn_rate * step, first_moment, second)

    def gathered(spot, rows):
        total = grad_refs[0][spot : spot + rows, :]
        for ref in grad_refs[1:]:
            total = total + ref[spot : spot + rows, :]
        return total

    spot = 0
    for ref, out in zip(state_refs[:3], out_refs[:3]):
        rows, width = ref.shape[2:]
        for cut in blocks(width):
            new = update([ref[i, 0, :, cut] for i in range(3)], gathered(spot, rows))
            spot += rows
            for i in range(3):
                out[i, 0, :, cut] = new[i]
    ref, out = (state_refs[3], out_refs[3])
    share = ref.shape[2]
    gradient = block_row(gathered(spot, 16), wide_rows(share))[:, :share]
    new = update([ref[i] for i in range(3)], gradient)
    for i in range(3):
        out[i] = new[i]


def shaped(shape, dtype):
    return jax.ShapeDtypeStruct(shape, dtype)


def per_device(
    ray_codes,
    target,
    direction,
    entries,
    exits,
    depth_bins,
    in_layer,
    mid_layer,
    feat_layer,
    vectors,
):
    regions = lax.axis_size("region")
    shards = lax.axis_size("rays")
    samples, ray_count = depth_bins.shape[1:]
    own_rows = ray_count // regions
    layers = (in_layer, mid_layer, feat_layer)
    states = (*layers, vectors)
    shapes = tuple(layer.shape[2:] for layer in layers)
    vec_share = vectors.shape[2]
    hidden = shapes[0][1]
    feat = shapes[2][1]
    code_width = ray_codes.shape[2]
    pack_rows = sum(rows * (width // LANES) for rows, width in shapes) + 16
    block_rows = own_rows * (feat // LANES) + 8
    total = samples * ray_count
    sizes = dict(shapes=shapes, vec_share=vec_share)
    pair = shards == 2
    flops = 2 * total * (code_width * hidden + hidden * hidden + hidden * (feat + LANES))

    arguments = (*states, ray_codes, depth_bins, entries, exits, direction[None], target)
    aligned = own_rows % 16 == 0
    pack, encoded, geometry, *own_target = call(
        functools.partial(
            prepare_body,
            unit_length=depth_scale / (regions * BINS),
            own_rows=own_rows if aligned else 0,
        ),
        (
            pltpu.VMEM((pack_rows, LANES), bf16),
            pltpu.VMEM((total, code_width), bf16),
            pltpu.VMEM((samples + 8, ray_count), f32),
        )
        + ((pltpu.VMEM((own_rows, feat), bf16),) if aligned else ()),
        [in_hbm(a) for a in arguments],
        16,
        scratch=[pltpu.VMEM(a.shape[1:], f32) for a in states]
        + [pltpu.VMEM(a.shape, a.dtype) for a in arguments[4:9]]
        + [pltpu.SemaphoreType.DMA((10,))],
        specs=[pl.BlockSpec(memory_space=pltpu.HBM)] * 10,
    )
    if aligned:
        own_target = own_target[0]
    else:
        first = lax.axis_index("region") * own_rows
        own_target = lax.dynamic_slice_in_dim(target, first, own_rows, 0)
    if pair:
        packs = (pack, lax.ppermute(pack, "rays", [(0, 1), (1, 0)]))
    else:
        packs = (lax.all_gather(pack, "rays", axis=0),)
    send, *kept = call(
        functools.partial(forward_body, regions=regions, pair=pair, **sizes),
        (
            shaped((regions, block_rows, LANES), bf16),
            pltpu.VMEM((total, hidden), bf16),
            pltpu.VMEM((total, hidden), bf16),
            pltpu.VMEM((total, feat), f32),
            pltpu.VMEM((3, samples, ray_count), f32),
            pltpu.VMEM((hidden, hidden), bf16),
            pltpu.VMEM((hidden, feat + LANES), bf16),
        ),
        [in_vmem(v) for v in (*packs, encoded, geometry)],
        16,
        scratch=[pltpu.VMEM((2, pack_rows, LANES), bf16)] if pair else (),
        flops=flops,
        moved=total * (feat + hidden) * 4,
    )
    got = lax.all_to_all(send, "region", 0, 0)
    reply = call(
        owner_body, shaped((regions, block_rows, LANES), bf16), (got, own_target), 8
    )
    answer = lax.all_to_all(reply, "region", 0, 0)
    share = shaped((pack_rows, LANES), f32)
    shares = shaped((shards, pack_rows, LANES), f32)
    depth_grad, *grads = call(
        functools.partial(backward_body, shards=shards, **sizes),
        (shaped((1, ray_count), f32),) + ((share, share) if pair else (shares,)),
        (answer, *[in_vmem(v) for v in (encoded, *kept)]),
        24,
        scratch=[
            pltpu.VMEM((total, feat + LANES), bf16),
            pltpu.VMEM((total, hidden), bf16),
            pltpu.VMEM((total, hidden), bf16),
            pltpu.VMEM((shards, pack_rows, LANES), f32),
        ],
        flops=2 * flops,
        moved=total * (feat + hidden) * 4,
    )
    if pair:
        parts = (grads[0], lax.ppermute(grads[1], "rays", [(0, 1), (1, 0)]))
    else:
        exchanged = lax.all_to_all(grads[0], "rays", 0, 0)
        parts = tuple(exchanged[s] for s in range(shards))
    new = call(
        functools.partial(adam_body, shards=shards),
        tuple(shaped(s.shape, f32) for s in states),
        (*parts, *states),
        16,
    )
    return (*new, depth_grad)


def solution(mesh):
    placed = (
        P(None, "rays", None),
        P("rays", None),
        P("rays"),
        P("region", "rays"),
        P("region", "rays"),
        P("region", None, "rays"),
        P(None, "region", "rays", None),
        P(None, "region", "rays", None),
        P(None, "region", "rays", None),
        P(None, "region", "rays"),
    )
    return jax.shard_map(
        per_device,
        mesh=mesh,
        in_specs=placed,
        out_specs=(
            P(None, "region", "rays", None),
            P(None, "region", "rays", None),
            P(None, "region", "rays", None),
            P(None, "region", "rays"),
            P("region", "rays"),
        ),
        check_vma=False,
    )
```

time: 74.8 us -> 59.4 us (0.79)
  blocking collectives: 2.31 us -> 37.7 us
  waiting for transfers between devices: 28.2 us -> 2.8 us
  starting transfers between devices: 12.1 us -> 0.58 us
  local copies, waits for them, and re-layouts: 9.03 us -> 0.01 us
  Pallas kernels: 21.7 us -> 17.4 us
    all_to_all x0 -> x2, blocking collectives: none -> 37.7 us  [the longest x1 21.6 us: per_device(): got = lax.all_to_all(send, 'region', 0, 0)]
    all_to_all x2 -> x0, waiting for transfers between devices: 26.5 us -> none  [the longest x1 13.3 us: per_device(): got = lax.all_to_all(send, 'region', 0, 0)]
    all_to_all x2 -> x0, starting transfers between devices: 12 us -> none  [the longest x1 8.23 us: per_device(): got = lax.all_to_all(send, 'region', 0, 0)]
    unnamed x30 -> x8, local copies, waits for them, and re-layouts: 8.12 us -> 0.01 us
    pallas_call x5, Pallas kernels: 21.7 us -> 17.4 us  [call(): pl.pallas_call(body, out_shape=out_shape, in_specs=specs or [spec] * len(...]
    all_gather x1 -> x0, blocking collectives: 2.31 us -> none  [per_device(): packs = lax.all_gather(pack, 'rays', axis=0)]
    ppermute x1 -> x2, waiting for transfers between devices: 1.72 us -> 2.8 us  [the longest x1 1.72 us: per_device(): parts = (grads[0], lax.ppermute(grads[1], 'rays', [(0, 1), (1, 0)]))]
    broadcast_in_dim x2 -> x0, local copies, waits for them, and re-layouts: 0.85 us -> none  [per_device(): own_direction[:, None]]
  transfers between devices with their start and end apart: 3 -> 2, of which waited for: 3 -> 2; matrix products, arithmetic and copies ran while one was open for 1% -> 0% of each run, Pallas kernels for 0% -> 0%
where the time goes in v2:
time: 59.4 us; the launch traced here: 59.2 us
  blocking collectives  37.7 us (63%)
  Pallas kernels  17.4 us (29%)
  waiting for transfers between devices  2.8 us (5%)
  between operations  0.68 us (1%)
    all_to_all x1, blocking collectives, per_device(): got = lax.all_to_all(send, 'region', 0, 0)  21.6 us
    pallas_call x5, Pallas kernels, call(): pl.pallas_call(body, out_shape=out_shape, in_specs=specs or [spec] * len(...  17.4 us
    all_to_all x1, blocking collectives, per_device(): answer = lax.all_to_all(reply, 'region', 0, 0)  16.1 us
    ppermute x1, waiting for transfers between devices, per_device(): parts = (grads[0], lax.ppermute(grads[1], 'rays', [(0, 1), (1, 0)]))  1.72 us
  transfers between devices with their start and end apart: 2, of which 2 were waited for; matrix products, arithmetic and copies ran while one was open for 0% of the time, Pallas kernels for 0%

profile of v2, /device:TPU:0, one launch (start us, length us, event | category | flops | bytes accessed | tf_op | source)
XLA Modules:
  0.0 59.2 jit_solution(3310549197005302049)
XLA Ops:
  0.6 2.0 %shard_map.137 = (bf16[784,128]{1,0:T(8,128)(2,1)S(1)}, bf16[4096,128]{1,0:T(8,128)(2,1)S(1)}, f32[16,512]{1,0:T(8,128)S(1)}, bf16[32,384]{1,0:T(8,128)(2,1)S(1)}) custom-call(f32[3,1,64,256]{3,2,1,0:T(8,128)} %refs_2_.3, f32[3,1,128,256]{3,2,1,0:T(8,128)} %refs_3_.3, f32[3,1,128,384]{3,2,1,0:T(8,128)} %refs_4_.3, f32[3,1,576]{2,1,0:T(1,128)} %refs_5_.3, ...), custom_call_target="tpu_custom_call" | custom-call | flops 1000000 | bytes 1000000 | tf_op jit(solution)/shard_map/pallas_call | solution.py:36
  2.7 0.5 collective-permute-start
  3.2 1.1 %collective-permute-done.refs_1_ = bf16[784,128]{1,0:T(8,128)(2,1)S(1)} collective-permute-done((bf16[784,128]{1,0:T(8,128)(2,1)S(1)}, bf16[784,128]{1,0:T(8,128)(2,1)S(1)}, u32[]{:S(2)}, u32[]{:S(2)}) %collective-permute-start) | collective-permute-done | bytes 200736 | tf_op jit(solution)/shard_map/ppermute | solution.py:486
  4.2 4.4 %shard_map.138 = (bf16[16,104,128]{2,1,0:T(8,128)(2,1)S(1)}, bf16[4096,256]{1,0:T(8,128)(2,1)S(1)}, bf16[4096,256]{1,0:T(8,128)(2,1)S(1)}, f32[4096,384]{1,0:T(8...) custom-call(bf16[784,128]{1,0:T(8,128)(2,1)S(1)} %get-tuple-element.23.refs_0_, ...), custom_call_target="tpu_custom_call" | custom-call | flops 1879048192 | bytes 10485760 | tf_op jit(solution)/shard_map/pallas_call | solution.py:36
  8.6 21.6 %all_to_all.10.got_ref = bf16[16,104,128]{2,1,0:T(8,128)(2,1)S(1)} all-to-all(bf16[16,104,128]{2,1,0:T(8,128)(2,1)S(1)} %get-tuple-element.26), channel_id=1, replica_groups=mesh['region'=16,'rays'=2] {'region'}, dimensions={0} | all-to-all | bytes 851968 | tf_op jit(solution)/shard_map/all_to_all | solution.py:506
  30.2 1.5 %shard_map.139 = bf16[16,104,128]{2,1,0:T(8,128)(2,1)S(1)} custom-call(bf16[16,104,128]{2,1,0:T(8,128)(2,1)S(1)} %all_to_all.10.got_ref, bf16[32,384]{1,0:T(8,128)(2,1)S(1)} %get-tuple-element.27.target_ref), custom_call_target="tpu_custom_call" | custom-call | flops 1000000 | bytes 1000000 | tf_op jit(solution)/shard_map/pallas_call | solution.py:36
  31.8 16.1 %all_to_all.11.got_ref = bf16[16,104,128]{2,1,0:T(8,128)(2,1)S(1)} all-to-all(bf16[16,104,128]{2,1,0:T(8,128)(2,1)S(1)} %shard_map.139), channel_id=1, replica_groups=mesh['region'=16,'rays'=2] {'region'}, dimensions={0} | all-to-all | bytes 851968 | tf_op jit(solution)/shard_map/all_to_all | solution.py:510
  47.9 0.0 copy-start
  47.9 0.0 copy-start.1
  47.9 0.0 copy-start.2
  47.9 0.0 copy-start.3
  47.9 8.3 %shard_map.140 = (f32[1,512]{1,0:T(1,128)}, f32[784,128]{1,0:T(8,128)S(1)}, f32[784,128]{1,0:T(8,128)S(1)}) custom-call(bf16[16,104,128]{2,1,0:T(8,128)(2,1)S(1)} %all_to_all.11.got_ref, bf16[4096,128]{1,0:T(8,128)(2,1)S(1)} %get-tuple-element.24.refs_2_.enc_ref, bf16[4096,256]{1,0:T(8,128)(2,1)S(1)} %get-tuple-element.28.one_ref, ...), custom_call_target="tpu_custom_call" | custom-call | flops 3758096384 | bytes 10485760 | tf_op jit(solution)/shard_map/pallas_call | solution.py:36
  56.2 0.1 collective-permute-start.1
  56.3 1.7 %collective-permute-done.1.refs_1_ = f32[784,128]{1,0:T(8,128)S(1)} collective-permute-done((f32[784,128]{1,0:T(8,128)S(1)}, f32[784,128]{1,0:T(8,128)S(1)}, u32[]{:S(2)}, u32[]{:S(2)}) %collective-permute-start.1) | collective-permute-done | bytes 401440 | tf_op jit(solution)/shard_map/ppermute | solution.py:528
  58.0 0.0 copy-done
  58.0 0.0 copy-done.1
  58.0 0.0 copy-done.2
  58.0 0.0 copy-done.3
  58.0 1.1 %shard_map.141 = (f32[3,1,64,256]{3,2,1,0:T(8,128)}, f32[3,1,128,256]{3,2,1,0:T(8,128)}, f32[3,1,128,384]{3,2,1,0:T(8,128)}, f32[3,1,576]{2,1,0:T(1,128)}) custom-call(f32[784,128]{1,0:T(8,128)S(1)} %get-tuple-element.34.refs_0_, f32[784,128]{1,0:T(8,128)S(1)} %collective-permute-done.1.refs_1_, f32[3,1,64,256]{3,2,1,0:T(8,128)S(1)} %copy-done.2, ...), custom_call_target="tpu_custom_call" | custom-call | flops 1000000 | bytes 1000000 | tf_op jit(solution)/shard_map/pallas_call | solution.py:36
Async XLA Ops:
  2.7 1.6 %collective-permute-start = (bf16[784,128]{1,0:T(8,128)(2,1)S(1)}, bf16[784,128]{1,0:T(8,128)(2,1)S(1)}, u32[]{:S(2)}, u32[]{:S(2)}) collective-permute-start(bf16[784,128]{1,0:T(8,128)(2,1)S(1)} %get-tuple-element.23.refs_0_), channel_id=1, source_target_pairs={{0,1},{1,0},{2,3},{3,2},{4,5},{5,4},{6,7},{7,6},{8,9},{9,8},{10,11... | collective-permute-start | bytes 602120 | tf_op jit(solution)/shard_map/ppermute | solution.py:486
  47.9 10.1 %copy-start = (f32[3,1,128,384]{3,2,1,0:T(8,128)S(1)}, f32[3,1,128,384]{3,2,1,0:T(8,128)}, u32[]{:S(2)}) copy-start(f32[3,1,128,384]{3,2,1,0:T(8,128)} %refs_4_.3) | copy-start | bytes 1769476
  47.9 10.1 %copy-start.1 = (f32[3,1,128,256]{3,2,1,0:T(8,128)S(1)}, f32[3,1,128,256]{3,2,1,0:T(8,128)}, u32[]{:S(2)}) copy-start(f32[3,1,128,256]{3,2,1,0:T(8,128)} %refs_3_.3) | copy-start | bytes 1179652
  47.9 10.1 %copy-start.2 = (f32[3,1,64,256]{3,2,1,0:T(8,128)S(1)}, f32[3,1,64,256]{3,2,1,0:T(8,128)}, u32[]{:S(2)}) copy-start(f32[3,1,64,256]{3,2,1,0:T(8,128)} %refs_2_.3) | copy-start | bytes 589828
  47.9 10.1 %copy-start.3 = (f32[3,1,576]{2,1,0:T(1,128)S(1)}, f32[3,1,576]{2,1,0:T(1,128)}, u32[]{:S(2)}) copy-start(f32[3,1,576]{2,1,0:T(1,128)} %refs_5_.3) | copy-start | bytes 20740
  56.2 1.8 %collective-permute-start.1 = (f32[784,128]{1,0:T(8,128)S(1)}, f32[784,128]{1,0:T(8,128)S(1)}, u32[]{:S(2)}, u32[]{:S(2)}) collective-permute-start(f32[784,128]{1,0:T(8,128)S(1)} %get-tuple-element.35), channel_id=1, source_target_pairs={{0,1},{1,0},{2,3},{3,2},{4,5},{5,4},{6,7},{7,6},{8,9},{9,8},{10,11... | collective-permute-start | bytes 1204232 | tf_op jit(solution)/shard_map/ppermute | solution.py:528

commit v3 on v2

v3 whole, which is shorter than its diff:
```python
import functools

import jax
import jax.numpy as jnp
from jax import lax
from jax.experimental import pallas as pl
from jax.experimental.pallas import tpu as pltpu
from jax.sharding import PartitionSpec as P

BINS = 64
LANES = 128
QUAD = 4

depth_scale = 4.0
beta_one = 0.9
beta_two = 0.999
learn_rate = 0.001
epsilon = 1e-08
first_fix = 1.0 - 0.9**10
second_fix = 1.0 - 0.999**10

f32 = jnp.float32
bf16 = jnp.bfloat16


def in_vmem(value):
    return pltpu.with_memory_space_constraint(value, pltpu.VMEM)


def in_hbm(value):
    return pltpu.with_memory_space_constraint(value, pltpu.HBM)


def call(body, out_shape, inputs, limit, scratch=(), specs=None, flops=1000000, moved=1000000):
    many = isinstance(out_shape, (tuple, list))
    spec = pl.BlockSpec(memory_space=pltpu.VMEM)
    return pl.pallas_call(
        body,
        out_shape=out_shape,
        in_specs=specs or [spec] * len(inputs),
        out_specs=tuple(spec for _ in out_shape) if many else spec,
        scratch_shapes=list(scratch),
        compiler_params=pltpu.CompilerParams(vmem_limit_bytes=limit * 1024 * 1024),
        cost_estimate=pl.CostEstimate(flops=flops, bytes_accessed=moved, transcendentals=0),
    )(*inputs)


def blocks(width):
    return [slice(LANES * k, LANES * (k + 1)) for k in range(width // LANES)]


def wide_rows(count):
    return -(-count // LANES)


def row_block(row, rows):
    width = row.shape[1]
    padded = wide_rows(width) * LANES
    if padded != width:
        row = jnp.concatenate([row, jnp.zeros((1, padded - width), f32)], 1)
    place = lax.broadcasted_iota(jnp.int32, (rows, LANES), 0)
    out = jnp.zeros((rows, LANES), f32)
    for k, cut in enumerate(blocks(padded)):
        out = jnp.where(place == k, jnp.broadcast_to(row[:, cut], (rows, LANES)), out)
    return out


def block_row(block, count):
    return jnp.concatenate([block[k : k + 1] for k in range(count)], 1)


def split3(value):
    high = value.astype(bf16).astype(f32)
    rest = value - high
    mid = rest.astype(bf16).astype(f32)
    return (high, mid, rest - mid)


def lanes_of(shape):
    return lax.broadcasted_iota(jnp.int32, shape, 1)


def turned(rows, ray_count):
    fill = LANES - rows.shape[0]
    return jnp.concatenate([rows, jnp.zeros((fill, ray_count), f32)], 0).T


def fold(extra):
    rays = extra.shape[0]
    groups = rays // 8
    out = extra[:8]
    for g in range(1, groups):
        out = out + pltpu.roll(extra[8 * g : 8 * (g + 1)], (LANES // groups) * g, 1)
    return out


def unfold(folded, rays, used):
    groups = rays // 8
    keep = lanes_of(folded.shape) < used
    parts = []
    for g in range(groups):
        piece = pltpu.roll(folded, LANES - (LANES // groups) * g, 1) if g else folded
        parts.append(jnp.where(keep, piece, 0.0))
    return jnp.concatenate(parts, 0)


def prepare_body(*refs, unit_length, slots):
    ins, refs = (refs[:10], refs[10:])
    pack_ref, enc_ref, geometry_ref, target_ref, *held, flat_geometry, flat_position, sems = refs
    group_rows = target_ref.shape[0]
    spot_in_quad = lax.rem(lax.axis_index("region"), slots)
    copies = []

    def fetch(source, place):
        copies.append(pltpu.make_async_copy(source, place, sems.at[len(copies)]))
        copies[-1].start()

    def group(k):
        return pl.ds(pl.multiple_of((spot_in_quad ^ k) * group_rows, group_rows), group_rows)

    for ref, hold in zip(ins[:4], held[:4]):
        fetch(ref.at[0], hold)
    for ref, hold in zip(ins[4:9], held[4:9]):
        fetch(ref, hold)
    fetch(ins[9].at[group(0)], target_ref)
    spot = 0
    for copy, hold in zip(copies[:3], held[:3]):
        copy.wait()
        rows, width = hold.shape[1:]
        for cut in blocks(width):
            pack_ref[spot : spot + rows, :] = hold[0, :, cut].astype(bf16)
            spot += rows
    for copy in copies[3:]:
        copy.wait()
    pack_ref[spot : spot + 16, :] = row_block(held[3][...], 16).astype(bf16)
    codes, bins, entry, exit_, direction = held[4:9]
    bins = bins[0].astype(f32)
    samples, ray_count = bins.shape
    slot = lax.broadcasted_iota(jnp.int32, bins.shape, 0)
    following = jnp.where(slot == samples - 1, float(BINS), pltpu.roll(bins, samples - 1, 0))
    inside = ((slot >= entry[...]) & (slot < exit_[...])).astype(f32)
    flat_geometry[:samples] = (following - bins) * unit_length * inside
    flat_geometry[samples : samples + 1] = direction[...].astype(f32)
    flat_position[...] = turned((bins + 0.5) / BINS, ray_count)
    for k in range(slots):
        geometry_ref[k] = flat_geometry[:, group(k)]
        code_zero = codes[0, group(k)].astype(f32)
        code_one = codes[1, group(k)].astype(f32)
        position = flat_position[group(k), :]
        for j in range(samples):
            encoded = code_zero + position[:, j : j + 1] * code_one
            enc_ref[k, group_rows * j : group_rows * (j + 1), :] = encoded.astype(bf16)


def assemble(packs, shapes, vec_share):
    shards = len(packs)
    spot = 0
    mats = []
    for rows, width in shapes:
        pieces = []
        for cut in blocks(width):
            pieces.append(jnp.concatenate([p[spot : spot + rows, :] for p in packs], 0))
            spot += rows
        mats.append(jnp.concatenate(pieces, 1))
    vec_total = vec_share * shards
    vec = jnp.zeros((1, vec_total), f32)
    for s, p in enumerate(packs):
        block = p[spot : spot + 16, :].astype(f32)
        count = wide_rows(vec_share)
        row = block_row(block, count)
        fill = vec_total - count * LANES
        if fill:
            row = jnp.concatenate([row, jnp.zeros((1, fill), f32)], 1)
        if s:
            row = pltpu.roll(row, vec_share * s, 1)
        vec = vec + row
    return (*mats, vec)


def forward_slots(slots, weights, enc_ref, geometry_ref, message_refs, kept):
    in_weight, mid_ref, head_ref, vec = weights
    one_ref, two_ref, colour_ref, scalar_ref = kept
    samples, ray_count = scalar_ref.shape[2:]
    hidden = mid_ref.shape[0]
    feat = colour_ref.shape[2]
    bias_one = vec[:, :hidden]
    bias_two = vec[:, hidden : 2 * hidden]
    bias_feat = vec[:, 3 * hidden :]
    lane = lanes_of((ray_count, LANES))
    for i, k in enumerate(slots):
        one = jnp.dot(enc_ref[k], in_weight, preferred_element_type=f32) + bias_one
        one = jnp.maximum(one, 0.0).astype(bf16)
        one_ref[i] = one
        two = jnp.dot(one, mid_ref[...], preferred_element_type=f32) + bias_two
        two = jnp.maximum(two, 0.0).astype(bf16)
        two_ref[i] = two
        raw = jnp.dot(two, head_ref[...], preferred_element_type=f32)
        colour_ref[i] = 0.5 * jnp.tanh(0.5 * (raw[:, :feat] + bias_feat)) + 0.5
        density = jnp.zeros((ray_count, LANES), f32)
        for j in range(samples):
            rows = slice(ray_count * j, ray_count * (j + 1))
            density = jnp.where(lane == j, raw[rows, feat:], density)
        density = density.T[:samples]
        geometry = geometry_ref[k, :samples]
        soft = jnp.maximum(density, 0.0) + jnp.log1p(jnp.exp(-jnp.abs(density)))
        optical = soft * geometry
        before = [jnp.zeros((1, ray_count), f32)]
        for j in range(samples):
            before.append(before[-1] + optical[j : j + 1])
        depth = before.pop()
        optical_before = jnp.concatenate(before, 0)
        opacity = jnp.tanh(0.5 * optical) * (1.0 + jnp.exp(-optical))
        local_weight = jnp.exp(-optical_before) * opacity
        sig = 0.5 * jnp.tanh(0.5 * density) + 0.5
        scalar_ref[i, 0] = local_weight
        scalar_ref[i, 1] = jnp.exp(-(optical_before + optical))
        scalar_ref[i, 2] = geometry * sig
        direction = geometry_ref[k, samples : samples + 1]
        columns = turned(
            jnp.concatenate([*split3(depth), direction, local_weight], 0), ray_count
        )
        total = jnp.zeros((ray_count, feat), f32)
        for j in range(samples):
            rows = slice(ray_count * j, ray_count * (j + 1))
            total = total + columns[:, 4 + j : 5 + j] * colour_ref[i, rows, :]
        extra = jnp.where(lane < 4, columns, 0.0)
        message_refs[i][...] = as_message([total[:, cut] for cut in blocks(feat)], extra)


def as_message(parts, extra):
    return jnp.concatenate([*parts, fold(extra)], 0).astype(bf16)


def from_message(value, rays, used):
    value = value.astype(f32)
    count = value.shape[0] // rays
    parts = [value[rays * k : rays * (k + 1)] for k in range(count)]
    return (parts, unfold(value[rays * count :], rays, used))


def forward_first_body(*refs, shapes, vec_share, pair, slots):
    both = None
    if pair:
        own_ref, other_ref, *refs, both = refs
        mine = lax.axis_index("rays")
        both[mine] = own_ref[...]
        both[1 - mine] = other_ref[...]
        packs = [both.at[0], both.at[1]]
    else:
        packs_ref, *refs = refs
        packs = [packs_ref.at[s] for s in range(packs_ref.shape[0])]
    enc_ref, geometry_ref, in_ref, mid_ref, head_ref, vec_ref, *refs = refs
    hidden = mid_ref.shape[0]
    in_weight, mid_weight, feat_weight, vec = assemble(packs, shapes, vec_share)
    density_row = vec[:, 2 * hidden : 3 * hidden]
    density_cols = jnp.broadcast_to(density_row, (LANES, hidden)).T
    in_ref[...] = in_weight
    mid_ref[...] = mid_weight
    head_ref[...] = jnp.concatenate([feat_weight, density_cols.astype(bf16)], 1)
    vec_ref[...] = vec
    weights = (in_weight, mid_ref, head_ref, vec)
    forward_slots(slots, weights, enc_ref, geometry_ref, refs[4:], refs[:4])


def forward_own_body(in_ref, mid_ref, head_ref, vec_ref, enc_ref, geometry_ref, *refs):
    weights = (in_ref[...], mid_ref, head_ref, vec_ref[...])
    forward_slots([0], weights, enc_ref, geometry_ref, refs[4:], refs[:4])


def sides(values):
    below, above = ([jnp.zeros_like(values[0])], [jnp.zeros_like(values[0])])
    for q in range(len(values) - 1):
        below.append(below[-1] + values[q])
        above.append(above[-1] + values[len(values) - 1 - q])
    return (below, above[::-1])


def gather_messages(refs, store, own, rays):
    for k, ref in enumerate(refs):
        store[own ^ k] = ref[...]
    members = [from_message(store[p], rays, 4) for p in range(len(refs))]
    parts = [m[0] for m in members]
    extras = [m[1] for m in members]
    lane = lanes_of(extras[0].shape)
    depth = [jnp.sum(jnp.where(lane < 3, e, 0.0), 1, keepdims=True) for e in extras]
    onward = extras[0][:, 3:4] < 0.5
    below, above = sides(depth)
    trans = [jnp.exp(-jnp.where(onward, b, a)) for b, a in zip(below, above)]
    return (parts, depth, onward, trans)


def weighted_sum(factors, parts):
    out = []
    for k in range(len(parts[0])):
        total = factors[0] * parts[0][k]
        for factor, part in zip(factors[1:], parts[1:]):
            total = total + factor * part[k]
        out.append(total)
    return out


def inner(left, right):
    total = left[0] * right[0]
    for a, b in zip(left[1:], right[1:]):
        total = total + a * b
    return jnp.sum(total, 1, keepdims=True)


def plane_body(*refs, rays):
    *messages, out_ref, store = refs
    own = lax.rem(lax.axis_index("region"), len(messages))
    parts, depth, onward, trans = gather_messages(messages, store, own, rays)
    total = depth[0]
    for value in depth[1:]:
        total = total + value
    lane = lanes_of((rays, LANES))
    extra = jnp.where(lane == 3, jnp.where(onward, 0.0, 1.0), 0.0)
    for i, piece in enumerate(split3(total)):
        extra = jnp.where(lane == i, piece, extra)
    out_ref[...] = as_message(weighted_sum(trans, parts), extra)


def owner_body(*refs, slots, planes):
    quad_refs, plane_refs = (refs[:slots], refs[slots : slots + planes])
    target_ref, *out_refs, quad_store, plane_store, reply = refs[slots + planes :]
    rays, feat = target_ref.shape
    region = lax.axis_index("region")
    own, own_plane = (lax.rem(region, slots), lax.div(region, slots))
    parts, _, onward, trans = gather_messages(quad_refs, quad_store, own, rays)
    plane_parts, _, _, plane_trans = gather_messages(plane_refs, plane_store, own_plane, rays)
    rendered = weighted_sum(plane_trans, plane_parts)
    grads = [
        (value - target_ref[:, cut].astype(f32)).astype(bf16).astype(f32)
        for value, cut in zip(rendered, blocks(feat))
    ]

    def later(values):
        below, above = sides(values)
        return [jnp.where(onward, a, b) for b, a in zip(below, above)]

    plane_after = later([t * inner(grads, p) for t, p in zip(plane_trans, plane_parts)])
    ahead = jnp.zeros((rays, 1), f32)
    reach = jnp.zeros((rays, 1), f32)
    for z in range(planes):
        ahead = jnp.where(own_plane == z, plane_trans[z], ahead)
        reach = jnp.where(own_plane == z, plane_after[z], reach)
    trans = [ahead * t for t in trans]
    after = later([t * inner(grads, p) for t, p in zip(trans, parts)])
    lane = lanes_of((rays, LANES))
    for p in range(slots):
        extra = jnp.zeros((rays, LANES), f32)
        for i, piece in enumerate((*split3(trans[p]), *split3(after[p] + reach))):
            extra = jnp.where(lane == i, piece, extra)
        reply[p] = fold(extra)
    for k, out_ref in enumerate(out_refs):
        out_ref[...] = jnp.concatenate([*grads, reply[own ^ k]], 0).astype(bf16)


def over_rows(left, right):
    return lax.dot_general(left, right, (((0,), (0,)), ((), ())), preferred_element_type=f32)


def across(left, right):
    return lax.dot_general(left, right, (((1,), (1,)), ((), ())), preferred_element_type=f32)


def backward_body(*refs, slots, group_count, shapes, vec_share, shards):
    last = 0 not in slots
    messages, refs = (refs[: len(slots)], refs[len(slots) :])
    enc_ref, one_ref, two_ref, colour_ref, scalar_ref, mid_ref, head_ref, *refs = refs
    if last:
        earlier, refs = (refs[:5], refs[5:])
        depth_ref, *outs, head_grad_ref, second_ref, first_ref, shares = refs
    else:
        *outs, depth_ref, head_grad_ref, second_ref, first_ref = refs
    samples, ray_count = scalar_ref.shape[2:]
    feat = colour_ref.shape[2]
    spot_in_quad = lax.rem(lax.axis_index("region"), group_count)

    def group(k):
        return pl.ds(pl.multiple_of((spot_in_quad ^ k) * ray_count, ray_count), ray_count)

    if last:
        depth_ref[:, group(0)] = earlier[4][...]
    lane = lanes_of((ray_count, LANES))
    first_sum, second_sum, colour_sum = (0.0, 0.0, 0.0)
    for i, k in enumerate(slots):
        grads, extra = from_message(messages[i][...], ray_count, 6)
        grad = jnp.concatenate(grads, 1)
        extra = extra.T
        trans = extra[0:1] + extra[1:2] + extra[2:3]
        after = extra[3:4] + extra[4:5] + extra[5:6]
        if last:
            depth_ref[:, group(k)] = -after
        else:
            depth_ref[...] = -after
        sample_grad = jnp.zeros((ray_count, LANES), f32)
        for j in range(samples):
            rows = slice(ray_count * j, ray_count * (j + 1))
            product = jnp.sum(colour_ref[i, rows, :] * grad, 1, keepdims=True)
            sample_grad = jnp.where(lane == j, product, sample_grad)
        sample_grad = sample_grad.T[:samples]
        local_weight = scalar_ref[i, 0]
        weighted = local_weight * sample_grad
        later = [jnp.zeros((1, ray_count), f32)]
        for j in range(samples - 1, 0, -1):
            later.append(later[-1] + weighted[j : j + 1])
        later = jnp.concatenate(later[::-1], 0)
        optical_grad = trans * (scalar_ref[i, 1] * sample_grad - later) - after
        density_grad = optical_grad * scalar_ref[i, 2]
        columns = turned(jnp.concatenate([trans * local_weight, density_grad], 0), ray_count)
        for j in range(samples):
            rows = slice(ray_count * j, ray_count * (j + 1))
            colour = colour_ref[i, rows, :]
            colour_grad = (columns[:, j : j + 1] * grad * colour * (1.0 - colour)).astype(bf16)
            density_part = jnp.where(lane == samples + j, columns, 0.0).astype(bf16)
            head_grad_ref[i, rows, :] = jnp.concatenate([colour_grad, density_part], 1)
            colour_sum = colour_sum + jnp.sum(colour_grad.astype(f32), 0, keepdims=True)
        hidden_grad = across(head_grad_ref[i], head_ref[...])
        second = jnp.where(two_ref[i].astype(f32) > 0, hidden_grad, 0.0).astype(bf16)
        second_ref[i] = second
        second_sum = second_sum + jnp.sum(second.astype(f32), 0, keepdims=True)
        below = across(second, mid_ref[...])
        first = jnp.where(one_ref[i].astype(f32) > 0, below, 0.0).astype(bf16)
        first_ref[i] = first
        first_sum = first_sum + jnp.sum(first.astype(f32), 0, keepdims=True)

    def rows_of(ref):
        return ref[...].reshape(-1, ref.shape[2])

    encoded = enc_ref[slots[0] : slots[-1] + 1].reshape(-1, enc_ref.shape[2])
    in_grad = over_rows(encoded, rows_of(first_ref))
    mid_grad = over_rows(rows_of(one_ref), rows_of(second_ref))
    head_grad = over_rows(rows_of(two_ref), rows_of(head_grad_ref))
    density_sum = jnp.sum(head_grad[:, feat:].T, 0, keepdims=True)
    vec = jnp.concatenate([first_sum, second_sum, density_sum, colour_sum], 1)
    values = [in_grad, mid_grad, head_grad[:, :feat], vec]
    if not last:
        for value, ref in zip(values, outs):
            ref[...] = value
        return
    values = [value + ref[...] for value, ref in zip(values, earlier)]
    vec = values.pop()
    mine = lax.axis_index("rays")
    total = vec.shape[1]
    for s in range(shards):
        place = lax.rem(s + shards - mine, shards) if shards == 2 else s
        spot = 0
        for (rows, width), value in zip(shapes, values):
            for cut in blocks(width):
                shares[place, spot : spot + rows, :] = value[rows * s : rows * (s + 1), cut]
                spot += rows
        row = pltpu.roll(vec, total - vec_share * s, 1) if s else vec
        shares[place, spot : spot + 16, :] = row_block(row[:, : wide_rows(vec_share) * LANES], 16)
    if shards == 2:
        outs[0][...] = shares[0]
        outs[1][...] = shares[1]
    else:
        outs[0][...] = shares[...]


def adam_body(*refs, shards):
    grad_refs = refs[:shards]
    state_refs, out_refs = (refs[shards : shards + 4], refs[shards + 4 :])

    def update(stacked, gradient):
        first_moment = beta_one * stacked[1] + (1.0 - beta_one) * gradient
        second = beta_two * stacked[2] + (1.0 - beta_two) * gradient * gradient
        step = first_moment / first_fix / (jnp.sqrt(second / second_fix) + epsilon)
        return (stacked[0] - learn_rate * step, first_moment, second)

    def gathered(spot, rows):
        total = grad_refs[0][spot : spot + rows, :]
        for ref in grad_refs[1:]:
            total = total + ref[spot : spot + rows, :]
        return total

    spot = 0
    for ref, out in zip(state_refs[:3], out_refs[:3]):
        rows, width = ref.shape[2:]
        for cut in blocks(width):
            new = update([ref[i, 0, :, cut] for i in range(3)], gathered(spot, rows))
            spot += rows
            for i in range(3):
                out[i, 0, :, cut] = new[i]
    ref, out = (state_refs[3], out_refs[3])
    share = ref.shape[2]
    gradient = block_row(gathered(spot, 16), wide_rows(share))[:, :share]
    new = update([ref[i] for i in range(3)], gradient)
    for i in range(3):
        out[i] = new[i]


def shaped(shape, dtype):
    return jax.ShapeDtypeStruct(shape, dtype)


def swap(value, distance, size):
    return lax.ppermute(value, "region", [(i, i ^ distance) for i in range(size)])


def per_device(
    ray_codes,
    target,
    direction,
    entries,
    exits,
    depth_bins,
    in_layer,
    mid_layer,
    feat_layer,
    vectors,
):
    regions = lax.axis_size("region")
    shards = lax.axis_size("rays")
    samples, ray_count = depth_bins.shape[1:]
    quad = min(QUAD, regions)
    planes = regions // quad
    rays = ray_count // quad
    layers = (in_layer, mid_layer, feat_layer)
    states = (*layers, vectors)
    shapes = tuple(layer.shape[2:] for layer in layers)
    vec_share = vectors.shape[2]
    hidden = shapes[0][1]
    feat = shapes[2][1]
    code_width = ray_codes.shape[2]
    pack_rows = sum(rows * (width // LANES) for rows, width in shapes) + 16
    rows = samples * rays
    sizes = dict(shapes=shapes, vec_share=vec_share)
    pair = shards == 2
    flops = 2 * rows * (code_width * hidden + hidden * hidden + hidden * (feat + LANES))

    arguments = (*states, ray_codes, depth_bins, entries, exits, direction[None], target)
    pack, encoded, geometry, own_target = call(
        functools.partial(prepare_body, unit_length=depth_scale / (regions * BINS), slots=quad),
        (
            pltpu.VMEM((pack_rows, LANES), bf16),
            pltpu.VMEM((quad, rows, code_width), bf16),
            pltpu.VMEM((quad, samples + 8, rays), f32),
            pltpu.VMEM((rays, feat), bf16),
        ),
        [in_hbm(a) for a in arguments],
        16,
        scratch=[pltpu.VMEM(a.shape[1:], f32) for a in states]
        + [pltpu.VMEM(a.shape, a.dtype) for a in arguments[4:9]]
        + [
            pltpu.VMEM((samples + 8, ray_count), f32),
            pltpu.VMEM((ray_count, LANES), f32),
            pltpu.SemaphoreType.DMA((10,)),
        ],
        specs=[pl.BlockSpec(memory_space=pltpu.HBM)] * 10,
    )
    if pair:
        packs = (pack, lax.ppermute(pack, "rays", [(0, 1), (1, 0)]))
    else:
        packs = (lax.all_gather(pack, "rays", axis=0),)

    message = pltpu.VMEM((rays * (feat // LANES) + 8, LANES), bf16)

    def kept_shapes(count):
        return (
            pltpu.VMEM((count, rows, hidden), bf16),
            pltpu.VMEM((count, rows, hidden), bf16),
            pltpu.VMEM((count, rows, feat), f32),
            pltpu.VMEM((count, 3, samples, rays), f32),
        )

    def moved(count):
        return count * rows * (feat + hidden) * 4

    others = tuple(range(1, quad))
    found = call(
        functools.partial(forward_first_body, pair=pair, slots=others, **sizes),
        (
            pltpu.VMEM((shapes[0][0] * shards, hidden), bf16),
            pltpu.VMEM((hidden, hidden), bf16),
            pltpu.VMEM((hidden, feat + LANES), bf16),
            pltpu.VMEM((1, vec_share * shards), f32),
        )
        + kept_shapes(quad - 1)
        + (message,) * (quad - 1),
        [in_vmem(v) for v in (*packs, encoded, geometry)],
        16,
        scratch=[pltpu.VMEM((2, pack_rows, LANES), bf16)] if pair else (),
        flops=(quad - 1) * flops,
        moved=moved(quad - 1),
    )
    weights, kept, sent = (found[:4], found[4:8], found[8:])
    got = [swap(value, k, regions) for k, value in zip(others, sent)]
    *kept_own, own_message = call(
        forward_own_body,
        kept_shapes(1) + (message,),
        [in_vmem(v) for v in (*weights, encoded, geometry)],
        16,
        flops=flops,
        moved=moved(1),
    )
    quad_messages = [in_vmem(v) for v in (own_message, *got)]
    store = pltpu.VMEM((quad, *message.shape), bf16)
    plane_store = pltpu.VMEM((planes, *message.shape), bf16)
    plane_message = call(
        functools.partial(plane_body, rays=rays), message, quad_messages, 16, scratch=[store]
    )
    plane_messages = [plane_message] + [
        swap(plane_message, quad * k, regions) for k in range(1, planes)
    ]
    replies = call(
        functools.partial(owner_body, slots=quad, planes=planes),
        (message,) * quad,
        quad_messages + [in_vmem(v) for v in (*plane_messages, own_target)],
        16,
        scratch=[store, plane_store, pltpu.VMEM((quad, 8, LANES), f32)],
    )
    answers = [swap(value, k, regions) for k, value in zip(others, replies[1:])]

    def rows_scratch(count):
        return [
            pltpu.VMEM((count, rows, feat + LANES), bf16),
            pltpu.VMEM((count, rows, hidden), bf16),
            pltpu.VMEM((count, rows, hidden), bf16),
        ]

    earlier = call(
        functools.partial(
            backward_body, slots=(0,), group_count=quad, shards=shards, **sizes
        ),
        (
            pltpu.VMEM((shapes[0][0] * shards, hidden), f32),
            pltpu.VMEM((hidden, hidden), f32),
            pltpu.VMEM((hidden, feat), f32),
            pltpu.VMEM((1, vec_share * shards), f32),
            pltpu.VMEM((1, rays), f32),
        ),
        [in_vmem(v) for v in (replies[0], encoded, *kept_own, weights[1], weights[2])],
        16,
        scratch=rows_scratch(1),
        flops=2 * flops,
        moved=moved(1),
    )
    share = pltpu.VMEM((pack_rows, LANES), f32)
    shares = shaped((shards, pack_rows, LANES), f32)
    depth_grad, *grads = call(
        functools.partial(
            backward_body, slots=others, group_count=quad, shards=shards, **sizes
        ),
        (shaped((1, ray_count), f32),) + ((share, share) if pair else (shares,)),
        [in_vmem(v) for v in (*answers, encoded, *kept, weights[1], weights[2], *earlier)],
        24,
        scratch=rows_scratch(quad - 1) + [pltpu.VMEM((shards, pack_rows, LANES), f32)],
        flops=2 * (quad - 1) * flops,
        moved=moved(quad - 1),
    )
    if pair:
        parts = (grads[0], lax.ppermute(grads[1], "rays", [(0, 1), (1, 0)]))
    else:
        exchanged = lax.all_to_all(grads[0], "rays", 0, 0)
        parts = tuple(exchanged[s] for s in range(shards))
    new = call(
        functools.partial(adam_body, shards=shards),
        tuple(shaped(s.shape, f32) for s in states),
        (*parts, *states),
        16,
    )
    return (*new, depth_grad)


def solution(mesh):
    placed = (
        P(None, "rays", None),
        P("rays", None),
        P("rays"),
        P("region", "rays"),
        P("region", "rays"),
        P("region", None, "rays"),
        P(None, "region", "rays", None),
        P(None, "region", "rays", None),
        P(None, "region", "rays", None),
        P(None, "region", "rays"),
    )
    return jax.shard_map(
        per_device,
        mesh=mesh,
        in_specs=placed,
        out_specs=(
            P(None, "region", "rays", None),
            P(None, "region", "rays", None),
            P(None, "region", "rays", None),
            P(None, "region", "rays"),
            P("region", "rays"),
        ),
        check_vma=False,
    )
```

time: 59.4 us -> 46.2 us (0.78)
  blocking collectives: 37.7 us -> 0 us
  waiting for transfers between devices: 2.8 us -> 15.6 us
  starting transfers between devices: 0.58 us -> 13.1 us
  Pallas kernels: 17.4 us -> 16.7 us
    all_to_all x2 -> x0, blocking collectives: 37.7 us -> none  [the longest x1 21.6 us: per_device(): got = lax.all_to_all(send, 'region', 0, 0)]
    ppermute x0 -> x9, waiting for transfers between devices: none -> 12.8 us  [swap(): lax.ppermute(value, 'region', [(i, i ^ distance) for i in range(size)])]
    ppermute x0 -> x9, starting transfers between devices: none -> 12.5 us  [swap(): lax.ppermute(value, 'region', [(i, i ^ distance) for i in range(size)])]
    pallas_call x5 -> x8, Pallas kernels: 17.4 us -> 16.7 us  [call(): pl.pallas_call(body, out_shape=out_shape, in_specs=specs or [spec] * len(...]
  transfers between devices with their start and end apart: 2 -> 11, of which waited for: 2 -> 9; matrix products, arithmetic and copies ran while one was open for 0% -> 0% of each run, Pallas kernels for 0% -> 8%
where the time goes in v3:
time: 46.2 us; the launch traced here: 46.1 us
  Pallas kernels  16.7 us (36%)
  waiting for transfers between devices  15.6 us (34%)
  starting transfers between devices  13.1 us (28%)
  between operations  0.71 us (2%)
    pallas_call x8, Pallas kernels, call(): pl.pallas_call(body, out_shape=out_shape, in_specs=specs or [spec] * len(...  16.7 us
    ppermute x9, waiting for transfers between devices, swap(): lax.ppermute(value, 'region', [(i, i ^ distance) for i in range(size)])  12.8 us
    ppermute x9, starting transfers between devices, swap(): lax.ppermute(value, 'region', [(i, i ^ distance) for i in range(size)])  12.5 us
    ppermute x1, waiting for transfers between devices, per_device(): parts = (grads[0], lax.ppermute(grads[1], 'rays', [(0, 1), (1, 0)]))  1.72 us
    ppermute x1, waiting for transfers between devices, per_device(): packs = (pack, lax.ppermute(pack, 'rays', [(0, 1), (1, 0)]))  1.08 us
  transfers between devices with their start and end apart: 11, of which 9 were waited for; matrix products, arithmetic and copies ran while one was open for 0% of the time, Pallas kernels for 8%

profile of v3, /device:TPU:0, one launch (start us, length us, event | category | flops | bytes accessed | tf_op | source)
XLA Modules:
  0.0 46.1 jit_solution(15652988696609543704)
XLA Ops:
  0.6 2.2 %shard_map.137 = (bf16[784,128]{1,0:T(8,128)(2,1)S(1)}, bf16[4,1024,128]{2,1,0:T(8,128)(2,1)S(1)}, f32[4,16,128]{2,1,0:T(8,128)S(1)}, bf16[128,384]{1,0:T(8,128)(2,1)S(1)}) custom-call(f32[3,1,64,256]{3,2,1,0:T(8,128)} %refs_2_.3, f32[3,1,128,256]{3,2,1,0:T(8,128)} %refs_3_.3, f32[3,1,128,384]{3,2,1,0:T(8,128)} %refs_4_.3, f32[3,1,576]{2,1,0:T(1,128)} %refs_5_.3, ...), custom_call_target="tpu_custom_call" | custom-call | flops 1000000 | bytes 1000000 | tf_op jit(solution)/shard_map/pallas_call | solution.py:37
  2.8 0.5 %collective-permute-start = (bf16[784,128]{1,0:T(8,128)(2,1)S(1)}, bf16[784,128]{1,0:T(8,128)(2,1)S(1)}, u32[]{:S(2)}, u32[]{:S(2)}) collective-permute-start(bf16[784,128]{1,0:T(8,128)(2,1)S(1)} %get-tuple-element.41.refs_0_), channel_id=1, source_target_pairs={{0,1},{1,0},{2,3},{3,2},{4,5},{5,4},{6,7},{7,6},{8,9},{9,8},{10,11... | collective-permute-start | bytes 602120 | tf_op jit(solution)/shard_map/ppermute | solution.py:554
  3.3 1.1 %collective-permute-done.refs_1_ = bf16[784,128]{1,0:T(8,128)(2,1)S(1)} collective-permute-done((bf16[784,128]{1,0:T(8,128)(2,1)S(1)}, bf16[784,128]{1,0:T(8,128)(2,1)S(1)}, u32[]{:S(2)}, u32[]{:S(2)}) %collective-permute-start) | collective-permute-done | bytes 200736 | tf_op jit(solution)/shard_map/ppermute | solution.py:554
  4.4 2.7 %shard_map.138 = (bf16[128,256]{1,0:T(8,128)(2,1)S(1)}, bf16[256,256]{1,0:T(8,128)(2,1)S(1)}, bf16[256,512]{1,0:T(8,128)(2,1)S(1)}, f32[1,1152]{1,0:T(1,128)S(1)...) custom-call(bf16[784,128]{1,0:T(8,128)(2,1)S(1)} %get-tuple-element., ...), custom_call_target="tpu_custom_call" | custom-call | flops 1409286144 | bytes 7864320 | tf_op jit(solution)/shard_map/pallas_call | solution.py:37
  7.1 2.9 %collective-permute-start.1 = (bf16[392,128]{1,0:T(8,128)(2,1)S(1)}, bf16[392,128]{1,0:T(8,128)(2,1)S(1)}, u32[]{:S(2)}, u32[]{:S(2)}) collective-permute-start(bf16[392,128]{1,0:T(8,128)(2,1)S(1)} %get-tuple-element.49), channel_id=1, source_target_pairs={{0,2},{2,0},{4,6},{6,4},{8,10},{10,8},{12,14},{14,12},{16,18},{18,... | collective-permute-start | bytes 301064 | tf_op jit(solution)/shard_map/ppermute | solution.py:499
  10.0 1.5 %collective-permute-start.2 = (bf16[392,128]{1,0:T(8,128)(2,1)S(1)}, bf16[392,128]{1,0:T(8,128)(2,1)S(1)}, u32[]{:S(2)}, u32[]{:S(2)}) collective-permute-start(bf16[392,128]{1,0:T(8,128)(2,1)S(1)} %get-tuple-element.50), channel_id=1, source_target_pairs={{0,4},{2,6},{4,0},{6,2},{8,12},{10,14},{12,8},{14,10},{16,20},{18,... | collective-permute-start | bytes 301064 | tf_op jit(solution)/shard_map/ppermute | solution.py:499
  11.5 0.0 collective-permute-start.3
  11.6 1.2 %shard_map.139 = (bf16[1,1024,256]{2,1,0:T(8,128)(2,1)S(1)}, bf16[1,1024,256]{2,1,0:T(8,128)(2,1)S(1)}, f32[1,1024,384]{2,1,0:T(8,128)S(1)}, f32[1,3,8,128]{3,2,1,0:T(8,128)S(1)}, bf16[392,128]{1,0:T(8,128)(2,1)S(1)}) custom-call(bf16[128,256]{1,0:T(8,128)(2,1)S(1)} %get-tuple-element.44.in_ref, ...), custom_call_target="tpu_custom_call" | custom-call | flops 469762048 | bytes 2621440 | tf_op jit(solution)/shard_map/pallas_call | solution.py:37
  12.8 0.4 collective-permute-done.1.refs_1_
  13.2 2.6 %collective-permute-done.2.refs_2_ = bf16[392,128]{1,0:T(8,128)(2,1)S(1)} collective-permute-done((bf16[392,128]{1,0:T(8,128)(2,1)S(1)}, bf16[392,128]{1,0:T(8,128)(2,1)S(1)}, u32[]{:S(2)}, u32[]{:S(2)}) %collective-permute-start.2) | collective-permute-done | bytes 100384 | tf_op jit(solution)/shard_map/ppermute | solution.py:499
  15.8 1.2 %collective-permute-done.3.refs_3_ = bf16[392,128]{1,0:T(8,128)(2,1)S(1)} collective-permute-done((bf16[392,128]{1,0:T(8,128)(2,1)S(1)}, bf16[392,128]{1,0:T(8,128)(2,1)S(1)}, u32[]{:S(2)}, u32[]{:S(2)}) %collective-permute-start.3) | collective-permute-done | bytes 100384 | tf_op jit(solution)/shard_map/ppermute | solution.py:499
  17.1 0.4 shard_map.140.refs_4_
  17.5 3.7 %collective-permute-start.6 = (bf16[392,128]{1,0:T(8,128)(2,1)S(1)}, bf16[392,128]{1,0:T(8,128)(2,1)S(1)}, u32[]{:S(2)}, u32[]{:S(2)}) collective-permute-start(bf16[392,128]{1,0:T(8,128)(2,1)S(1)} %shard_map.140.refs_4_), channel_id=1, source_target_pairs={{0,24},{2,26},{4,28},{6,30},{8,16},{10,18},{12,20},{14,22},{16,8},... | collective-permute-start | bytes 301064 | tf_op jit(solution)/shard_map/ppermute | solution.py:499
  21.2 0.0 collective-permute-start.5
  21.2 0.8 %collective-permute-start.4 = (bf16[392,128]{1,0:T(8,128)(2,1)S(1)}, bf16[392,128]{1,0:T(8,128)(2,1)S(1)}, u32[]{:S(2)}, u32[]{:S(2)}) collective-permute-start(bf16[392,128]{1,0:T(8,128)(2,1)S(1)} %shard_map.140.refs_4_), channel_id=1, source_target_pairs={{0,8},{2,10},{4,12},{6,14},{8,0},{10,2},{12,4},{14,6},{16,24},{18,... | collective-permute-start | bytes 301064 | tf_op jit(solution)/shard_map/ppermute | solution.py:499
  22.0 2.2 %collective-permute-done.6.refs_7_ = bf16[392,128]{1,0:T(8,128)(2,1)S(1)} collective-permute-done((bf16[392,128]{1,0:T(8,128)(2,1)S(1)}, bf16[392,128]{1,0:T(8,128)(2,1)S(1)}, u32[]{:S(2)}, u32[]{:S(2)}) %collective-permute-start.6) | collective-permute-done | bytes 100384 | tf_op jit(solution)/shard_map/ppermute | solution.py:499
  24.1 4.2 %collective-permute-done.5.refs_6_ = bf16[392,128]{1,0:T(8,128)(2,1)S(1)} collective-permute-done((bf16[392,128]{1,0:T(8,128)(2,1)S(1)}, bf16[392,128]{1,0:T(8,128)(2,1)S(1)}, u32[]{:S(2)}, u32[]{:S(2)}) %collective-permute-start.5) | collective-permute-done | bytes 100384 | tf_op jit(solution)/shard_map/ppermute | solution.py:499
  28.3 0.0 collective-permute-done.4.refs_5_
  28.3 1.5 %shard_map.141 = (bf16[392,128]{1,0:T(8,128)(2,1)S(1)}, bf16[392,128]{1,0:T(8,128)(2,1)S(1)}, bf16[392,128]{1,0:T(8,128)(2,1)S(1)}, bf16[392,128]{1,0:T(8,128)(2,1)S(1)}) custom-call(bf16[392,128]{1,0:T(8,128)(2,1)S(1)} %get-tuple-element.48.refs_0_, bf16[392,128]{1,0:T(8,128)(2,1)S(1)} %collective-permute-done.1.refs_1_, ...), custom_call_target="tpu_custom_call" | custom-call | flops 1000000 | bytes 1000000 | tf_op jit(solution)/shard_map/pallas_call | solution.py:37
  29.8 1.8 %collective-permute-start.7 = (bf16[392,128]{1,0:T(8,128)(2,1)S(1)}, bf16[392,128]{1,0:T(8,128)(2,1)S(1)}, u32[]{:S(2)}, u32[]{:S(2)}) collective-permute-start(bf16[392,128]{1,0:T(8,128)(2,1)S(1)} %get-tuple-element.53), channel_id=1, source_target_pairs={{0,2},{2,0},{4,6},{6,4},{8,10},{10,8},{12,14},{14,12},{16,18},{18,... | collective-permute-start | bytes 301064 | tf_op jit(solution)/shard_map/ppermute | solution.py:499
  31.6 0.5 %collective-permute-start.8 = (bf16[392,128]{1,0:T(8,128)(2,1)S(1)}, bf16[392,128]{1,0:T(8,128)(2,1)S(1)}, u32[]{:S(2)}, u32[]{:S(2)}) collective-permute-start(bf16[392,128]{1,0:T(8,128)(2,1)S(1)} %get-tuple-element.54), channel_id=1, source_target_pairs={{0,4},{2,6},{4,0},{6,2},{8,12},{10,14},{12,8},{14,10},{16,20},{18,... | collective-permute-start | bytes 301064 | tf_op jit(solution)/shard_map/ppermute | solution.py:499
  32.1 1.2 %collective-permute-start.9 = (bf16[392,128]{1,0:T(8,128)(2,1)S(1)}, bf16[392,128]{1,0:T(8,128)(2,1)S(1)}, u32[]{:S(2)}, u32[]{:S(2)}) collective-permute-start(bf16[392,128]{1,0:T(8,128)(2,1)S(1)} %get-tuple-element.55), channel_id=1, source_target_pairs={{0,6},{2,4},{4,2},{6,0},{8,14},{10,12},{12,10},{14,8},{16,22},{18,... | collective-permute-start | bytes 301064 | tf_op jit(solution)/shard_map/ppermute | solution.py:499
  33.3 2.2 %shard_map.142 = (f32[128,256]{1,0:T(8,128)S(1)}, f32[256,256]{1,0:T(8,128)S(1)}, f32[256,384]{1,0:T(8,128)S(1)}, f32[1,1152]{1,0:T(1,128)S(1)}, f32[1,128]{1,0:T(1,128)S(1)}) custom-call(bf16[392,128]{1,0:T(8,128)(2,1)S(1)} %get-tuple-element.60.refs_0_, bf16[4,1024,128]{2,1,0:T(8,128)(2,1)S(1)} %get-tuple-element.42.refs_2_.enc_ref.refs_1_.refs_3_, ...), custom_call_target="tpu_custom_call" | custom-call | flops 939524096 | bytes 2621440 | tf_op jit(solution)/shard_map/pallas_call | solution.py:37
  35.6 0.0 collective-permute-done.7.refs_0_
  35.6 1.1 %collective-permute-done.8.refs_1_ = bf16[392,128]{1,0:T(8,128)(2,1)S(1)} collective-permute-done((bf16[392,128]{1,0:T(8,128)(2,1)S(1)}, bf16[392,128]{1,0:T(8,128)(2,1)S(1)}, u32[]{:S(2)}, u32[]{:S(2)}) %collective-permute-start.8) | collective-permute-done | bytes 100384 | tf_op jit(solution)/shard_map/ppermute | solution.py:499
  36.6 1.1 %collective-permute-done.9.refs_2_ = bf16[392,128]{1,0:T(8,128)(2,1)S(1)} collective-permute-done((bf16[392,128]{1,0:T(8,128)(2,1)S(1)}, bf16[392,128]{1,0:T(8,128)(2,1)S(1)}, u32[]{:S(2)}, u32[]{:S(2)}) %collective-permute-start.9) | collective-permute-done | bytes 100384 | tf_op jit(solution)/shard_map/ppermute | solution.py:499
  37.7 0.0 copy-start
  37.7 0.0 copy-start.1
  37.7 0.0 copy-start.2
  37.7 0.0 copy-start.3
  37.7 5.4 %shard_map.143 = (f32[1,512]{1,0:T(1,128)}, f32[784,128]{1,0:T(8,128)S(1)}, f32[784,128]{1,0:T(8,128)S(1)}) custom-call(bf16[392,128]{1,0:T(8,128)(2,1)S(1)} %collective-permute-done.7.refs_0_, bf16[392,128]{1,0:T(8,128)(2,1)S(1)} %collective-permute-done.8.refs_1_, bf16[392,128]{1,0:T(8,128)(2,1)S(1)} %collective-permute-done.9.refs_2_, ...), custom_call_target="tpu_custom_call" | custom-call | flops 2818572288 | bytes 7864320 | tf_op jit(solution)/shard_map/pallas_call | solution.py:37
  43.1 0.1 collective-permute-start.10
  43.2 1.7 %collective-permute-done.10.refs_1_ = f32[784,128]{1,0:T(8,128)S(1)} collective-permute-done((f32[784,128]{1,0:T(8,128)S(1)}, f32[784,128]{1,0:T(8,128)S(1)}, u32[]{:S(2)}, u32[]{:S(2)}) %collective-permute-start.10) | collective-permute-done | bytes 401440 | tf_op jit(solution)/shard_map/ppermute | solution.py:654
  44.9 0.0 copy-done
  44.9 0.0 copy-done.1
  44.9 0.0 copy-done.2
  44.9 0.0 copy-done.3
  44.9 1.1 %shard_map.144 = (f32[3,1,64,256]{3,2,1,0:T(8,128)}, f32[3,1,128,256]{3,2,1,0:T(8,128)}, f32[3,1,128,384]{3,2,1,0:T(8,128)}, f32[3,1,576]{2,1,0:T(1,128)}) custom-call(f32[784,128]{1,0:T(8,128)S(1)} %get-tuple-element.70.refs_0_, f32[784,128]{1,0:T(8,128)S(1)} %collective-permute-done.10.refs_1_, f32[3,1,64,256]{3,2,1,0:T(8,128)S(1)} %copy-done.2, ...), custom_call_target="tpu_custom_call" | custom-call | flops 1000000 | bytes 1000000 | tf_op jit(solution)/shard_map/pallas_call | solution.py:37
Async XLA Ops:
  2.8 1.6 %collective-permute-start = (bf16[784,128]{1,0:T(8,128)(2,1)S(1)}, bf16[784,128]{1,0:T(8,128)(2,1)S(1)}, u32[]{:S(2)}, u32[]{:S(2)}) collective-permute-start(bf16[784,128]{1,0:T(8,128)(2,1)S(1)} %get-tuple-element.41.refs_0_), channel_id=1, source_target_pairs={{0,1},{1,0},{2,3},{3,2},{4,5},{5,4},{6,7},{7,6},{8,9},{9,8},{10,11... | collective-permute-start | bytes 602120 | tf_op jit(solution)/shard_map/ppermute | solution.py:554
  7.1 6.1 %collective-permute-start.1 = (bf16[392,128]{1,0:T(8,128)(2,1)S(1)}, bf16[392,128]{1,0:T(8,128)(2,1)S(1)}, u32[]{:S(2)}, u32[]{:S(2)}) collective-permute-start(bf16[392,128]{1,0:T(8,128)(2,1)S(1)} %get-tuple-element.49), channel_id=1, source_target_pairs={{0,2},{2,0},{4,6},{6,4},{8,10},{10,8},{12,14},{14,12},{16,18},{18,... | collective-permute-start | bytes 301064 | tf_op jit(solution)/shard_map/ppermute | solution.py:499
  10.0 5.8 %collective-permute-start.2 = (bf16[392,128]{1,0:T(8,128)(2,1)S(1)}, bf16[392,128]{1,0:T(8,128)(2,1)S(1)}, u32[]{:S(2)}, u32[]{:S(2)}) collective-permute-start(bf16[392,128]{1,0:T(8,128)(2,1)S(1)} %get-tuple-element.50), channel_id=1, source_target_pairs={{0,4},{2,6},{4,0},{6,2},{8,12},{10,14},{12,8},{14,10},{16,20},{18,... | collective-permute-start | bytes 301064 | tf_op jit(solution)/shard_map/ppermute | solution.py:499
  11.5 5.5 %collective-permute-start.3 = (bf16[392,128]{1,0:T(8,128)(2,1)S(1)}, bf16[392,128]{1,0:T(8,128)(2,1)S(1)}, u32[]{:S(2)}, u32[]{:S(2)}) collective-permute-start(bf16[392,128]{1,0:T(8,128)(2,1)S(1)} %get-tuple-element.51), channel_id=1, source_target_pairs={{0,6},{2,4},{4,2},{6,0},{8,14},{10,12},{12,10},{14,8},{16,22},{18,... | collective-permute-start | bytes 301064 | tf_op jit(solution)/shard_map/ppermute | solution.py:499
  17.5 6.6 %collective-permute-start.6 = (bf16[392,128]{1,0:T(8,128)(2,1)S(1)}, bf16[392,128]{1,0:T(8,128)(2,1)S(1)}, u32[]{:S(2)}, u32[]{:S(2)}) collective-permute-start(bf16[392,128]{1,0:T(8,128)(2,1)S(1)} %shard_map.140.refs_4_), channel_id=1, source_target_pairs={{0,24},{2,26},{4,28},{6,30},{8,16},{10,18},{12,20},{14,22},{16,8},... | collective-permute-start | bytes 301064 | tf_op jit(solution)/shard_map/ppermute | solution.py:499
  21.2 7.1 %collective-permute-start.5 = (bf16[392,128]{1,0:T(8,128)(2,1)S(1)}, bf16[392,128]{1,0:T(8,128)(2,1)S(1)}, u32[]{:S(2)}, u32[]{:S(2)}) collective-permute-start(bf16[392,128]{1,0:T(8,128)(2,1)S(1)} %shard_map.140.refs_4_), channel_id=1, source_target_pairs={{0,16},{2,18},{4,20},{6,22},{8,24},{10,26},{12,28},{14,30},{16,0},... | collective-permute-start | bytes 301064 | tf_op jit(solution)/shard_map/ppermute | solution.py:499
  21.2 7.1 %collective-permute-start.4 = (bf16[392,128]{1,0:T(8,128)(2,1)S(1)}, bf16[392,128]{1,0:T(8,128)(2,1)S(1)}, u32[]{:S(2)}, u32[]{:S(2)}) collective-permute-start(bf16[392,128]{1,0:T(8,128)(2,1)S(1)} %shard_map.140.refs_4_), channel_id=1, source_target_pairs={{0,8},{2,10},{4,12},{6,14},{8,0},{10,2},{12,4},{14,6},{16,24},{18,... | collective-permute-start | bytes 301064 | tf_op jit(solution)/shard_map/ppermute | solution.py:499
  29.8 5.8 %collective-permute-start.7 = (bf16[392,128]{1,0:T(8,128)(2,1)S(1)}, bf16[392,128]{1,0:T(8,128)(2,1)S(1)}, u32[]{:S(2)}, u32[]{:S(2)}) collective-permute-start(bf16[392,128]{1,0:T(8,128)(2,1)S(1)} %get-tuple-element.53), channel_id=1, source_target_pairs={{0,2},{2,0},{4,6},{6,4},{8,10},{10,8},{12,14},{14,12},{16,18},{18,... | collective-permute-start | bytes 301064 | tf_op jit(solution)/shard_map/ppermute | solution.py:499
  31.6 5.1 %collective-permute-start.8 = (bf16[392,128]{1,0:T(8,128)(2,1)S(1)}, bf16[392,128]{1,0:T(8,128)(2,1)S(1)}, u32[]{:S(2)}, u32[]{:S(2)}) collective-permute-start(bf16[392,128]{1,0:T(8,128)(2,1)S(1)} %get-tuple-element.54), channel_id=1, source_target_pairs={{0,4},{2,6},{4,0},{6,2},{8,12},{10,14},{12,8},{14,10},{16,20},{18,... | collective-permute-start | bytes 301064 | tf_op jit(solution)/shard_map/ppermute | solution.py:499
  32.1 5.6 %collective-permute-start.9 = (bf16[392,128]{1,0:T(8,128)(2,1)S(1)}, bf16[392,128]{1,0:T(8,128)(2,1)S(1)}, u32[]{:S(2)}, u32[]{:S(2)}) collective-permute-start(bf16[392,128]{1,0:T(8,128)(2,1)S(1)} %get-tuple-element.55), channel_id=1, source_target_pairs={{0,6},{2,4},{4,2},{6,0},{8,14},{10,12},{12,10},{14,8},{16,22},{18,... | collective-permute-start | bytes 301064 | tf_op jit(solution)/shard_map/ppermute | solution.py:499
  37.7 7.2 %copy-start = (f32[3,1,128,384]{3,2,1,0:T(8,128)S(1)}, f32[3,1,128,384]{3,2,1,0:T(8,128)}, u32[]{:S(2)}) copy-start(f32[3,1,128,384]{3,2,1,0:T(8,128)} %refs_4_.3) | copy-start | bytes 1769476
  37.7 7.2 %copy-start.1 = (f32[3,1,128,256]{3,2,1,0:T(8,128)S(1)}, f32[3,1,128,256]{3,2,1,0:T(8,128)}, u32[]{:S(2)}) copy-start(f32[3,1,128,256]{3,2,1,0:T(8,128)} %refs_3_.3) | copy-start | bytes 1179652
  37.7 7.2 %copy-start.2 = (f32[3,1,64,256]{3,2,1,0:T(8,128)S(1)}, f32[3,1,64,256]{3,2,1,0:T(8,128)}, u32[]{:S(2)}) copy-start(f32[3,1,64,256]{3,2,1,0:T(8,128)} %refs_2_.3) | copy-start | bytes 589828
  37.7 7.2 %copy-start.3 = (f32[3,1,576]{2,1,0:T(1,128)S(1)}, f32[3,1,576]{2,1,0:T(1,128)}, u32[]{:S(2)}) copy-start(f32[3,1,576]{2,1,0:T(1,128)} %refs_5_.3) | copy-start | bytes 20740
  43.1 1.8 %collective-permute-start.10 = (f32[784,128]{1,0:T(8,128)S(1)}, f32[784,128]{1,0:T(8,128)S(1)}, u32[]{:S(2)}, u32[]{:S(2)}) collective-permute-start(f32[784,128]{1,0:T(8,128)S(1)} %get-tuple-element.71), channel_id=1, source_target_pairs={{0,1},{1,0},{2,3},{3,2},{4,5},{5,4},{6,7},{7,6},{8,9},{9,8},{10,11... | collective-permute-start | bytes 1204232 | tf_op jit(solution)/shard_map/ppermute | solution.py:654

commit v4 on v3

v4 whole, which is shorter than its diff:
```python
import functools

import jax
import jax.numpy as jnp
from jax import lax
from jax.experimental import pallas as pl
from jax.experimental.pallas import tpu as pltpu
from jax.sharding import PartitionSpec as P

BINS = 64
LANES = 128
QUAD = 4

depth_scale = 4.0
beta_one = 0.9
beta_two = 0.999
learn_rate = 0.001
epsilon = 1e-08
first_fix = 1.0 - 0.9**10
second_fix = 1.0 - 0.999**10

f32 = jnp.float32
bf16 = jnp.bfloat16


def in_vmem(value):
    return pltpu.with_memory_space_constraint(value, pltpu.VMEM)


def in_hbm(value):
    return pltpu.with_memory_space_constraint(value, pltpu.HBM)


def call(body, out_shape, inputs, limit, scratch=(), specs=None, flops=1000000, moved=1000000):
    many = isinstance(out_shape, (tuple, list))
    spec = pl.BlockSpec(memory_space=pltpu.VMEM)
    return pl.pallas_call(
        body,
        out_shape=out_shape,
        in_specs=specs or [spec] * len(inputs),
        out_specs=tuple(spec for _ in out_shape) if many else spec,
        scratch_shapes=list(scratch),
        compiler_params=pltpu.CompilerParams(vmem_limit_bytes=limit * 1024 * 1024),
        cost_estimate=pl.CostEstimate(flops=flops, bytes_accessed=moved, transcendentals=0),
    )(*inputs)


def blocks(width):
    return [slice(LANES * k, LANES * (k + 1)) for k in range(width // LANES)]


def wide_rows(count):
    return -(-count // LANES)


def row_block(row, rows):
    width = row.shape[1]
    padded = wide_rows(width) * LANES
    if padded != width:
        row = jnp.concatenate([row, jnp.zeros((1, padded - width), f32)], 1)
    place = lax.broadcasted_iota(jnp.int32, (rows, LANES), 0)
    out = jnp.zeros((rows, LANES), f32)
    for k, cut in enumerate(blocks(padded)):
        out = jnp.where(place == k, jnp.broadcast_to(row[:, cut], (rows, LANES)), out)
    return out


def block_row(block, count):
    return jnp.concatenate([block[k : k + 1] for k in range(count)], 1)


def split3(value):
    high = value.astype(bf16).astype(f32)
    rest = value - high
    mid = rest.astype(bf16).astype(f32)
    return (high, mid, rest - mid)


def lanes_of(shape):
    return lax.broadcasted_iota(jnp.int32, shape, 1)


def turned(rows, ray_count):
    fill = LANES - rows.shape[0]
    return jnp.concatenate([rows, jnp.zeros((fill, ray_count), f32)], 0).T


def own_group(k, slots, rows):
    place = lax.rem(lax.axis_index("region"), slots) ^ k
    return pl.ds(pl.multiple_of(place * rows, rows), rows)


def fetch_body(*refs, slots):
    ins, (pack_ref, *refs) = (refs[:10], refs[10:])
    outs, held, sems = (refs[:6], refs[6:10], refs[10])
    target_ref = outs[5]
    copies = []

    def fetch(source, place):
        copies.append(pltpu.make_async_copy(source, place, sems.at[len(copies)]))
        copies[-1].start()

    for ref, hold in zip(ins[:4], held):
        fetch(ref.at[0], hold)
    for ref, out in zip(ins[4:9], outs):
        fetch(ref, out)
    fetch(ins[9].at[own_group(0, slots, target_ref.shape[0])], target_ref)
    spot = 0
    for copy, hold in zip(copies[:3], held[:3]):
        copy.wait()
        rows, width = hold.shape[1:]
        for cut in blocks(width):
            pack_ref[spot : spot + rows, :] = hold[0, :, cut].astype(bf16)
            spot += rows
    copies[3].wait()
    pack_ref[spot : spot + 16, :] = row_block(held[3][...], 16).astype(bf16)
    for copy in copies[4:]:
        copy.wait()


def encode_body(*refs, unit_length, slots):
    codes, bins, entry, exit_, direction, enc_ref, geometry_ref, *refs = refs
    flat_geometry, flat_position = refs
    bins = bins[0].astype(f32)
    samples, ray_count = bins.shape
    group_rows = ray_count // slots
    slot = lax.broadcasted_iota(jnp.int32, bins.shape, 0)
    following = jnp.where(slot == samples - 1, float(BINS), pltpu.roll(bins, samples - 1, 0))
    inside = ((slot >= entry[...]) & (slot < exit_[...])).astype(f32)
    flat_geometry[:samples] = (following - bins) * unit_length * inside
    flat_geometry[samples : samples + 1] = direction[...].astype(f32)
    flat_position[...] = turned((bins + 0.5) / BINS, ray_count)
    for k in range(slots):
        group = own_group(k, slots, group_rows)
        geometry_ref[k] = flat_geometry[:, group]
        code_zero = codes[0, group].astype(f32)
        code_one = codes[1, group].astype(f32)
        position = flat_position[group, :]
        for j in range(samples):
            encoded = code_zero + position[:, j : j + 1] * code_one
            enc_ref[k, group_rows * j : group_rows * (j + 1), :] = encoded.astype(bf16)


def assemble(packs, shapes, vec_share):
    shards = len(packs)
    spot = 0
    mats = []
    for rows, width in shapes:
        pieces = []
        for cut in blocks(width):
            pieces.append(jnp.concatenate([p[spot : spot + rows, :] for p in packs], 0))
            spot += rows
        mats.append(jnp.concatenate(pieces, 1))
    vec_total = vec_share * shards
    vec = jnp.zeros((1, vec_total), f32)
    for s, p in enumerate(packs):
        block = p[spot : spot + 16, :].astype(f32)
        count = wide_rows(vec_share)
        row = block_row(block, count)
        fill = vec_total - count * LANES
        if fill:
            row = jnp.concatenate([row, jnp.zeros((1, fill), f32)], 1)
        if s:
            row = pltpu.roll(row, vec_share * s, 1)
        vec = vec + row
    return (*mats, vec)


def forward_slots(slots, weights, enc_ref, geometry_ref, message_refs, kept):
    in_weight, mid_ref, head_ref, vec = weights
    one_ref, two_ref, turn_ref, scalar_ref = kept
    samples, ray_count = scalar_ref.shape[2:]
    hidden = mid_ref.shape[0]
    feat = turn_ref.shape[2]
    bias_one = vec[:, :hidden]
    bias_two = vec[:, hidden : 2 * hidden]
    half_bias = 0.5 * vec[:, 3 * hidden :]
    lane = lanes_of((ray_count, LANES))
    densities = []
    for i, k in enumerate(slots):
        one = jnp.dot(enc_ref[k], in_weight, preferred_element_type=f32) + bias_one
        one = jnp.maximum(one, 0.0).astype(bf16)
        one_ref[i] = one
        two = jnp.dot(one, mid_ref[...], preferred_element_type=f32) + bias_two
        two = jnp.maximum(two, 0.0).astype(bf16)
        two_ref[i] = two
        raw = jnp.dot(two, head_ref[...], preferred_element_type=f32)
        turn_ref[i] = jnp.tanh(raw[:, :feat] + half_bias)
        density = jnp.zeros((ray_count, LANES), f32)
        for j in range(samples):
            rows = slice(ray_count * j, ray_count * (j + 1))
            density = jnp.where(lane == j, raw[rows, feat:], density)
        densities.append(density)
    density = side_by_side([value.T[:samples] for value in densities])
    geometry = side_by_side([geometry_ref[k, :samples] for k in slots])
    direction = side_by_side([geometry_ref[k, samples : samples + 1] for k in slots])
    soft = jnp.maximum(density, 0.0) + jnp.log1p(jnp.exp(-jnp.abs(density)))
    optical = soft * geometry
    before = [jnp.zeros_like(direction)]
    for j in range(samples):
        before.append(before[-1] + optical[j : j + 1])
    depth = before.pop()
    optical_before = jnp.concatenate(before, 0)
    opacity = jnp.tanh(0.5 * optical) * (1.0 + jnp.exp(-optical))
    local_weight = jnp.exp(-optical_before) * opacity
    half_weight = 0.5 * local_weight
    half_sum = jnp.sum(half_weight, 0, keepdims=True)
    columns = turned(jnp.concatenate([half_weight, half_sum], 0), depth.shape[1])
    shared = jnp.concatenate([*split3(depth), direction], 0)
    sig = 0.5 * jnp.tanh(0.5 * density) + 0.5
    scalars = (local_weight, jnp.exp(-(optical_before + optical)), geometry * sig)
    for i, k in enumerate(slots):
        cut = slice(ray_count * i, ray_count * (i + 1))
        for q, value in enumerate(scalars):
            scalar_ref[i, q] = value[:, cut]
        own = columns[cut]
        total = jnp.zeros((ray_count, feat), f32) + own[:, samples : samples + 1]
        for j in range(samples):
            rows = slice(ray_count * j, ray_count * (j + 1))
            total = total + own[:, j : j + 1] * turn_ref[i, rows, :]
        message_refs[i][...] = as_message([total[:, k] for k in blocks(feat)], shared[:, cut])


def side_by_side(values):
    return jnp.concatenate(values, 1) if len(values) > 1 else values[0]


def as_message(parts, rows):
    count, rays = rows.shape
    if count < 8:
        rows = jnp.concatenate([rows, jnp.zeros((8 - count, rays), f32)], 0)
    if rays < LANES:
        rows = jnp.concatenate([rows, jnp.zeros((8, LANES - rays), f32)], 1)
    return jnp.concatenate([*parts, rows], 0).astype(bf16)


def from_message(value, rays):
    value = value.astype(f32)
    count = value.shape[0] // rays
    parts = [value[rays * k : rays * (k + 1)] for k in range(count)]
    return (parts, value[rays * count :, :rays])


def forward_first_body(*refs, shapes, vec_share, pair, slots):
    both = None
    if pair:
        own_ref, other_ref, *refs, both = refs
        mine = lax.axis_index("rays")
        both[mine] = own_ref[...]
        both[1 - mine] = other_ref[...]
        packs = [both.at[0], both.at[1]]
    else:
        packs_ref, *refs = refs
        packs = [packs_ref.at[s] for s in range(packs_ref.shape[0])]
    enc_ref, geometry_ref, in_ref, mid_ref, head_ref, vec_ref, *refs = refs
    hidden = mid_ref.shape[0]
    in_weight, mid_weight, feat_weight, vec = assemble(packs, shapes, vec_share)
    density_row = vec[:, 2 * hidden : 3 * hidden]
    density_cols = jnp.broadcast_to(density_row, (LANES, hidden)).T
    in_ref[...] = in_weight
    mid_ref[...] = mid_weight
    half_weight = (0.5 * feat_weight.astype(f32)).astype(bf16)
    head_ref[...] = jnp.concatenate([half_weight, density_cols.astype(bf16)], 1)
    vec_ref[...] = vec
    weights = (in_weight, mid_ref, head_ref, vec)
    forward_slots(slots, weights, enc_ref, geometry_ref, refs[4:], refs[:4])


def forward_rest_body(in_ref, mid_ref, head_ref, vec_ref, enc_ref, geometry_ref, *refs, slots):
    weights = (in_ref[...], mid_ref, head_ref, vec_ref[...])
    forward_slots(slots, weights, enc_ref, geometry_ref, refs[4:], refs[:4])


def sides(values):
    below, above = ([jnp.zeros_like(values[0])], [jnp.zeros_like(values[0])])
    for q in range(len(values) - 1):
        below.append(below[-1] + values[q])
        above.append(above[-1] + values[len(values) - 1 - q])
    return (below, above[::-1])


def gather_messages(refs, store, own, rays):
    for k, ref in enumerate(refs):
        store[own ^ k] = ref[...]
    members = [from_message(store[p], rays) for p in range(len(refs))]
    parts = [m[0] for m in members]
    depth = [m[1][0:1] + m[1][1:2] + m[1][2:3] for m in members]
    direction = members[0][1][3:4]
    below, above = sides(depth)
    trans = [jnp.exp(-jnp.where(direction < 0.5, b, a)) for b, a in zip(below, above)]
    return (parts, depth, direction, trans)


def as_columns(rows):
    columns = turned(jnp.concatenate(rows, 0), rows[0].shape[1])
    return [columns[:, i : i + 1] for i in range(len(rows))]


def weighted_sum(factors, parts):
    out = []
    for k in range(len(parts[0])):
        total = factors[0] * parts[0][k]
        for factor, part in zip(factors[1:], parts[1:]):
            total = total + factor * part[k]
        out.append(total)
    return out


def inner(left, right):
    total = left[0] * right[0]
    for a, b in zip(left[1:], right[1:]):
        total = total + a * b
    return jnp.sum(total, 1, keepdims=True)


def plane_body(*refs, rays):
    *messages, out_ref, store = refs
    own = lax.rem(lax.axis_index("region"), len(messages))
    parts, depth, direction, trans = gather_messages(messages, store, own, rays)
    total = depth[0]
    for value in depth[1:]:
        total = total + value
    rows = jnp.concatenate([*split3(total), direction], 0)
    out_ref[...] = as_message(weighted_sum(as_columns(trans), parts), rows)


def owner_body(*refs, slots, planes):
    quad_refs, plane_refs = (refs[:slots], refs[slots : slots + planes])
    target_ref, _, *out_refs, quad_store, plane_store, reply = refs[slots + planes :]
    rays, feat = target_ref.shape
    region = lax.axis_index("region")
    own, own_plane = (lax.rem(region, slots), lax.div(region, slots))
    parts, _, direction, trans = gather_messages(quad_refs, quad_store, own, rays)
    plane_parts, _, _, plane_trans = gather_messages(plane_refs, plane_store, own_plane, rays)
    rendered = weighted_sum(as_columns(plane_trans), plane_parts)
    grads = [
        (value - target_ref[:, cut].astype(f32)).astype(bf16).astype(f32)
        for value, cut in zip(rendered, blocks(feat))
    ]
    lane = lanes_of((rays, LANES))
    inners = jnp.zeros((rays, LANES), f32)
    for i, value in enumerate((*plane_parts, *parts)):
        inners = jnp.where(lane == i, inner(grads, value), inners)
    inners = inners.T

    def later(values):
        below, above = sides(values)
        return [jnp.where(direction < 0.5, a, b) for b, a in zip(below, above)]

    plane_after = later([t * inners[z : z + 1] for z, t in enumerate(plane_trans)])
    ahead = jnp.zeros((1, rays), f32)
    reach = jnp.zeros((1, rays), f32)
    for z in range(planes):
        ahead = jnp.where(own_plane == z, plane_trans[z], ahead)
        reach = jnp.where(own_plane == z, plane_after[z], reach)
    trans = [ahead * t for t in trans]
    after = later([t * inners[planes + p : planes + p + 1] for p, t in enumerate(trans)])
    for p in range(slots):
        reply[p, :6, :rays] = jnp.concatenate([*split3(trans[p]), *split3(after[p] + reach)], 0)
    for k, out_ref in enumerate(out_refs):
        out_ref[...] = as_message(grads, reply[own ^ k, :6, :rays])


def with_ones(value):
    return jnp.concatenate([value.T, jnp.ones((16, value.shape[0]), bf16)], 0)


def ready_body(*refs):
    enc_ref, mid_ref, head_ref, *refs = refs
    count = (len(refs) - 3) // 7
    sources = [refs[4 * n : 4 * n + 4] for n in range(count)]
    enc_turned, mid_turned, head_turned, *refs = refs[4 * count :]
    results = [refs[3 * n : 3 * n + 3] for n in range(count)]
    mid_turned[...] = mid_ref[...].T
    feat = sources[0][2].shape[2]
    head = head_ref[...].astype(f32)
    lane = lanes_of(head.shape)
    head_turned[...] = jnp.where(lane < feat, 2.0 * head, head).astype(bf16).T
    for k in range(enc_ref.shape[0]):
        enc_turned[k] = with_ones(enc_ref[k])
    for source, outs in zip(sources, results):
        one_ref, two_ref, turn_ref, scalar_ref = source
        one_turned, two_turned, slope_ref = outs
        samples, ray_count = scalar_ref.shape[2:]
        for i in range(one_ref.shape[0]):
            one_turned[i] = with_ones(one_ref[i])
            two_turned[i] = with_ones(two_ref[i])
            columns = turned(0.25 * scalar_ref[i, 0], ray_count)
            for j in range(samples):
                rows = slice(ray_count * j, ray_count * (j + 1))
                turn = turn_ref[i, rows, :]
                slope_ref[i, rows, :] = columns[:, j : j + 1] * (1.0 - turn * turn)


def product(left, right):
    return jnp.dot(left, right, preferred_element_type=f32)


def backward_body(*refs, slots, offset, before, last, group_count, shapes, vec_share, shards):
    begun = not before
    messages, refs = (refs[: len(slots)], refs[len(slots) :])
    one_ref, two_ref, turn_ref, scalar_ref, *refs = refs
    one_turned, two_turned, slope_ref, enc_turned, mid_turned, head_turned, *refs = refs
    if not begun:
        earlier, refs = (refs[:3], refs[3:])
    if last:
        depths, (depth_ref, *outs, shares) = (refs[: len(before)], refs[len(before) :])
    else:
        *outs, depth_ref = refs
    samples, ray_count = scalar_ref.shape[2:]
    hidden = one_ref.shape[2]
    feat = turn_ref.shape[2]
    lane = lanes_of((ray_count, LANES))
    if last:
        for ref, group in zip(depths, before):
            for i, k in enumerate(group):
                depth_ref[:, own_group(k, group_count, ray_count)] = ref[i : i + 1]
    sums = [0.0, 0.0, 0.0] if begun else [ref[...] for ref in earlier]
    grads, extras, spreads = ([], [], [])
    for i, k in enumerate(slots):
        parts, extra = from_message(messages[i][...], ray_count)
        grad = jnp.concatenate(parts, 1)
        grads.append(grad)
        extras.append(extra)
        grad_sum = jnp.sum(grad, 1, keepdims=True)
        spread = jnp.where(lane == samples, grad_sum, 0.0)
        for j in range(samples):
            rows = slice(ray_count * j, ray_count * (j + 1))
            value = jnp.sum(turn_ref[offset + i, rows, :] * grad, 1, keepdims=True)
            spread = jnp.where(lane == j, value, spread)
        spreads.append(spread.T)
    extra = side_by_side(extras)
    trans = extra[0:1] + extra[1:2] + extra[2:3]
    after = extra[3:4] + extra[4:5] + extra[5:6]
    for i, k in enumerate(slots):
        cut = slice(ray_count * i, ray_count * (i + 1))
        if last:
            depth_ref[:, own_group(k, group_count, ray_count)] = -after[:, cut]
        else:
            depth_ref[i : i + 1] = -after[:, cut]
    spread = side_by_side(spreads)
    sample_grad = 0.5 * (spread[:samples] + spread[samples : samples + 1])
    local_weight, trans_after, slope = [
        side_by_side([scalar_ref[offset + i, q] for i in range(len(slots))]) for q in range(3)
    ]
    weighted = local_weight * sample_grad
    later = [jnp.zeros_like(after)]
    for j in range(samples - 1, 0, -1):
        later.append(later[-1] + weighted[j : j + 1])
    later = jnp.concatenate(later[::-1], 0)
    optical_grad = trans * (trans_after * sample_grad - later) - after
    columns = turned(jnp.concatenate([optical_grad * slope, trans], 0), after.shape[1])
    zero = jnp.zeros((), bf16)
    for i, k in enumerate(slots):
        own = columns[ray_count * i : ray_count * (i + 1)]
        grad_ahead = grads[i] * own[:, samples : samples + 1]
        pieces = []
        for j in range(samples):
            rows = slice(ray_count * j, ray_count * (j + 1))
            colour_grad = (grad_ahead * slope_ref[offset + i, rows, :]).astype(bf16)
            density_part = jnp.where(lane == j, own, 0.0).astype(bf16)
            pieces.append(jnp.concatenate([colour_grad, density_part], 1))
        head_grad = jnp.concatenate(pieces, 0)
        second = product(head_grad, head_turned[...]).astype(bf16)
        second = jnp.where(two_ref[offset + i] > 0, second, zero)
        first = product(second, mid_turned[...]).astype(bf16)
        first = jnp.where(one_ref[offset + i] > 0, first, zero)
        sums[0] = sums[0] + product(enc_turned[k], first)
        sums[1] = sums[1] + product(one_turned[offset + i], second)
        sums[2] = sums[2] + product(two_turned[offset + i], head_grad)
    if not last:
        for value, ref in zip(sums, outs):
            ref[...] = value
        return
    values = [value[:-16] for value in sums]
    first_sum, second_sum, head_sum = [value[-16:-15] for value in sums]
    density_sum = jnp.sum(values[2][:, feat:].T, 0, keepdims=True)
    vec = jnp.concatenate([first_sum, second_sum, density_sum, head_sum[:, :feat]], 1)
    mine = lax.axis_index("rays")
    total = vec.shape[1]
    for s in range(shards):
        place = lax.rem(s + shards - mine, shards) if shards == 2 else s
        spot = 0
        for (rows, width), value in zip(shapes, values):
            for cut in blocks(width):
                shares[place, spot : spot + rows, :] = value[rows * s : rows * (s + 1), cut]
                spot += rows
        row = pltpu.roll(vec, total - vec_share * s, 1) if s else vec
        shares[place, spot : spot + 16, :] = row_block(row[:, : wide_rows(vec_share) * LANES], 16)
    if shards == 2:
        outs[0][...] = shares[0]
        outs[1][...] = shares[1]
    else:
        outs[0][...] = shares[...]


def adam_body(*refs, shards):
    grad_refs = refs[:shards]
    state_refs, out_refs = (refs[shards : shards + 4], refs[shards + 4 :])

    def update(stacked, gradient):
        first_moment = beta_one * stacked[1] + (1.0 - beta_one) * gradient
        second = beta_two * stacked[2] + (1.0 - beta_two) * gradient * gradient
        step = first_moment / first_fix / (jnp.sqrt(second / second_fix) + epsilon)
        return (stacked[0] - learn_rate * step, first_moment, second)

    def gathered(spot, rows):
        total = grad_refs[0][spot : spot + rows, :]
        for ref in grad_refs[1:]:
            total = total + ref[spot : spot + rows, :]
        return total

    spot = 0
    for ref, out in zip(state_refs[:3], out_refs[:3]):
        rows, width = ref.shape[2:]
        for cut in blocks(width):
            new = update([ref[i, 0, :, cut] for i in range(3)], gathered(spot, rows))
            spot += rows
            for i in range(3):
                out[i, 0, :, cut] = new[i]
    ref, out = (state_refs[3], out_refs[3])
    share = ref.shape[2]
    gradient = block_row(gathered(spot, 16), wide_rows(share))[:, :share]
    new = update([ref[i] for i in range(3)], gradient)
    for i in range(3):
        out[i] = new[i]


def shaped(shape, dtype):
    return jax.ShapeDtypeStruct(shape, dtype)


def swap(value, distance, size):
    return lax.ppermute(value, "region", [(i, i ^ distance) for i in range(size)])


def per_device(
    ray_codes,
    target,
    direction,
    entries,
    exits,
    depth_bins,
    in_layer,
    mid_layer,
    feat_layer,
    vectors,
):
    regions = lax.axis_size("region")
    shards = lax.axis_size("rays")
    samples, ray_count = depth_bins.shape[1:]
    quad = min(QUAD, regions)
    planes = regions // quad
    rays = ray_count // quad
    layers = (in_layer, mid_layer, feat_layer)
    states = (*layers, vectors)
    shapes = tuple(layer.shape[2:] for layer in layers)
    vec_share = vectors.shape[2]
    hidden = shapes[0][1]
    feat = shapes[2][1]
    code_width = ray_codes.shape[2]
    pack_rows = sum(rows * (width // LANES) for rows, width in shapes) + 16
    rows = samples * rays
    sizes = dict(shapes=shapes, vec_share=vec_share)
    pair = shards == 2
    flops = 2 * rows * (code_width * hidden + hidden * hidden + hidden * (feat + LANES))

    arguments = (*states, ray_codes, depth_bins, entries, exits, direction[None], target)
    pack, *geometric, own_target = call(
        functools.partial(fetch_body, slots=quad),
        (pltpu.VMEM((pack_rows, LANES), bf16),)
        + tuple(pltpu.VMEM(a.shape, a.dtype) for a in arguments[4:9])
        + (pltpu.VMEM((rays, feat), bf16),),
        [in_hbm(a) for a in arguments],
        16,
        scratch=[pltpu.VMEM(a.shape[1:], f32) for a in states]
        + [pltpu.SemaphoreType.DMA((10,))],
        specs=[pl.BlockSpec(memory_space=pltpu.HBM)] * 10,
    )
    if pair:
        packs = (pack, lax.ppermute(pack, "rays", [(0, 1), (1, 0)]))
    else:
        packs = (lax.all_gather(pack, "rays", axis=0),)
    encoded, geometry = call(
        functools.partial(encode_body, unit_length=depth_scale / (regions * BINS), slots=quad),
        (
            pltpu.VMEM((quad, rows, code_width), bf16),
            pltpu.VMEM((quad, samples + 8, rays), f32),
        ),
        [in_vmem(v) for v in geometric],
        16,
        scratch=[
            pltpu.VMEM((samples + 8, ray_count), f32),
            pltpu.VMEM((ray_count, LANES), f32),
        ],
        flops=10 * quad * rows * code_width,
        moved=quad * rows * code_width * 4,
    )

    message = pltpu.VMEM((rays * (feat // LANES) + 8, LANES), bf16)

    def kept_shapes(count):
        return (
            pltpu.VMEM((count, rows, hidden), bf16),
            pltpu.VMEM((count, rows, hidden), bf16),
            pltpu.VMEM((count, rows, feat), f32),
            pltpu.VMEM((count, 3, samples, rays), f32),
        )

    def moved(count):
        return count * rows * (feat + hidden) * 4

    weight_shapes = (
        pltpu.VMEM((shapes[0][0] * shards, hidden), bf16),
        pltpu.VMEM((hidden, hidden), bf16),
        pltpu.VMEM((hidden, feat + LANES), bf16),
        pltpu.VMEM((1, vec_share * shards), f32),
    )

    def forward(slots, inputs, first):
        if first:
            body = functools.partial(forward_first_body, pair=pair, slots=slots, **sizes)
        else:
            body = functools.partial(forward_rest_body, slots=slots)
        out = call(
            body,
            (weight_shapes if first else ())
            + kept_shapes(len(slots))
            + (message,) * len(slots),
            [in_vmem(v) for v in (*inputs, encoded, geometry)],
            16,
            scratch=[pltpu.VMEM((2, pack_rows, LANES), bf16)] if first and pair else (),
            flops=len(slots) * flops,
            moved=moved(len(slots)),
        )
        found, out = (out[:4], out[4:]) if first else (None, out)
        return (out[:4], list(out[4:]), found)

    groups = [tuple(range(1, quad)), (0,)]
    kept, sent, weights = ([], {}, None)
    for slots in groups:
        arrays, messages, found = forward(slots, packs if not kept else weights, not kept)
        weights = weights or found
        kept.append(arrays)
        for k, value in zip(slots, messages):
            sent[k] = swap(value, k, regions) if k else value
    quad_messages = [in_vmem(sent[k]) for k in range(quad)]
    store = pltpu.VMEM((quad, *message.shape), bf16)
    plane_store = pltpu.VMEM((planes, *message.shape), bf16)
    plane_message = call(
        functools.partial(plane_body, rays=rays), message, quad_messages, 16, scratch=[store]
    )
    plane_messages = [plane_message] + [
        swap(plane_message, quad * k, regions) for k in range(1, planes)
    ]
    def ready_shapes(count):
        return (
            pltpu.VMEM((count, hidden + 16, rows), bf16),
            pltpu.VMEM((count, hidden + 16, rows), bf16),
            pltpu.VMEM((count, rows, feat), f32),
        )

    enc_turned, *results = call(
        ready_body,
        (
            pltpu.VMEM((quad, code_width + 16, rows), bf16),
            pltpu.VMEM((hidden, hidden), bf16),
            pltpu.VMEM((feat + LANES, hidden), bf16),
        )
        + sum((ready_shapes(len(slots)) for slots in groups), ()),
        [in_vmem(v) for v in (encoded, weights[1], weights[2], *sum(map(list, kept), []))],
        16,
        flops=quad * flops,
        moved=2 * moved(quad),
    )
    turned_weights, results = (results[:2], results[2:])
    ready = [results[3 * n : 3 * n + 3] for n in range(len(groups))]
    replies = call(
        functools.partial(owner_body, slots=quad, planes=planes),
        (message,) * quad,
        quad_messages + [in_vmem(v) for v in (*plane_messages, own_target, turned_weights[0])],
        16,
        scratch=[store, plane_store, pltpu.VMEM((quad, 8, LANES), f32)],
    )
    answers = [replies[0]] + [swap(replies[k], k, regions) for k in range(1, quad)]
    gradient_shapes = (
        pltpu.VMEM((code_width + 16, hidden), f32),
        pltpu.VMEM((hidden + 16, hidden), f32),
        pltpu.VMEM((hidden + 16, feat + LANES), f32),
    )
    earlier, depths, before = ((), [], ())
    steps = [(1, (0,), 0), (0, (1,), 0), (0, tuple(range(2, quad)), 1)]
    for n, slots, offset in steps:
        last = slots == steps[-1][1]
        if last:
            share = pltpu.VMEM((pack_rows, LANES), f32)
            out_shape = (shaped((1, ray_count), f32), share, share)
            if not pair:
                out_shape = (out_shape[0], shaped((shards, pack_rows, LANES), f32))
        else:
            out_shape = gradient_shapes + (pltpu.VMEM((len(slots), rays), f32),)
        inputs = [answers[k] for k in slots] + [*kept[n], *ready[n], enc_turned, *turned_weights]
        inputs += [*earlier] + (depths if last else [])
        out = call(
            functools.partial(
                backward_body,
                slots=slots,
                offset=offset,
                before=before,
                last=last,
                group_count=quad,
                shards=shards,
                **sizes,
            ),
            out_shape,
            [in_vmem(v) for v in inputs],
            24,
            scratch=[pltpu.VMEM((shards, pack_rows, LANES), f32)] if last else (),
            flops=2 * len(slots) * flops,
            moved=moved(len(slots)),
        )
        earlier, before = (out[:3], before + (slots,))
        if not last:
            depths.append(out[3])
    depth_grad, *grads = out
    if pair:
        parts = (grads[0], lax.ppermute(grads[1], "rays", [(0, 1), (1, 0)]))
    else:
        exchanged = lax.all_to_all(grads[0], "rays", 0, 0)
        parts = tuple(exchanged[s] for s in range(shards))
    new = call(
        functools.partial(adam_body, shards=shards),
        tuple(shaped(s.shape, f32) for s in states),
        (*parts, *states),
        16,
    )
    return (*new, depth_grad)


def solution(mesh):
    placed = (
        P(None, "rays", None),
        P("rays", None),
        P("rays"),
        P("region", "rays"),
        P("region", "rays"),
        P("region", None, "rays"),
        P(None, "region", "rays", None),
        P(None, "region", "rays", None),
        P(None, "region", "rays", None),
        P(None, "region", "rays"),
    )
    return jax.shard_map(
        per_device,
        mesh=mesh,
        in_specs=placed,
        out_specs=(
            P(None, "region", "rays", None),
            P(None, "region", "rays", None),
            P(None, "region", "rays", None),
            P(None, "region", "rays"),
            P("region", "rays"),
        ),
        check_vma=False,
    )
```

time: 46.2 us -> 42.8 us (0.926)
  waiting for transfers between devices: 15.6 us -> 10.4 us
  Pallas kernels: 16.7 us -> 18.5 us
    ppermute x9, waiting for transfers between devices: 12.8 us -> 8.39 us  [swap(): lax.ppermute(value, 'region', [(i, i ^ distance) for i in range(size)])]
    pallas_call x8 -> x11, Pallas kernels: 16.7 us -> 18.5 us  [call(): pl.pallas_call(body, out_shape=out_shape, in_specs=specs or [spec] * len(...]
    ppermute x1, waiting for transfers between devices: 1.08 us -> 0.24 us  [per_device(): packs = (pack, lax.ppermute(pack, 'rays', [(0, 1), (1, 0)]))]
  transfers between devices with their start and end apart: 11 -> 11, of which waited for: 9 -> 7; matrix products, arithmetic and copies ran while one was open for 0% -> 0% of each run, Pallas kernels for 8% -> 20%
where the time goes in v4:
time: 42.8 us; the launch traced here: 42.6 us
  Pallas kernels  18.5 us (43%)
  starting transfers between devices  13 us (30%)
  waiting for transfers between devices  10.4 us (24%)
  between operations  0.73 us (2%)
    pallas_call x11, Pallas kernels, call(): pl.pallas_call(body, out_shape=out_shape, in_specs=specs or [spec] * len(...  18.5 us
    ppermute x9, starting transfers between devices, swap(): lax.ppermute(value, 'region', [(i, i ^ distance) for i in range(size)])  12.5 us
    ppermute x9, waiting for transfers between devices, swap(): lax.ppermute(value, 'region', [(i, i ^ distance) for i in range(size)])  8.39 us
    ppermute x1, waiting for transfers between devices, per_device(): parts = (grads[0], lax.ppermute(grads[1], 'rays', [(0, 1), (1, 0)]))  1.73 us
  transfers between devices with their start and end apart: 11, of which 7 were waited for; matrix products, arithmetic and copies ran while one was open for 0% of the time, Pallas kernels for 20%

profile of v4, /device:TPU:0, one launch (start us, length us, event | category | flops | bytes accessed | tf_op | source)
XLA Modules:
  0.0 42.6 jit_solution(15415136795733531078)
XLA Ops:
  0.6 1.3 %shard_map.137 = (bf16[784,128]{1,0:T(8,128)(2,1)S(1)}, bf16[2,512,128]{2,1,0:T(8,128)(2,1)S(1)}, s32[1,8,512]{2,1,0:T(8,128)S(1)}, s32[1,512]{1,0:T(1,128)S(1)}...) custom-call(f32[3,1,64,256]{3,2,1,0:T(8,128)} %refs_2_.3, f32[3,1,128,256]{3,2,1,0:T(8,128)} %refs_3_.3, ...), custom_call_target="tpu_custom_call" | custom-call | flops 1000000 | bytes 1000000 | tf_op jit(solution)/shard_map/pallas_call | solution.py:37
  2.0 0.5 %collective-permute-start = (bf16[784,128]{1,0:T(8,128)(2,1)S(1)}, bf16[784,128]{1,0:T(8,128)(2,1)S(1)}, u32[]{:S(2)}, u32[]{:S(2)}) collective-permute-start(bf16[784,128]{1,0:T(8,128)(2,1)S(1)} %get-tuple-element.58.refs_0_), channel_id=1, source_target_pairs={{0,1},{1,0},{2,3},{3,2},{4,5},{5,4},{6,7},{7,6},{8,9},{9,8},{10,11... | collective-permute-start | bytes 602120 | tf_op jit(solution)/shard_map/ppermute | solution.py:581
  2.5 0.8 %shard_map.138 = (bf16[4,1024,128]{2,1,0:T(8,128)(2,1)S(1)}, f32[4,16,128]{2,1,0:T(8,128)S(1)}) custom-call(bf16[2,512,128]{2,1,0:T(8,128)(2,1)S(1)} %get-tuple-element.59.refs_0_, s32[1,8,512]{2,1,0:T(8,128)S(1)} %get-tuple-element.60.refs_1_, s32[1,512]{1,0:T(1,128)S(1)} %get-tuple-element.61.refs_2_, s32[1,512]{1,0:T(1,128)S(1)} %get-tuple-element.62.refs_3_, ...), custom_call_target="tpu_custom_call" | custom-call | flops 5242880 | bytes 2097152 | tf_op jit(solution)/shard_map/pallas_call | solution.py:37
  3.3 0.2 collective-permute-done.refs_1_
  3.6 2.5 %shard_map.139 = (bf16[128,256]{1,0:T(8,128)(2,1)S(1)}, bf16[256,256]{1,0:T(8,128)(2,1)S(1)}, bf16[256,512]{1,0:T(8,128)(2,1)S(1)}, f32[1,1152]{1,0:T(1,128)S(1)...) custom-call(bf16[784,128]{1,0:T(8,128)(2,1)S(1)} %get-tuple-element., ...), custom_call_target="tpu_custom_call" | custom-call | flops 1409286144 | bytes 7864320 | tf_op jit(solution)/shard_map/pallas_call | solution.py:37
  6.1 2.9 %collective-permute-start.1 = (bf16[392,128]{1,0:T(8,128)(2,1)S(1)}, bf16[392,128]{1,0:T(8,128)(2,1)S(1)}, u32[]{:S(2)}, u32[]{:S(2)}) collective-permute-start(bf16[392,128]{1,0:T(8,128)(2,1)S(1)} %get-tuple-element.71), channel_id=1, source_target_pairs={{0,2},{2,0},{4,6},{6,4},{8,10},{10,8},{12,14},{14,12},{16,18},{18,... | collective-permute-start | bytes 301064 | tf_op jit(solution)/shard_map/ppermute | solution.py:534
  9.0 1.5 %collective-permute-start.2 = (bf16[392,128]{1,0:T(8,128)(2,1)S(1)}, bf16[392,128]{1,0:T(8,128)(2,1)S(1)}, u32[]{:S(2)}, u32[]{:S(2)}) collective-permute-start(bf16[392,128]{1,0:T(8,128)(2,1)S(1)} %get-tuple-element.72), channel_id=1, source_target_pairs={{0,4},{2,6},{4,0},{6,2},{8,12},{10,14},{12,8},{14,10},{16,20},{18,... | collective-permute-start | bytes 301064 | tf_op jit(solution)/shard_map/ppermute | solution.py:534
  10.5 0.0 collective-permute-start.3
  10.6 1.2 %shard_map.140 = (bf16[1,1024,256]{2,1,0:T(8,128)(2,1)S(1)}, bf16[1,1024,256]{2,1,0:T(8,128)(2,1)S(1)}, f32[1,1024,384]{2,1,0:T(8,128)S(1)}, f32[1,3,8,128]{3,2,1,0:T(8,128)S(1)}, bf16[392,128]{1,0:T(8,128)(2,1)S(1)}) custom-call(bf16[128,256]{1,0:T(8,128)(2,1)S(1)} %get-tuple-element.66.in_ref, bf16[256,256]{1,0:T(8,128)(2,1)S(1)} %get-tuple-element.67.mid_ref.refs_1_, ...), custom_call_target="tpu_custom_call" | custom-call | flops 469762048 | bytes 2621440 | tf_op jit(solution)/shard_map/pallas_call | solution.py:37
  11.8 0.4 %collective-permute-done.1.refs_1_ = bf16[392,128]{1,0:T(8,128)(2,1)S(1)} collective-permute-done((bf16[392,128]{1,0:T(8,128)(2,1)S(1)}, bf16[392,128]{1,0:T(8,128)(2,1)S(1)}, u32[]{:S(2)}, u32[]{:S(2)}) %collective-permute-start.1) | collective-permute-done | bytes 100384 | tf_op jit(solution)/shard_map/ppermute | solution.py:534
  12.2 2.6 %collective-permute-done.2.refs_2_ = bf16[392,128]{1,0:T(8,128)(2,1)S(1)} collective-permute-done((bf16[392,128]{1,0:T(8,128)(2,1)S(1)}, bf16[392,128]{1,0:T(8,128)(2,1)S(1)}, u32[]{:S(2)}, u32[]{:S(2)}) %collective-permute-start.2) | collective-permute-done | bytes 100384 | tf_op jit(solution)/shard_map/ppermute | solution.py:534
  14.8 1.2 %collective-permute-done.3.refs_3_ = bf16[392,128]{1,0:T(8,128)(2,1)S(1)} collective-permute-done((bf16[392,128]{1,0:T(8,128)(2,1)S(1)}, bf16[392,128]{1,0:T(8,128)(2,1)S(1)}, u32[]{:S(2)}, u32[]{:S(2)}) %collective-permute-start.3) | collective-permute-done | bytes 100384 | tf_op jit(solution)/shard_map/ppermute | solution.py:534
  16.1 0.3 shard_map.141.refs_4_
  16.4 1.6 %collective-permute-start.4 = (bf16[392,128]{1,0:T(8,128)(2,1)S(1)}, bf16[392,128]{1,0:T(8,128)(2,1)S(1)}, u32[]{:S(2)}, u32[]{:S(2)}) collective-permute-start(bf16[392,128]{1,0:T(8,128)(2,1)S(1)} %shard_map.141.refs_4_), channel_id=1, source_target_pairs={{0,8},{2,10},{4,12},{6,14},{8,0},{10,2},{12,4},{14,6},{16,24},{18,... | collective-permute-start | bytes 301064 | tf_op jit(solution)/shard_map/ppermute | solution.py:534
  18.0 2.6 %collective-permute-start.5 = (bf16[392,128]{1,0:T(8,128)(2,1)S(1)}, bf16[392,128]{1,0:T(8,128)(2,1)S(1)}, u32[]{:S(2)}, u32[]{:S(2)}) collective-permute-start(bf16[392,128]{1,0:T(8,128)(2,1)S(1)} %shard_map.141.refs_4_), channel_id=1, source_target_pairs={{0,16},{2,18},{4,20},{6,22},{8,24},{10,26},{12,28},{14,30},{16,0},... | collective-permute-start | bytes 301064 | tf_op jit(solution)/shard_map/ppermute | solution.py:534
  20.6 0.2 collective-permute-start.6
  20.8 2.5 %shard_map.142 = (bf16[4,144,1024]{2,1,0:T(8,128)(2,1)S(1)}, bf16[256,256]{1,0:T(8,128)(2,1)S(1)}, bf16[512,256]{1,0:T(8,128)(2,1)S(1)}, bf16[3,272,1024]{2,1,0:...) custom-call(bf16[4,1024,128]{2,1,0:T(8,128)(2,1)S(1)} %get-tuple-ele, ...), custom_call_target="tpu_custom_call" | custom-call | flops 1879048192 | bytes 20971520 | tf_op jit(solution)/shard_map/pallas_call | solution.py:37
  23.4 0.0 collective-permute-done.4.refs_5_
  23.4 3.9 %collective-permute-done.5.refs_6_ = bf16[392,128]{1,0:T(8,128)(2,1)S(1)} collective-permute-done((bf16[392,128]{1,0:T(8,128)(2,1)S(1)}, bf16[392,128]{1,0:T(8,128)(2,1)S(1)}, u32[]{:S(2)}, u32[]{:S(2)}) %collective-permute-start.5) | collective-permute-done | bytes 100384 | tf_op jit(solution)/shard_map/ppermute | solution.py:534
  27.3 0.0 collective-permute-done.6.refs_7_
  27.3 0.6 %shard_map.143 = (bf16[392,128]{1,0:T(8,128)(2,1)S(1)}, bf16[392,128]{1,0:T(8,128)(2,1)S(1)}, bf16[392,128]{1,0:T(8,128)(2,1)S(1)}, bf16[392,128]{1,0:T(8,128)(2,1)S(1)}) custom-call(bf16[392,128]{1,0:T(8,128)(2,1)S(1)} %get-tuple-element.70.refs_0_, bf16[392,128]{1,0:T(8,128)(2,1)S(1)} %collective-permute-done.1.refs_1_, ...), custom_call_target="tpu_custom_call" | custom-call | flops 1000000 | bytes 1000000 | tf_op jit(solution)/shard_map/pallas_call | solution.py:37
  27.8 1.9 %collective-permute-start.9 = (bf16[392,128]{1,0:T(8,128)(2,1)S(1)}, bf16[392,128]{1,0:T(8,128)(2,1)S(1)}, u32[]{:S(2)}, u32[]{:S(2)}) collective-permute-start(bf16[392,128]{1,0:T(8,128)(2,1)S(1)} %get-tuple-element.91), channel_id=1, source_target_pairs={{0,2},{2,0},{4,6},{6,4},{8,10},{10,8},{12,14},{14,12},{16,18},{18,... | collective-permute-start | bytes 301064 | tf_op jit(solution)/shard_map/ppermute | solution.py:534
  29.7 0.5 %collective-permute-start.7 = (bf16[392,128]{1,0:T(8,128)(2,1)S(1)}, bf16[392,128]{1,0:T(8,128)(2,1)S(1)}, u32[]{:S(2)}, u32[]{:S(2)}) collective-permute-start(bf16[392,128]{1,0:T(8,128)(2,1)S(1)} %get-tuple-element.84), channel_id=1, source_target_pairs={{0,4},{2,6},{4,0},{6,2},{8,12},{10,14},{12,8},{14,10},{16,20},{18,... | collective-permute-start | bytes 301064 | tf_op jit(solution)/shard_map/ppermute | solution.py:534
  30.2 1.2 %collective-permute-start.8 = (bf16[392,128]{1,0:T(8,128)(2,1)S(1)}, bf16[392,128]{1,0:T(8,128)(2,1)S(1)}, u32[]{:S(2)}, u32[]{:S(2)}) collective-permute-start(bf16[392,128]{1,0:T(8,128)(2,1)S(1)} %get-tuple-element.85), channel_id=1, source_target_pairs={{0,6},{2,4},{4,2},{6,0},{8,14},{10,12},{12,10},{14,8},{16,22},{18,... | collective-permute-start | bytes 301064 | tf_op jit(solution)/shard_map/ppermute | solution.py:534
  31.4 2.0 %shard_map.144 = (f32[144,256]{1,0:T(8,128)S(1)}, f32[272,256]{1,0:T(8,128)S(1)}, f32[272,512]{1,0:T(8,128)S(1)}, f32[1,128]{1,0:T(1,128)S(1)}) custom-call(bf16[392,128]{1,0:T(8,128)(2,1)S(1)} %get-tuple-element.92.refs_0_, bf16[1,1024,256]{2,1,0:T(8,128)(2,1)S(1)} %get-tuple-element.79.refs_7_.refs_1_, ...), custom_call_target="tpu_custom_call" | custom-call | flops 939524096 | bytes 2621440 | tf_op jit(solution)/shard_map/pallas_call | solution.py:37
  33.4 0.0 collective-permute-done.9.refs_0_
  33.4 2.1 %shard_map.145 = (f32[144,256]{1,0:T(8,128)S(1)}, f32[272,256]{1,0:T(8,128)S(1)}, f32[272,512]{1,0:T(8,128)S(1)}, f32[1,128]{1,0:T(1,128)S(1)}) custom-call(bf16[392,128]{1,0:T(8,128)(2,1)S(1)} %collective-permute-done.9.refs_0_, bf16[3,1024,256]{2,1,0:T(8,128)(2,1)S(1)} %get-tuple-element.75.refs_3_.refs_1_.refs_2_, ...), custom_call_target="tpu_custom_call" | custom-call | flops 939524096 | bytes 2621440 | tf_op jit(solution)/shard_map/pallas_call | solution.py:37
  35.5 0.0 collective-permute-done.7.refs_0_
  35.5 0.2 collective-permute-done.8.refs_1_
  35.7 0.0 copy-start
  35.7 0.0 copy-start.1
  35.7 0.0 copy-start.2
  35.7 0.0 copy-start.3
  35.7 4.0 %shard_map.146 = (f32[1,512]{1,0:T(1,128)}, f32[784,128]{1,0:T(8,128)S(1)}, f32[784,128]{1,0:T(8,128)S(1)}) custom-call(bf16[392,128]{1,0:T(8,128)(2,1)S(1)} %collective-permute-done.7.refs_0_, bf16[392,128]{1,0:T(8,128)(2,1)S(1)} %collective-permute-done.8.refs_1_, bf16[3,1024,256]{2,1,0:T(8,128)(2,1)S(1)} %get-tuple-element.75.refs_3_.refs_1_.refs_2_, ...), custom_call_target="tpu_custom_call" | custom-call | flops 1879048192 | bytes 5242880 | tf_op jit(solution)/shard_map/pallas_call | solution.py:37
  39.7 0.0 collective-permute-start.10
  39.7 1.7 %collective-permute-done.10.refs_1_ = f32[784,128]{1,0:T(8,128)S(1)} collective-permute-done((f32[784,128]{1,0:T(8,128)S(1)}, f32[784,128]{1,0:T(8,128)S(1)}, u32[]{:S(2)}, u32[]{:S(2)}) %collective-permute-start.10) | collective-permute-done | bytes 401440 | tf_op jit(solution)/shard_map/ppermute | solution.py:727
  41.5 0.0 copy-done
  41.5 0.0 copy-done.1
  41.5 0.0 copy-done.2
  41.5 0.0 copy-done.3
  41.5 1.1 %shard_map.147 = (f32[3,1,64,256]{3,2,1,0:T(8,128)}, f32[3,1,128,256]{3,2,1,0:T(8,128)}, f32[3,1,128,384]{3,2,1,0:T(8,128)}, f32[3,1,576]{2,1,0:T(1,128)}) custom-call(f32[784,128]{1,0:T(8,128)S(1)} %get-tuple-element.104.refs_0_, f32[784,128]{1,0:T(8,128)S(1)} %collective-permute-done.10.refs_1_, f32[3,1,64,256]{3,2,1,0:T(8,128)S(1)} %copy-done.2, ...), custom_call_target="tpu_custom_call" | custom-call | flops 1000000 | bytes 1000000 | tf_op jit(solution)/shard_map/pallas_call | solution.py:37
Async XLA Ops:
  2.0 1.6 %collective-permute-start = (bf16[784,128]{1,0:T(8,128)(2,1)S(1)}, bf16[784,128]{1,0:T(8,128)(2,1)S(1)}, u32[]{:S(2)}, u32[]{:S(2)}) collective-permute-start(bf16[784,128]{1,0:T(8,128)(2,1)S(1)} %get-tuple-element.58.refs_0_), channel_id=1, source_target_pairs={{0,1},{1,0},{2,3},{3,2},{4,5},{5,4},{6,7},{7,6},{8,9},{9,8},{10,11... | collective-permute-start | bytes 602120 | tf_op jit(solution)/shard_map/ppermute | solution.py:581
  6.1 6.1 %collective-permute-start.1 = (bf16[392,128]{1,0:T(8,128)(2,1)S(1)}, bf16[392,128]{1,0:T(8,128)(2,1)S(1)}, u32[]{:S(2)}, u32[]{:S(2)}) collective-permute-start(bf16[392,128]{1,0:T(8,128)(2,1)S(1)} %get-tuple-element.71), channel_id=1, source_target_pairs={{0,2},{2,0},{4,6},{6,4},{8,10},{10,8},{12,14},{14,12},{16,18},{18,... | collective-permute-start | bytes 301064 | tf_op jit(solution)/shard_map/ppermute | solution.py:534
  9.0 5.8 %collective-permute-start.2 = (bf16[392,128]{1,0:T(8,128)(2,1)S(1)}, bf16[392,128]{1,0:T(8,128)(2,1)S(1)}, u32[]{:S(2)}, u32[]{:S(2)}) collective-permute-start(bf16[392,128]{1,0:T(8,128)(2,1)S(1)} %get-tuple-element.72), channel_id=1, source_target_pairs={{0,4},{2,6},{4,0},{6,2},{8,12},{10,14},{12,8},{14,10},{16,20},{18,... | collective-permute-start | bytes 301064 | tf_op jit(solution)/shard_map/ppermute | solution.py:534
  10.5 5.5 %collective-permute-start.3 = (bf16[392,128]{1,0:T(8,128)(2,1)S(1)}, bf16[392,128]{1,0:T(8,128)(2,1)S(1)}, u32[]{:S(2)}, u32[]{:S(2)}) collective-permute-start(bf16[392,128]{1,0:T(8,128)(2,1)S(1)} %get-tuple-element.73), channel_id=1, source_target_pairs={{0,6},{2,4},{4,2},{6,0},{8,14},{10,12},{12,10},{14,8},{16,22},{18,... | collective-permute-start | bytes 301064 | tf_op jit(solution)/shard_map/ppermute | solution.py:534
  16.4 7.0 %collective-permute-start.4 = (bf16[392,128]{1,0:T(8,128)(2,1)S(1)}, bf16[392,128]{1,0:T(8,128)(2,1)S(1)}, u32[]{:S(2)}, u32[]{:S(2)}) collective-permute-start(bf16[392,128]{1,0:T(8,128)(2,1)S(1)} %shard_map.141.refs_4_), channel_id=1, source_target_pairs={{0,8},{2,10},{4,12},{6,14},{8,0},{10,2},{12,4},{14,6},{16,24},{18,... | collective-permute-start | bytes 301064 | tf_op jit(solution)/shard_map/ppermute | solution.py:534
  18.0 9.2 %collective-permute-start.5 = (bf16[392,128]{1,0:T(8,128)(2,1)S(1)}, bf16[392,128]{1,0:T(8,128)(2,1)S(1)}, u32[]{:S(2)}, u32[]{:S(2)}) collective-permute-start(bf16[392,128]{1,0:T(8,128)(2,1)S(1)} %shard_map.141.refs_4_), channel_id=1, source_target_pairs={{0,16},{2,18},{4,20},{6,22},{8,24},{10,26},{12,28},{14,30},{16,0},... | collective-permute-start | bytes 301064 | tf_op jit(solution)/shard_map/ppermute | solution.py:534
  20.6 6.6 %collective-permute-start.6 = (bf16[392,128]{1,0:T(8,128)(2,1)S(1)}, bf16[392,128]{1,0:T(8,128)(2,1)S(1)}, u32[]{:S(2)}, u32[]{:S(2)}) collective-permute-start(bf16[392,128]{1,0:T(8,128)(2,1)S(1)} %shard_map.141.refs_4_), channel_id=1, source_target_pairs={{0,24},{2,26},{4,28},{6,30},{8,16},{10,18},{12,20},{14,22},{16,8},... | collective-permute-start | bytes 301064 | tf_op jit(solution)/shard_map/ppermute | solution.py:534
  27.8 5.6 %collective-permute-start.9 = (bf16[392,128]{1,0:T(8,128)(2,1)S(1)}, bf16[392,128]{1,0:T(8,128)(2,1)S(1)}, u32[]{:S(2)}, u32[]{:S(2)}) collective-permute-start(bf16[392,128]{1,0:T(8,128)(2,1)S(1)} %get-tuple-element.91), channel_id=1, source_target_pairs={{0,2},{2,0},{4,6},{6,4},{8,10},{10,8},{12,14},{14,12},{16,18},{18,... | collective-permute-start | bytes 301064 | tf_op jit(solution)/shard_map/ppermute | solution.py:534
  29.7 5.8 %collective-permute-start.7 = (bf16[392,128]{1,0:T(8,128)(2,1)S(1)}, bf16[392,128]{1,0:T(8,128)(2,1)S(1)}, u32[]{:S(2)}, u32[]{:S(2)}) collective-permute-start(bf16[392,128]{1,0:T(8,128)(2,1)S(1)} %get-tuple-element.84), channel_id=1, source_target_pairs={{0,4},{2,6},{4,0},{6,2},{8,12},{10,14},{12,8},{14,10},{16,20},{18,... | collective-permute-start | bytes 301064 | tf_op jit(solution)/shard_map/ppermute | solution.py:534
  30.2 5.5 %collective-permute-start.8 = (bf16[392,128]{1,0:T(8,128)(2,1)S(1)}, bf16[392,128]{1,0:T(8,128)(2,1)S(1)}, u32[]{:S(2)}, u32[]{:S(2)}) collective-permute-start(bf16[392,128]{1,0:T(8,128)(2,1)S(1)} %get-tuple-element.85), channel_id=1, source_target_pairs={{0,6},{2,4},{4,2},{6,0},{8,14},{10,12},{12,10},{14,8},{16,22},{18,... | collective-permute-start | bytes 301064 | tf_op jit(solution)/shard_map/ppermute | solution.py:534
  35.7 5.7 %copy-start = (f32[3,1,128,384]{3,2,1,0:T(8,128)S(1)}, f32[3,1,128,384]{3,2,1,0:T(8,128)}, u32[]{:S(2)}) copy-start(f32[3,1,128,384]{3,2,1,0:T(8,128)} %refs_4_.3) | copy-start | bytes 1769476
  35.7 5.7 %copy-start.1 = (f32[3,1,128,256]{3,2,1,0:T(8,128)S(1)}, f32[3,1,128,256]{3,2,1,0:T(8,128)}, u32[]{:S(2)}) copy-start(f32[3,1,128,256]{3,2,1,0:T(8,128)} %refs_3_.3) | copy-start | bytes 1179652
  35.7 5.7 %copy-start.2 = (f32[3,1,64,256]{3,2,1,0:T(8,128)S(1)}, f32[3,1,64,256]{3,2,1,0:T(8,128)}, u32[]{:S(2)}) copy-start(f32[3,1,64,256]{3,2,1,0:T(8,128)} %refs_2_.3) | copy-start | bytes 589828
  35.7 5.8 %copy-start.3 = (f32[3,1,576]{2,1,0:T(1,128)S(1)}, f32[3,1,576]{2,1,0:T(1,128)}, u32[]{:S(2)}) copy-start(f32[3,1,576]{2,1,0:T(1,128)} %refs_5_.3) | copy-start | bytes 20740
  39.7 1.7 %collective-permute-start.10 = (f32[784,128]{1,0:T(8,128)S(1)}, f32[784,128]{1,0:T(8,128)S(1)}, u32[]{:S(2)}, u32[]{:S(2)}) collective-permute-start(f32[784,128]{1,0:T(8,128)S(1)} %get-tuple-element.105), channel_id=1, source_target_pairs={{0,1},{1,0},{2,3},{3,2},{4,5},{5,4},{6,7},{7,6},{8,9},{9,8},{10,11... | collective-permute-start | bytes 1204232 | tf_op jit(solution)/shard_map/ppermute | solution.py:727

commit v5 on v4

--- a/solution.py
+++ b/solution.py
@@ -166,6 +166,10 @@
     return (*mats, vec)
 
 
+def product(left, right):
+    return jnp.dot(left, right, preferred_element_type=f32)
+
+
 def forward_slots(slots, weights, enc_ref, geometry_ref, message_refs, kept):
     in_weight, mid_ref, head_ref, vec = weights
     one_ref, two_ref, turn_ref, scalar_ref = kept
@@ -176,21 +180,24 @@
     bias_two = vec[:, hidden : 2 * hidden]
     half_bias = 0.5 * vec[:, 3 * hidden :]
     lane = lanes_of((ray_count, LANES))
-    densities = []
+    ones, twos, densities = ([], [], [])
     for i, k in enumerate(slots):
-        one = jnp.dot(enc_ref[k], in_weight, preferred_element_type=f32) + bias_one
-        one = jnp.maximum(one, 0.0).astype(bf16)
-        one_ref[i] = one
-        two = jnp.dot(one, mid_ref[...], preferred_element_type=f32) + bias_two
-        two = jnp.maximum(two, 0.0).astype(bf16)
-        two_ref[i] = two
-        raw = jnp.dot(two, head_ref[...], preferred_element_type=f32)
-        turn_ref[i] = jnp.tanh(raw[:, :feat] + half_bias)
+        one = product(enc_ref[k], in_weight) + bias_one
+        ones.append(jnp.maximum(one, 0.0).astype(bf16))
+        one_ref[i] = ones[i]
+    for i in range(len(slots)):
+        two = product(ones[i], mid_ref[...]) + bias_two
+        twos.append(jnp.maximum(two, 0.0).astype(bf16))
+        two_ref[i] = twos[i]
+    raws = [product(two, head_ref[:, feat:]) for two in twos]
+    for raw in raws:
         density = jnp.zeros((ray_count, LANES), f32)
         for j in range(samples):
             rows = slice(ray_count * j, ray_count * (j + 1))
-            density = jnp.where(lane == j, raw[rows, feat:], density)
+            density = jnp.where(lane == j, raw[rows], density)
         densities.append(density)
+    for i in range(len(slots)):
+        turn_ref[i] = jnp.tanh(product(twos[i], head_ref[:, :feat]) + half_bias)
     density = side_by_side([value.T[:samples] for value in densities])
     geometry = side_by_side([geometry_ref[k, :samples] for k in slots])
     direction = side_by_side([geometry_ref[k, samples : samples + 1] for k in slots])
@@ -366,11 +373,17 @@
 
 
 def ready_body(*refs):
-    enc_ref, mid_ref, head_ref, *refs = refs
-    count = (len(refs) - 3) // 7
+    *refs, sems = refs
+    states, (enc_ref, mid_ref, head_ref, *refs) = (refs[:4], refs[4:])
+    count = (len(refs) - 7) // 7
     sources = [refs[4 * n : 4 * n + 4] for n in range(count)]
-    enc_turned, mid_turned, head_turned, *refs = refs[4 * count :]
+    fetched, refs = (refs[4 * count : 4 * count + 4], refs[4 * count + 4 :])
+    enc_turned, mid_turned, head_turned, *refs = refs
     results = [refs[3 * n : 3 * n + 3] for n in range(count)]
+    copies = []
+    for n, (source, place) in enumerate(zip(states, fetched)):
+        copies.append(pltpu.make_async_copy(source, place, sems.at[n]))
+        copies[-1].start()
     mid_turned[...] = mid_ref[...].T
     feat = sources[0][2].shape[2]
     head = head_ref[...].astype(f32)
@@ -390,10 +403,8 @@
                 rows = slice(ray_count * j, ray_count * (j + 1))
                 turn = turn_ref[i, rows, :]
                 slope_ref[i, rows, :] = columns[:, j : j + 1] * (1.0 - turn * turn)
-
-
-def product(left, right):
-    return jnp.dot(left, right, preferred_element_type=f32)
+    for copy in copies:
+        copy.wait()
 
 
 def backward_body(*refs, slots, offset, before, last, group_count, shapes, vec_share, shards):
@@ -462,12 +473,12 @@
             pieces.append(jnp.concatenate([colour_grad, density_part], 1))
         head_grad = jnp.concatenate(pieces, 0)
         second = product(head_grad, head_turned[...]).astype(bf16)
+        sums[2] = sums[2] + product(two_turned[offset + i], head_grad)
         second = jnp.where(two_ref[offset + i] > 0, second, zero)
         first = product(second, mid_turned[...]).astype(bf16)
+        sums[1] = sums[1] + product(one_turned[offset + i], second)
         first = jnp.where(one_ref[offset + i] > 0, first, zero)
         sums[0] = sums[0] + product(enc_turned[k], first)
-        sums[1] = sums[1] + product(one_turned[offset + i], second)
-        sums[2] = sums[2] + product(two_turned[offset + i], head_grad)
     if not last:
         for value, ref in zip(sums, outs):
             ref[...] = value
@@ -495,8 +506,9 @@
 
 
 def adam_body(*refs, shards):
-    grad_refs = refs[:shards]
-    state_refs, out_refs = (refs[shards : shards + 4], refs[shards + 4 :])
+    grad_refs, (depth_ref, *refs) = (refs[:shards], refs[shards:])
+    state_refs, out_refs, depth_out = (refs[:4], refs[4:8], refs[8])
+    depth_out[...] = depth_ref[...]
 
     def update(stacked, gradient):
         first_moment = beta_one * stacked[1] + (1.0 - beta_one) * gradient
@@ -660,20 +672,26 @@
             pltpu.VMEM((count, rows, feat), f32),
         )
 
-    enc_turned, *results = call(
+    hbm, vmem = (pl.BlockSpec(memory_space=m) for m in (pltpu.HBM, pltpu.VMEM))
+    local = [encoded, weights[1], weights[2], *sum(map(list, kept), [])]
+    results = call(
         ready_body,
-        (
+        tuple(pltpu.VMEM(s.shape, f32) for s in states)
+        + (
             pltpu.VMEM((quad, code_width + 16, rows), bf16),
             pltpu.VMEM((hidden, hidden), bf16),
             pltpu.VMEM((feat + LANES, hidden), bf16),
         )
         + sum((ready_shapes(len(slots)) for slots in groups), ()),
-        [in_vmem(v) for v in (encoded, weights[1], weights[2], *sum(map(list, kept), []))],
+        [in_hbm(s) for s in states] + [in_vmem(v) for v in local],
         16,
+        scratch=[pltpu.SemaphoreType.DMA((4,))],
+        specs=[hbm] * 4 + [vmem] * len(local),
         flops=quad * flops,
         moved=2 * moved(quad),
     )
-    turned_weights, results = (results[:2], results[2:])
+    states_near, enc_turned, turned_weights = (results[:4], results[4], results[5:7])
+    results = results[7:]
     ready = [results[3 * n : 3 * n + 3] for n in range(len(groups))]
     replies = call(
         functools.partial(owner_body, slots=quad, planes=planes),
@@ -694,7 +712,7 @@
         last = slots == steps[-1][1]
         if last:
             share = pltpu.VMEM((pack_rows, LANES), f32)
-            out_shape = (shaped((1, ray_count), f32), share, share)
+            out_shape = (pltpu.VMEM((1, ray_count), f32), share, share)
             if not pair:
                 out_shape = (out_shape[0], shaped((shards, pack_rows, LANES), f32))
         else:
@@ -728,13 +746,12 @@
     else:
         exchanged = lax.all_to_all(grads[0], "rays", 0, 0)
         parts = tuple(exchanged[s] for s in range(shards))
-    new = call(
+    return call(
         functools.partial(adam_body, shards=shards),
-        tuple(shaped(s.shape, f32) for s in states),
-        (*parts, *states),
+        tuple(shaped(s.shape, f32) for s in states) + (shaped(depth_grad.shape, f32),),
+        [in_vmem(v) for v in (*parts, depth_grad, *states_near)],
         16,
     )
-    return (*new, depth_grad)
 
 
 def solution(mesh):

time: 42.8 us -> 41.6 us (0.972)
  Pallas kernels: 18.5 us -> 16.3 us
  waiting for transfers between devices: 10.4 us -> 11.4 us
    pallas_call x11, Pallas kernels: 18.5 us -> 16.3 us  [call(): pl.pallas_call(body, out_shape=out_shape, in_specs=specs or [spec] * len(...]
    ppermute x9, waiting for transfers between devices: 8.39 us -> 9.41 us  [swap(): lax.ppermute(value, 'region', [(i, i ^ distance) for i in range(size)])]
  transfers between devices with their start and end apart: 11 -> 11, of which waited for: 7 -> 7; matrix products, arithmetic and copies ran while one was open for 0% -> 0% of each run, Pallas kernels for 20% -> 18%
where the time goes in v5:
time: 41.6 us; the launch traced here: 41.5 us
  Pallas kernels  16.3 us (39%)
  starting transfers between devices  13.1 us (31%)
  waiting for transfers between devices  11.4 us (27%)
  between operations  0.72 us (2%)
    pallas_call x11, Pallas kernels, call(): pl.pallas_call(body, out_shape=out_shape, in_specs=specs or [spec] * len(...  16.3 us
    ppermute x9, starting transfers between devices, swap(): lax.ppermute(value, 'region', [(i, i ^ distance) for i in range(size)])  12.5 us
    ppermute x9, waiting for transfers between devices, swap(): lax.ppermute(value, 'region', [(i, i ^ distance) for i in range(size)])  9.41 us
    ppermute x1, waiting for transfers between devices, per_device(): parts = (grads[0], lax.ppermute(grads[1], 'rays', [(0, 1), (1, 0)]))  1.72 us
  transfers between devices with their start and end apart: 11, of which 7 were waited for; matrix products, arithmetic and copies ran while one was open for 0% of the time, Pallas kernels for 18%

profile of v5, /device:TPU:0, one launch (start us, length us, event | category | flops | bytes accessed | tf_op | source)
XLA Modules:
  0.0 41.5 jit_solution(7910313431586780049)
XLA Ops:
  0.6 1.3 %shard_map.137 = (bf16[784,128]{1,0:T(8,128)(2,1)S(1)}, bf16[2,512,128]{2,1,0:T(8,128)(2,1)S(1)}, s32[1,8,512]{2,1,0:T(8,128)S(1)}, s32[1,512]{1,0:T(1,128)S(1)}...) custom-call(f32[3,1,64,256]{3,2,1,0:T(8,128)} %refs_0_.3, f32[3,1,128,256]{3,2,1,0:T(8,128)} %refs_1_.3, ...), custom_call_target="tpu_custom_call" | custom-call | flops 1000000 | bytes 1000000 | tf_op jit(solution)/shard_map/pallas_call | solution.py:37
  2.0 0.5 %collective-permute-start = (bf16[784,128]{1,0:T(8,128)(2,1)S(1)}, bf16[784,128]{1,0:T(8,128)(2,1)S(1)}, u32[]{:S(2)}, u32[]{:S(2)}) collective-permute-start(bf16[784,128]{1,0:T(8,128)(2,1)S(1)} %get-tuple-element.58.refs_0_), channel_id=1, source_target_pairs={{0,1},{1,0},{2,3},{3,2},{4,5},{5,4},{6,7},{7,6},{8,9},{9,8},{10,11... | collective-permute-start | bytes 602120 | tf_op jit(solution)/shard_map/ppermute | solution.py:593
  2.5 0.8 %shard_map.138 = (bf16[4,1024,128]{2,1,0:T(8,128)(2,1)S(1)}, f32[4,16,128]{2,1,0:T(8,128)S(1)}) custom-call(bf16[2,512,128]{2,1,0:T(8,128)(2,1)S(1)} %get-tuple-element.59.refs_0_, s32[1,8,512]{2,1,0:T(8,128)S(1)} %get-tuple-element.60.refs_1_, s32[1,512]{1,0:T(1,128)S(1)} %get-tuple-element.61.refs_2_, s32[1,512]{1,0:T(1,128)S(1)} %get-tuple-element.62.refs_3_, ...), custom_call_target="tpu_custom_call" | custom-call | flops 5242880 | bytes 2097152 | tf_op jit(solution)/shard_map/pallas_call | solution.py:37
  3.3 0.2 collective-permute-done.refs_1_
  3.6 2.5 %shard_map.139 = (bf16[128,256]{1,0:T(8,128)(2,1)S(1)}, bf16[256,256]{1,0:T(8,128)(2,1)S(1)}, bf16[256,512]{1,0:T(8,128)(2,1)S(1)}, f32[1,1152]{1,0:T(1,128)S(1)...) custom-call(bf16[784,128]{1,0:T(8,128)(2,1)S(1)} %get-tuple-element., ...), custom_call_target="tpu_custom_call" | custom-call | flops 1409286144 | bytes 7864320 | tf_op jit(solution)/shard_map/pallas_call | solution.py:37
  6.1 2.9 %collective-permute-start.1 = (bf16[392,128]{1,0:T(8,128)(2,1)S(1)}, bf16[392,128]{1,0:T(8,128)(2,1)S(1)}, u32[]{:S(2)}, u32[]{:S(2)}) collective-permute-start(bf16[392,128]{1,0:T(8,128)(2,1)S(1)} %get-tuple-element.71), channel_id=1, source_target_pairs={{0,2},{2,0},{4,6},{6,4},{8,10},{10,8},{12,14},{14,12},{16,18},{18,... | collective-permute-start | bytes 301064 | tf_op jit(solution)/shard_map/ppermute | solution.py:546
  9.0 1.5 %collective-permute-start.2 = (bf16[392,128]{1,0:T(8,128)(2,1)S(1)}, bf16[392,128]{1,0:T(8,128)(2,1)S(1)}, u32[]{:S(2)}, u32[]{:S(2)}) collective-permute-start(bf16[392,128]{1,0:T(8,128)(2,1)S(1)} %get-tuple-element.72), channel_id=1, source_target_pairs={{0,4},{2,6},{4,0},{6,2},{8,12},{10,14},{12,8},{14,10},{16,20},{18,... | collective-permute-start | bytes 301064 | tf_op jit(solution)/shard_map/ppermute | solution.py:546
  10.5 0.0 collective-permute-start.3
  10.5 1.1 %shard_map.140 = (bf16[1,1024,256]{2,1,0:T(8,128)(2,1)S(1)}, bf16[1,1024,256]{2,1,0:T(8,128)(2,1)S(1)}, f32[1,1024,384]{2,1,0:T(8,128)S(1)}, f32[1,3,8,128]{3,2,1,0:T(8,128)S(1)}, bf16[392,128]{1,0:T(8,128)(2,1)S(1)}) custom-call(bf16[128,256]{1,0:T(8,128)(2,1)S(1)} %get-tuple-element.66.in_ref, bf16[256,256]{1,0:T(8,128)(2,1)S(1)} %get-tuple-element.67.mid_ref.refs_5_, ...), custom_call_target="tpu_custom_call" | custom-call | flops 469762048 | bytes 2621440 | tf_op jit(solution)/shard_map/pallas_call | solution.py:37
  11.7 0.5 %collective-permute-done.1.refs_1_ = bf16[392,128]{1,0:T(8,128)(2,1)S(1)} collective-permute-done((bf16[392,128]{1,0:T(8,128)(2,1)S(1)}, bf16[392,128]{1,0:T(8,128)(2,1)S(1)}, u32[]{:S(2)}, u32[]{:S(2)}) %collective-permute-start.1) | collective-permute-done | bytes 100384 | tf_op jit(solution)/shard_map/ppermute | solution.py:546
  12.2 2.6 %collective-permute-done.2.refs_2_ = bf16[392,128]{1,0:T(8,128)(2,1)S(1)} collective-permute-done((bf16[392,128]{1,0:T(8,128)(2,1)S(1)}, bf16[392,128]{1,0:T(8,128)(2,1)S(1)}, u32[]{:S(2)}, u32[]{:S(2)}) %collective-permute-start.2) | collective-permute-done | bytes 100384 | tf_op jit(solution)/shard_map/ppermute | solution.py:546
  14.8 1.2 %collective-permute-done.3.refs_3_ = bf16[392,128]{1,0:T(8,128)(2,1)S(1)} collective-permute-done((bf16[392,128]{1,0:T(8,128)(2,1)S(1)}, bf16[392,128]{1,0:T(8,128)(2,1)S(1)}, u32[]{:S(2)}, u32[]{:S(2)}) %collective-permute-start.3) | collective-permute-done | bytes 100384 | tf_op jit(solution)/shard_map/ppermute | solution.py:546
  16.1 0.3 shard_map.141.refs_4_
  16.4 1.6 %collective-permute-start.4 = (bf16[392,128]{1,0:T(8,128)(2,1)S(1)}, bf16[392,128]{1,0:T(8,128)(2,1)S(1)}, u32[]{:S(2)}, u32[]{:S(2)}) collective-permute-start(bf16[392,128]{1,0:T(8,128)(2,1)S(1)} %shard_map.141.refs_4_), channel_id=1, source_target_pairs={{0,8},{2,10},{4,12},{6,14},{8,0},{10,2},{12,4},{14,6},{16,24},{18,... | collective-permute-start | bytes 301064 | tf_op jit(solution)/shard_map/ppermute | solution.py:546
  18.0 2.6 %collective-permute-start.5 = (bf16[392,128]{1,0:T(8,128)(2,1)S(1)}, bf16[392,128]{1,0:T(8,128)(2,1)S(1)}, u32[]{:S(2)}, u32[]{:S(2)}) collective-permute-start(bf16[392,128]{1,0:T(8,128)(2,1)S(1)} %shard_map.141.refs_4_), channel_id=1, source_target_pairs={{0,16},{2,18},{4,20},{6,22},{8,24},{10,26},{12,28},{14,30},{16,0},... | collective-permute-start | bytes 301064 | tf_op jit(solution)/shard_map/ppermute | solution.py:546
  20.6 0.2 collective-permute-start.6
  20.8 2.6 %shard_map.142 = (f32[3,1,64,256]{3,2,1,0:T(8,128)S(1)}, f32[3,1,128,256]{3,2,1,0:T(8,128)S(1)}, f32[3,1,128,384]{3,2,1,0:T(8,128)S(1)}, f32[3,1,576]{2,1,0:T(1,...) custom-call(f32[3,1,64,256]{3,2,1,0:T(8,128)} %refs_0_.3, ...), custom_call_target="tpu_custom_call" | custom-call | flops 1879048192 | bytes 20971520 | tf_op jit(solution)/shard_map/pallas_call | solution.py:37
  23.4 0.0 collective-permute-done.4.refs_5_
  23.4 3.8 %collective-permute-done.5.refs_6_ = bf16[392,128]{1,0:T(8,128)(2,1)S(1)} collective-permute-done((bf16[392,128]{1,0:T(8,128)(2,1)S(1)}, bf16[392,128]{1,0:T(8,128)(2,1)S(1)}, u32[]{:S(2)}, u32[]{:S(2)}) %collective-permute-start.5) | collective-permute-done | bytes 100384 | tf_op jit(solution)/shard_map/ppermute | solution.py:546
  27.2 0.0 collective-permute-done.6.refs_7_
  27.2 0.6 %shard_map.143 = (bf16[392,128]{1,0:T(8,128)(2,1)S(1)}, bf16[392,128]{1,0:T(8,128)(2,1)S(1)}, bf16[392,128]{1,0:T(8,128)(2,1)S(1)}, bf16[392,128]{1,0:T(8,128)(2,1)S(1)}) custom-call(bf16[392,128]{1,0:T(8,128)(2,1)S(1)} %get-tuple-element.70.refs_0_, bf16[392,128]{1,0:T(8,128)(2,1)S(1)} %collective-permute-done.1.refs_1_, ...), custom_call_target="tpu_custom_call" | custom-call | flops 1000000 | bytes 1000000 | tf_op jit(solution)/shard_map/pallas_call | solution.py:37
  27.8 1.9 %collective-permute-start.9 = (bf16[392,128]{1,0:T(8,128)(2,1)S(1)}, bf16[392,128]{1,0:T(8,128)(2,1)S(1)}, u32[]{:S(2)}, u32[]{:S(2)}) collective-permute-start(bf16[392,128]{1,0:T(8,128)(2,1)S(1)} %get-tuple-element.91), channel_id=1, source_target_pairs={{0,2},{2,0},{4,6},{6,4},{8,10},{10,8},{12,14},{14,12},{16,18},{18,... | collective-permute-start | bytes 301064 | tf_op jit(solution)/shard_map/ppermute | solution.py:546
  29.7 0.5 %collective-permute-start.7 = (bf16[392,128]{1,0:T(8,128)(2,1)S(1)}, bf16[392,128]{1,0:T(8,128)(2,1)S(1)}, u32[]{:S(2)}, u32[]{:S(2)}) collective-permute-start(bf16[392,128]{1,0:T(8,128)(2,1)S(1)} %get-tuple-element.84), channel_id=1, source_target_pairs={{0,4},{2,6},{4,0},{6,2},{8,12},{10,14},{12,8},{14,10},{16,20},{18,... | collective-permute-start | bytes 301064 | tf_op jit(solution)/shard_map/ppermute | solution.py:546
  30.2 1.2 %collective-permute-start.8 = (bf16[392,128]{1,0:T(8,128)(2,1)S(1)}, bf16[392,128]{1,0:T(8,128)(2,1)S(1)}, u32[]{:S(2)}, u32[]{:S(2)}) collective-permute-start(bf16[392,128]{1,0:T(8,128)(2,1)S(1)} %get-tuple-element.85), channel_id=1, source_target_pairs={{0,6},{2,4},{4,2},{6,0},{8,14},{10,12},{12,10},{14,8},{16,22},{18,... | collective-permute-start | bytes 301064 | tf_op jit(solution)/shard_map/ppermute | solution.py:546
  31.4 1.5 %shard_map.144 = (f32[144,256]{1,0:T(8,128)S(1)}, f32[272,256]{1,0:T(8,128)S(1)}, f32[272,512]{1,0:T(8,128)S(1)}, f32[1,128]{1,0:T(1,128)S(1)}) custom-call(bf16[392,128]{1,0:T(8,128)(2,1)S(1)} %get-tuple-element.92.refs_0_, bf16[1,1024,256]{2,1,0:T(8,128)(2,1)S(1)} %get-tuple-element.79.refs_11_.refs_1_, ...), custom_call_target="tpu_custom_call" | custom-call | flops 939524096 | bytes 2621440 | tf_op jit(solution)/shard_map/pallas_call | solution.py:37
  32.9 0.0 collective-permute-done.9.refs_0_
  32.9 1.6 %shard_map.145 = (f32[144,256]{1,0:T(8,128)S(1)}, f32[272,256]{1,0:T(8,128)S(1)}, f32[272,512]{1,0:T(8,128)S(1)}, f32[1,128]{1,0:T(1,128)S(1)}) custom-call(bf16[392,128]{1,0:T(8,128)(2,1)S(1)} %collective-permute-done.9.refs_0_, bf16[3,1024,256]{2,1,0:T(8,128)(2,1)S(1)} %get-tuple-element.75.refs_7_.refs_1_.refs_2_, ...), custom_call_target="tpu_custom_call" | custom-call | flops 939524096 | bytes 2621440 | tf_op jit(solution)/shard_map/pallas_call | solution.py:37
  34.5 0.0 collective-permute-done.7.refs_0_
  34.5 1.2 %collective-permute-done.8.refs_1_ = bf16[392,128]{1,0:T(8,128)(2,1)S(1)} collective-permute-done((bf16[392,128]{1,0:T(8,128)(2,1)S(1)}, bf16[392,128]{1,0:T(8,128)(2,1)S(1)}, u32[]{:S(2)}, u32[]{:S(2)}) %collective-permute-start.8) | collective-permute-done | bytes 100384 | tf_op jit(solution)/shard_map/ppermute | solution.py:546
  35.7 2.8 %shard_map.146 = (f32[1,512]{1,0:T(1,128)S(1)}, f32[784,128]{1,0:T(8,128)S(1)}, f32[784,128]{1,0:T(8,128)S(1)}) custom-call(bf16[392,128]{1,0:T(8,128)(2,1)S(1)} %collective-permute-done.7.refs_0_, bf16[392,128]{1,0:T(8,128)(2,1)S(1)} %collective-permute-done.8.refs_1_, bf16[3,1024,256]{2,1,0:T(8,128)(2,1)S(1)} %get-tuple-element.75.refs_7_.refs_1_.refs_2_, ...), custom_call_target="tpu_custom_call" | custom-call | flops 1879048192 | bytes 5242880 | tf_op jit(solution)/shard_map/pallas_call | solution.py:37
  38.5 0.1 collective-permute-start.10
  38.6 1.7 %collective-permute-done.10.refs_1_ = f32[784,128]{1,0:T(8,128)S(1)} collective-permute-done((f32[784,128]{1,0:T(8,128)S(1)}, f32[784,128]{1,0:T(8,128)S(1)}, u32[]{:S(2)}, u32[]{:S(2)}) %collective-permute-start.10) | collective-permute-done | bytes 401440 | tf_op jit(solution)/shard_map/ppermute | solution.py:745
  40.3 1.2 %shard_map.147 = (f32[3,1,64,256]{3,2,1,0:T(8,128)}, f32[3,1,128,256]{3,2,1,0:T(8,128)}, f32[3,1,128,384]{3,2,1,0:T(8,128)}, f32[3,1,576]{2,1,0:T(1,128)}, f32[1,512]{1,0:T(1,128)}) custom-call(f32[784,128]{1,0:T(8,128)S(1)} %get-tuple-element.104.refs_0_, f32[784,128]{1,0:T(8,128)S(1)} %collective-permute-done.10.refs_1_, ...), custom_call_target="tpu_custom_call" | custom-call | flops 1000000 | bytes 1000000 | tf_op jit(solution)/shard_map/pallas_call | solution.py:37
Async XLA Ops:
  2.0 1.6 %collective-permute-start = (bf16[784,128]{1,0:T(8,128)(2,1)S(1)}, bf16[784,128]{1,0:T(8,128)(2,1)S(1)}, u32[]{:S(2)}, u32[]{:S(2)}) collective-permute-start(bf16[784,128]{1,0:T(8,128)(2,1)S(1)} %get-tuple-element.58.refs_0_), channel_id=1, source_target_pairs={{0,1},{1,0},{2,3},{3,2},{4,5},{5,4},{6,7},{7,6},{8,9},{9,8},{10,11... | collective-permute-start | bytes 602120 | tf_op jit(solution)/shard_map/ppermute | solution.py:593
  6.1 6.1 %collective-permute-start.1 = (bf16[392,128]{1,0:T(8,128)(2,1)S(1)}, bf16[392,128]{1,0:T(8,128)(2,1)S(1)}, u32[]{:S(2)}, u32[]{:S(2)}) collective-permute-start(bf16[392,128]{1,0:T(8,128)(2,1)S(1)} %get-tuple-element.71), channel_id=1, source_target_pairs={{0,2},{2,0},{4,6},{6,4},{8,10},{10,8},{12,14},{14,12},{16,18},{18,... | collective-permute-start | bytes 301064 | tf_op jit(solution)/shard_map/ppermute | solution.py:546
  9.0 5.8 %collective-permute-start.2 = (bf16[392,128]{1,0:T(8,128)(2,1)S(1)}, bf16[392,128]{1,0:T(8,128)(2,1)S(1)}, u32[]{:S(2)}, u32[]{:S(2)}) collective-permute-start(bf16[392,128]{1,0:T(8,128)(2,1)S(1)} %get-tuple-element.72), channel_id=1, source_target_pairs={{0,4},{2,6},{4,0},{6,2},{8,12},{10,14},{12,8},{14,10},{16,20},{18,... | collective-permute-start | bytes 301064 | tf_op jit(solution)/shard_map/ppermute | solution.py:546
  10.5 5.5 %collective-permute-start.3 = (bf16[392,128]{1,0:T(8,128)(2,1)S(1)}, bf16[392,128]{1,0:T(8,128)(2,1)S(1)}, u32[]{:S(2)}, u32[]{:S(2)}) collective-permute-start(bf16[392,128]{1,0:T(8,128)(2,1)S(1)} %get-tuple-element.73), channel_id=1, source_target_pairs={{0,6},{2,4},{4,2},{6,0},{8,14},{10,12},{12,10},{14,8},{16,22},{18,... | collective-permute-start | bytes 301064 | tf_op jit(solution)/shard_map/ppermute | solution.py:546
  16.4 7.0 %collective-permute-start.4 = (bf16[392,128]{1,0:T(8,128)(2,1)S(1)}, bf16[392,128]{1,0:T(8,128)(2,1)S(1)}, u32[]{:S(2)}, u32[]{:S(2)}) collective-permute-start(bf16[392,128]{1,0:T(8,128)(2,1)S(1)} %shard_map.141.refs_4_), channel_id=1, source_target_pairs={{0,8},{2,10},{4,12},{6,14},{8,0},{10,2},{12,4},{14,6},{16,24},{18,... | collective-permute-start | bytes 301064 | tf_op jit(solution)/shard_map/ppermute | solution.py:546
  18.0 9.2 %collective-permute-start.5 = (bf16[392,128]{1,0:T(8,128)(2,1)S(1)}, bf16[392,128]{1,0:T(8,128)(2,1)S(1)}, u32[]{:S(2)}, u32[]{:S(2)}) collective-permute-start(bf16[392,128]{1,0:T(8,128)(2,1)S(1)} %shard_map.141.refs_4_), channel_id=1, source_target_pairs={{0,16},{2,18},{4,20},{6,22},{8,24},{10,26},{12,28},{14,30},{16,0},... | collective-permute-start | bytes 301064 | tf_op jit(solution)/shard_map/ppermute | solution.py:546
  20.6 6.6 %collective-permute-start.6 = (bf16[392,128]{1,0:T(8,128)(2,1)S(1)}, bf16[392,128]{1,0:T(8,128)(2,1)S(1)}, u32[]{:S(2)}, u32[]{:S(2)}) collective-permute-start(bf16[392,128]{1,0:T(8,128)(2,1)S(1)} %shard_map.141.refs_4_), channel_id=1, source_target_pairs={{0,24},{2,26},{4,28},{6,30},{8,16},{10,18},{12,20},{14,22},{16,8},... | collective-permute-start | bytes 301064 | tf_op jit(solution)/shard_map/ppermute | solution.py:546
  27.8 5.1 %collective-permute-start.9 = (bf16[392,128]{1,0:T(8,128)(2,1)S(1)}, bf16[392,128]{1,0:T(8,128)(2,1)S(1)}, u32[]{:S(2)}, u32[]{:S(2)}) collective-permute-start(bf16[392,128]{1,0:T(8,128)(2,1)S(1)} %get-tuple-element.91), channel_id=1, source_target_pairs={{0,2},{2,0},{4,6},{6,4},{8,10},{10,8},{12,14},{14,12},{16,18},{18,... | collective-permute-start | bytes 301064 | tf_op jit(solution)/shard_map/ppermute | solution.py:546
  29.7 4.8 %collective-permute-start.7 = (bf16[392,128]{1,0:T(8,128)(2,1)S(1)}, bf16[392,128]{1,0:T(8,128)(2,1)S(1)}, u32[]{:S(2)}, u32[]{:S(2)}) collective-permute-start(bf16[392,128]{1,0:T(8,128)(2,1)S(1)} %get-tuple-element.84), channel_id=1, source_target_pairs={{0,4},{2,6},{4,0},{6,2},{8,12},{10,14},{12,8},{14,10},{16,20},{18,... | collective-permute-start | bytes 301064 | tf_op jit(solution)/shard_map/ppermute | solution.py:546
  30.2 5.5 %collective-permute-start.8 = (bf16[392,128]{1,0:T(8,128)(2,1)S(1)}, bf16[392,128]{1,0:T(8,128)(2,1)S(1)}, u32[]{:S(2)}, u32[]{:S(2)}) collective-permute-start(bf16[392,128]{1,0:T(8,128)(2,1)S(1)} %get-tuple-element.85), channel_id=1, source_target_pairs={{0,6},{2,4},{4,2},{6,0},{8,14},{10,12},{12,10},{14,8},{16,22},{18,... | collective-permute-start | bytes 301064 | tf_op jit(solution)/shard_map/ppermute | solution.py:546
  38.5 1.8 %collective-permute-start.10 = (f32[784,128]{1,0:T(8,128)S(1)}, f32[784,128]{1,0:T(8,128)S(1)}, u32[]{:S(2)}, u32[]{:S(2)}) collective-permute-start(f32[784,128]{1,0:T(8,128)S(1)} %get-tuple-element.105), channel_id=1, source_target_pairs={{0,1},{1,0},{2,3},{3,2},{4,5},{5,4},{6,7},{7,6},{8,9},{9,8},{10,11... | collective-permute-start | bytes 1204232 | tf_op jit(solution)/shard_map/ppermute | solution.py:745

commit v6 on v5

--- a/solution.py
+++ b/solution.py
@@ -273,7 +273,8 @@
     forward_slots(slots, weights, enc_ref, geometry_ref, refs[4:], refs[:4])
 
 
-def forward_rest_body(in_ref, mid_ref, head_ref, vec_ref, enc_ref, geometry_ref, *refs, slots):
+def forward_rest_body(in_ref, mid_ref, head_ref, vec_ref, *refs, slots):
+    enc_ref, geometry_ref, *refs = refs[1:] if slots == (0,) else refs
     weights = (in_ref[...], mid_ref, head_ref, vec_ref[...])
     forward_slots(slots, weights, enc_ref, geometry_ref, refs[4:], refs[:4])
 
@@ -298,6 +299,13 @@
     return (parts, depth, direction, trans)
 
 
+def member_at(level, quad):
+    region = lax.axis_index("region")
+    if level == 0:
+        return lax.rem(region, quad)
+    return lax.rem(lax.div(region, quad << (level - 1)), 2)
+
+
 def as_columns(rows):
     columns = turned(jnp.concatenate(rows, 0), rows[0].shape[1])
     return [columns[:, i : i + 1] for i in range(len(rows))]
@@ -320,9 +328,10 @@
     return jnp.sum(total, 1, keepdims=True)
 
 
-def plane_body(*refs, rays):
+def combine_body(*refs, rays, level, quad):
     *messages, out_ref, store = refs
-    own = lax.rem(lax.axis_index("region"), len(messages))
+    messages = messages[: quad if level == 0 else 2]
+    own = member_at(level, quad)
     parts, depth, direction, trans = gather_messages(messages, store, own, rays)
     total = depth[0]
     for value in depth[1:]:
@@ -331,96 +340,111 @@
     out_ref[...] = as_message(weighted_sum(as_columns(trans), parts), rows)
 
 
-def owner_body(*refs, slots, planes):
-    quad_refs, plane_refs = (refs[:slots], refs[slots : slots + planes])
-    target_ref, _, *out_refs, quad_store, plane_store, reply = refs[slots + planes :]
+def owner_body(*refs, counts, quad):
+    levels = []
+    for count in counts:
+        messages, refs = (refs[:count], refs[count:])
+        levels.append(messages)
+    target_ref, _, *refs = refs
+    out_refs, stores, reply = (refs[:quad], refs[quad:-1], refs[-1])
     rays, feat = target_ref.shape
-    region = lax.axis_index("region")
-    own, own_plane = (lax.rem(region, slots), lax.div(region, slots))
-    parts, _, direction, trans = gather_messages(quad_refs, quad_store, own, rays)
-    plane_parts, _, _, plane_trans = gather_messages(plane_refs, plane_store, own_plane, rays)
-    rendered = weighted_sum(as_columns(plane_trans), plane_parts)
+    own = [member_at(n, quad) for n in range(len(counts))]
+    found = [
+        gather_messages(messages, stores[n], own[n], rays) for n, messages in enumerate(levels)
+    ]
+    direction = found[0][2]
+    parts, _, _, trans = found[-1]
+    rendered = weighted_sum(as_columns(trans), parts)
     grads = [
         (value - target_ref[:, cut].astype(f32)).astype(bf16).astype(f32)
         for value, cut in zip(rendered, blocks(feat))
     ]
     lane = lanes_of((rays, LANES))
     inners = jnp.zeros((rays, LANES), f32)
-    for i, value in enumerate((*plane_parts, *parts)):
+    for i, value in enumerate(sum((f[0] for f in found), [])):
         inners = jnp.where(lane == i, inner(grads, value), inners)
     inners = inners.T
 
-    def later(values):
-        below, above = sides(values)
-        return [jnp.where(direction < 0.5, a, b) for b, a in zip(below, above)]
-
-    plane_after = later([t * inners[z : z + 1] for z, t in enumerate(plane_trans)])
-    ahead = jnp.zeros((1, rays), f32)
+    def picked(values, place):
+        out = values[0]
+        for n, value in enumerate(values[1:]):
+            out = jnp.where(place == n + 1, value, out)
+        return out
+
+    ahead = jnp.ones((1, rays), f32)
     reach = jnp.zeros((1, rays), f32)
-    for z in range(planes):
-        ahead = jnp.where(own_plane == z, plane_trans[z], ahead)
-        reach = jnp.where(own_plane == z, plane_after[z], reach)
-    trans = [ahead * t for t in trans]
-    after = later([t * inners[planes + p : planes + p + 1] for p, t in enumerate(trans)])
-    for p in range(slots):
-        reply[p, :6, :rays] = jnp.concatenate([*split3(trans[p]), *split3(after[p] + reach)], 0)
+    for n in range(len(counts) - 1, -1, -1):
+        first = sum(counts[:n])
+        trans = [ahead * t for t in found[n][3]]
+        below, above = sides([t * inners[first + p : first + p + 1] for p, t in enumerate(trans)])
+        after = [reach + jnp.where(direction < 0.5, a, b) for b, a in zip(below, above)]
+        if n:
+            ahead, reach = (picked(trans, own[n]), picked(after, own[n]))
+    for p in range(quad):
+        reply[p, :6, :rays] = jnp.concatenate([*split3(trans[p]), *split3(after[p])], 0)
     for k, out_ref in enumerate(out_refs):
-        out_ref[...] = as_message(grads, reply[own ^ k, :6, :rays])
+        out_ref[...] = as_message(grads, reply[own[0] ^ k, :6, :rays])
 
 
 def with_ones(value):
     return jnp.concatenate([value.T, jnp.ones((16, value.shape[0]), bf16)], 0)
 
 
-def ready_body(*refs):
-    *refs, sems = refs
+def ready_shared_body(*refs):
     states, (enc_ref, mid_ref, head_ref, *refs) = (refs[:4], refs[4:])
-    count = (len(refs) - 7) // 7
-    sources = [refs[4 * n : 4 * n + 4] for n in range(count)]
-    fetched, refs = (refs[4 * count : 4 * count + 4], refs[4 * count + 4 :])
-    enc_turned, mid_turned, head_turned, *refs = refs
-    results = [refs[3 * n : 3 * n + 3] for n in range(count)]
+    source, fetched, refs = (refs[:4], refs[4:8], refs[8:])
+    enc_turned, mid_turned, head_turned, *results, sems = refs
     copies = []
-    for n, (source, place) in enumerate(zip(states, fetched)):
-        copies.append(pltpu.make_async_copy(source, place, sems.at[n]))
+    for n, (ref, place) in enumerate(zip(states, fetched)):
+        copies.append(pltpu.make_async_copy(ref, place, sems.at[n]))
         copies[-1].start()
+    feat = source[2].shape[2]
     mid_turned[...] = mid_ref[...].T
-    feat = sources[0][2].shape[2]
     head = head_ref[...].astype(f32)
     lane = lanes_of(head.shape)
     head_turned[...] = jnp.where(lane < feat, 2.0 * head, head).astype(bf16).T
     for k in range(enc_ref.shape[0]):
         enc_turned[k] = with_ones(enc_ref[k])
-    for source, outs in zip(sources, results):
-        one_ref, two_ref, turn_ref, scalar_ref = source
-        one_turned, two_turned, slope_ref = outs
-        samples, ray_count = scalar_ref.shape[2:]
-        for i in range(one_ref.shape[0]):
-            one_turned[i] = with_ones(one_ref[i])
-            two_turned[i] = with_ones(two_ref[i])
-            columns = turned(0.25 * scalar_ref[i, 0], ray_count)
-            for j in range(samples):
-                rows = slice(ray_count * j, ray_count * (j + 1))
-                turn = turn_ref[i, rows, :]
-                slope_ref[i, rows, :] = columns[:, j : j + 1] * (1.0 - turn * turn)
+    ready_slots(source, results)
     for copy in copies:
         copy.wait()
 
 
-def backward_body(*refs, slots, offset, before, last, group_count, shapes, vec_share, shards):
+def ready_body(*refs):
+    count = len(refs) // 7
+    for n in range(count):
+        ready_slots(refs[4 * n : 4 * n + 4], refs[4 * count + 3 * n : 4 * count + 3 * n + 3])
+
+
+def ready_slots(source, results):
+    one_ref, two_ref, turn_ref, scalar_ref = source
+    one_turned, two_turned, slope_ref = results
+    samples, ray_count = scalar_ref.shape[2:]
+    for i in range(one_ref.shape[0]):
+        one_turned[i] = with_ones(one_ref[i])
+        two_turned[i] = with_ones(two_ref[i])
+        columns = turned(0.25 * scalar_ref[i, 0], ray_count)
+        for j in range(samples):
+            rows = slice(ray_count * j, ray_count * (j + 1))
+            turn = turn_ref[i, rows, :]
+            slope_ref[i, rows, :] = columns[:, j : j + 1] * (1.0 - turn * turn)
+
+
+def backward_body(*refs, slots, places, sources, before, last, group_count, shapes, vec_share, shards):
     begun = not before
     messages, refs = (refs[: len(slots)], refs[len(slots) :])
-    one_ref, two_ref, turn_ref, scalar_ref, *refs = refs
-    one_turned, two_turned, slope_ref, enc_turned, mid_turned, head_turned, *refs = refs
+    held = [[ref.at[at] for ref in refs[7 * n : 7 * n + 7]] for n, at in places]
+    refs = refs[7 * sources :]
+    enc_turned, mid_turned, head_turned, *refs = refs
     if not begun:
         earlier, refs = (refs[:3], refs[3:])
     if last:
-        depths, (depth_ref, *outs, shares) = (refs[: len(before)], refs[len(before) :])
+        depths, (depth_ref, *outs) = (refs[: len(before)], refs[len(before) :])
     else:
         *outs, depth_ref = refs
-    samples, ray_count = scalar_ref.shape[2:]
-    hidden = one_ref.shape[2]
-    feat = turn_ref.shape[2]
+    samples, ray_count = held[0][3].shape[1:]
+    hidden = held[0][0].shape[1]
+    feat = held[0][2].shape[1]
     lane = lanes_of((ray_count, LANES))
     if last:
         for ref, group in zip(depths, before):
@@ -437,7 +461,7 @@
         spread = jnp.where(lane == samples, grad_sum, 0.0)
         for j in range(samples):
             rows = slice(ray_count * j, ray_count * (j + 1))
-            value = jnp.sum(turn_ref[offset + i, rows, :] * grad, 1, keepdims=True)
+            value = jnp.sum(held[i][2][rows, :] * grad, 1, keepdims=True)
             spread = jnp.where(lane == j, value, spread)
         spreads.append(spread.T)
     extra = side_by_side(extras)
@@ -452,7 +476,7 @@
     spread = side_by_side(spreads)
     sample_grad = 0.5 * (spread[:samples] + spread[samples : samples + 1])
     local_weight, trans_after, slope = [
-        side_by_side([scalar_ref[offset + i, q] for i in range(len(slots))]) for q in range(3)
+        side_by_side([refs_of[3][q] for refs_of in held]) for q in range(3)
     ]
     weighted = local_weight * sample_grad
     later = [jnp.zeros_like(after)]
@@ -463,21 +487,22 @@
     columns = turned(jnp.concatenate([optical_grad * slope, trans], 0), after.shape[1])
     zero = jnp.zeros((), bf16)
     for i, k in enumerate(slots):
+        one_ref, two_ref, _, _, one_turned, two_turned, slope_ref = held[i]
         own = columns[ray_count * i : ray_count * (i + 1)]
         grad_ahead = grads[i] * own[:, samples : samples + 1]
         pieces = []
         for j in range(samples):
             rows = slice(ray_count * j, ray_count * (j + 1))
-            colour_grad = (grad_ahead * slope_ref[offset + i, rows, :]).astype(bf16)
+            colour_grad = (grad_ahead * slope_ref[rows, :]).astype(bf16)
             density_part = jnp.where(lane == j, own, 0.0).astype(bf16)
             pieces.append(jnp.concatenate([colour_grad, density_part], 1))
         head_grad = jnp.concatenate(pieces, 0)
         second = product(head_grad, head_turned[...]).astype(bf16)
-        sums[2] = sums[2] + product(two_turned[offset + i], head_grad)
-        second = jnp.where(two_ref[offset + i] > 0, second, zero)
+        sums[2] = sums[2] + product(two_turned[...], head_grad)
+        second = jnp.where(two_ref[...] > 0, second, zero)
         first = product(second, mid_turned[...]).astype(bf16)
-        sums[1] = sums[1] + product(one_turned[offset + i], second)
-        first = jnp.where(one_ref[offset + i] > 0, first, zero)
+        sums[1] = sums[1] + product(one_turned[...], second)
+        first = jnp.where(one_ref[...] > 0, first, zero)
         sums[0] = sums[0] + product(enc_turned[k], first)
     if not last:
         for value, ref in zip(sums, outs):
@@ -487,22 +512,28 @@
     first_sum, second_sum, head_sum = [value[-16:-15] for value in sums]
     density_sum = jnp.sum(values[2][:, feat:].T, 0, keepdims=True)
     vec = jnp.concatenate([first_sum, second_sum, density_sum, head_sum[:, :feat]], 1)
-    mine = lax.axis_index("rays")
     total = vec.shape[1]
-    for s in range(shards):
-        place = lax.rem(s + shards - mine, shards) if shards == 2 else s
+
+    def write(s, ref):
         spot = 0
         for (rows, width), value in zip(shapes, values):
             for cut in blocks(width):
-                shares[place, spot : spot + rows, :] = value[rows * s : rows * (s + 1), cut]
+                ref[spot : spot + rows, :] = value[rows * s : rows * (s + 1), cut]
                 spot += rows
         row = pltpu.roll(vec, total - vec_share * s, 1) if s else vec
-        shares[place, spot : spot + 16, :] = row_block(row[:, : wide_rows(vec_share) * LANES], 16)
-    if shards == 2:
-        outs[0][...] = shares[0]
-        outs[1][...] = shares[1]
-    else:
-        outs[0][...] = shares[...]
+        ref[spot : spot + 16, :] = row_block(row[:, : wide_rows(vec_share) * LANES], 16)
+
+    if shards != 2:
+        for s in range(shards):
+            write(s, outs[0].at[s])
+        return
+    mine = lax.axis_index("rays")
+    for s in range(2):
+
+        @pl.when(mine == s)
+        def _():
+            write(s, outs[0])
+            write(1 - s, outs[1])
 
 
 def adam_body(*refs, shards):
@@ -648,23 +679,16 @@
         found, out = (out[:4], out[4:]) if first else (None, out)
         return (out[:4], list(out[4:]), found)
 
-    groups = [tuple(range(1, quad)), (0,)]
+    groups = [(quad - 1,), tuple(range(1, quad - 1)), (0,)]
     kept, sent, weights = ([], {}, None)
     for slots in groups:
-        arrays, messages, found = forward(slots, packs if not kept else weights, not kept)
+        inputs = packs if not kept else (*weights, sent[quad - 1]) if slots == (0,) else weights
+        arrays, messages, found = forward(slots, inputs, not kept)
         weights = weights or found
         kept.append(arrays)
         for k, value in zip(slots, messages):
             sent[k] = swap(value, k, regions) if k else value
     quad_messages = [in_vmem(sent[k]) for k in range(quad)]
-    store = pltpu.VMEM((quad, *message.shape), bf16)
-    plane_store = pltpu.VMEM((planes, *message.shape), bf16)
-    plane_message = call(
-        functools.partial(plane_body, rays=rays), message, quad_messages, 16, scratch=[store]
-    )
-    plane_messages = [plane_message] + [
-        swap(plane_message, quad * k, regions) for k in range(1, planes)
-    ]
     def ready_shapes(count):
         return (
             pltpu.VMEM((count, hidden + 16, rows), bf16),
@@ -673,32 +697,53 @@
         )
 
     hbm, vmem = (pl.BlockSpec(memory_space=m) for m in (pltpu.HBM, pltpu.VMEM))
-    local = [encoded, weights[1], weights[2], *sum(map(list, kept), [])]
+    local = [encoded, weights[1], weights[2], *kept[0]]
     results = call(
-        ready_body,
+        ready_shared_body,
         tuple(pltpu.VMEM(s.shape, f32) for s in states)
         + (
             pltpu.VMEM((quad, code_width + 16, rows), bf16),
             pltpu.VMEM((hidden, hidden), bf16),
             pltpu.VMEM((feat + LANES, hidden), bf16),
         )
-        + sum((ready_shapes(len(slots)) for slots in groups), ()),
+        + ready_shapes(len(groups[0])),
         [in_hbm(s) for s in states] + [in_vmem(v) for v in local],
         16,
         scratch=[pltpu.SemaphoreType.DMA((4,))],
         specs=[hbm] * 4 + [vmem] * len(local),
-        flops=quad * flops,
-        moved=2 * moved(quad),
+        flops=flops,
+        moved=2 * moved(1),
     )
     states_near, enc_turned, turned_weights = (results[:4], results[4], results[5:7])
-    results = results[7:]
-    ready = [results[3 * n : 3 * n + 3] for n in range(len(groups))]
+    ready = [results[7:]]
+    results = call(
+        ready_body,
+        sum((ready_shapes(len(slots)) for slots in groups[1:]), ()),
+        [in_vmem(v) for v in sum(map(list, kept[1:]), [])],
+        16,
+        flops=(quad - 1) * flops,
+        moved=2 * moved(quad - 1),
+    )
+    ready += [results[3 * n : 3 * n + 3] for n in range(len(groups) - 1)]
+    ahead = {1: [in_vmem(turned_weights[0])]}
+    levels = [quad_messages]
+    for level in range(planes.bit_length() - 1):
+        composite = call(
+            functools.partial(combine_body, rays=rays, level=level, quad=quad),
+            message,
+            levels[-1] + ahead.get(level, []),
+            16,
+            scratch=[pltpu.VMEM((len(levels[-1]), *message.shape), bf16)],
+        )
+        levels.append([in_vmem(composite), in_vmem(swap(composite, quad << level, regions))])
+    counts = tuple(len(level) for level in levels)
     replies = call(
-        functools.partial(owner_body, slots=quad, planes=planes),
+        functools.partial(owner_body, counts=counts, quad=quad),
         (message,) * quad,
-        quad_messages + [in_vmem(v) for v in (*plane_messages, own_target, turned_weights[0])],
+        sum(levels, []) + [in_vmem(v) for v in (own_target, results[0])],
         16,
-        scratch=[store, plane_store, pltpu.VMEM((quad, 8, LANES), f32)],
+        scratch=[pltpu.VMEM((count, *message.shape), bf16) for count in counts]
+        + [pltpu.VMEM((quad, 8, LANES), f32)],
     )
     answers = [replies[0]] + [swap(replies[k], k, regions) for k in range(1, quad)]
     gradient_shapes = (
@@ -707,9 +752,10 @@
         pltpu.VMEM((hidden + 16, feat + LANES), f32),
     )
     earlier, depths, before = ((), [], ())
-    steps = [(1, (0,), 0), (0, (1,), 0), (0, tuple(range(2, quad)), 1)]
-    for n, slots, offset in steps:
-        last = slots == steps[-1][1]
+    place = {k: (n, slots.index(k)) for n, slots in enumerate(groups) for k in slots}
+    steps = [(0,), (1,), tuple(range(2, quad))]
+    for slots in steps:
+        last = slots == steps[-1]
         if last:
             share = pltpu.VMEM((pack_rows, LANES), f32)
             out_shape = (pltpu.VMEM((1, ray_count), f32), share, share)
@@ -717,13 +763,16 @@
                 out_shape = (out_shape[0], shaped((shards, pack_rows, LANES), f32))
         else:
             out_shape = gradient_shapes + (pltpu.VMEM((len(slots), rays), f32),)
-        inputs = [answers[k] for k in slots] + [*kept[n], *ready[n], enc_turned, *turned_weights]
-        inputs += [*earlier] + (depths if last else [])
+        used = sorted({place[k][0] for k in slots})
+        inputs = [answers[k] for k in slots]
+        inputs += sum(([*kept[n], *ready[n]] for n in used), [])
+        inputs += [enc_turned, *turned_weights, *earlier] + (depths if last else [])
         out = call(
             functools.partial(
                 backward_body,
                 slots=slots,
-                offset=offset,
+                places=tuple((used.index(place[k][0]), place[k][1]) for k in slots),
+                sources=len(used),
                 before=before,
                 last=last,
                 group_count=quad,
@@ -733,7 +782,6 @@
             out_shape,
             [in_vmem(v) for v in inputs],
             24,
-            scratch=[pltpu.VMEM((shards, pack_rows, LANES), f32)] if last else (),
             flops=2 * len(slots) * flops,
             moved=moved(len(slots)),
         )

time: 41.6 us -> 40.5 us (0.974)
  waiting for transfers between devices: 11.4 us -> 8.75 us
  Pallas kernels: 16.3 us -> 17.9 us
    ppermute x9 -> x8, waiting for transfers between devices: 9.41 us -> 6.79 us  [swap(): lax.ppermute(value, 'region', [(i, i ^ distance) for i in range(size)])]
    pallas_call x11 -> x14, Pallas kernels: 16.3 us -> 17.9 us  [call(): pl.pallas_call(body, out_shape=out_shape, in_specs=specs or [spec] * len(...]
    ppermute x9 -> x8, starting transfers between devices: 12.5 us -> 12.4 us  [swap(): lax.ppermute(value, 'region', [(i, i ^ distance) for i in range(size)])]
  transfers between devices with their start and end apart: 11 -> 10, of which waited for: 7 -> 8; matrix products, arithmetic and copies ran while one was open for 0% -> 0% of each run, Pallas kernels for 18% -> 26%
where the time goes in v6:
time: 40.5 us; the launch traced here: 40.3 us
  Pallas kernels  17.9 us (44%)
  starting transfers between devices  12.9 us (32%)
  waiting for transfers between devices  8.75 us (22%)
  between operations  0.73 us (2%)
    pallas_call x14, Pallas kernels, call(): pl.pallas_call(body, out_shape=out_shape, in_specs=specs or [spec] * len(...  17.9 us
    ppermute x8, starting transfers between devices, swap(): lax.ppermute(value, 'region', [(i, i ^ distance) for i in range(size)])  12.4 us
    ppermute x8, waiting for transfers between devices, swap(): lax.ppermute(value, 'region', [(i, i ^ distance) for i in range(size)])  6.79 us
    ppermute x1, waiting for transfers between devices, per_device(): parts = (grads[0], lax.ppermute(grads[1], 'rays', [(0, 1), (1, 0)]))  1.72 us
  transfers between devices with their start and end apart: 10, of which 8 were waited for; matrix products, arithmetic and copies ran while one was open for 0% of the time, Pallas kernels for 26%

profile of v6, /device:TPU:0, one launch (start us, length us, event | category | flops | bytes accessed | tf_op | source)
XLA Modules:
  0.0 40.3 jit_solution(2153193113344328214)
XLA Ops:
  0.6 1.3 %shard_map.137 = (bf16[784,128]{1,0:T(8,128)(2,1)S(1)}, bf16[2,512,128]{2,1,0:T(8,128)(2,1)S(1)}, s32[1,8,512]{2,1,0:T(8,128)S(1)}, s32[1,512]{1,0:T(1,128)S(1)}...) custom-call(f32[3,1,64,256]{3,2,1,0:T(8,128)} %refs_0_.3, f32[3,1,128,256]{3,2,1,0:T(8,128)} %refs_1_.3, ...), custom_call_target="tpu_custom_call" | custom-call | flops 1000000 | bytes 1000000 | tf_op jit(solution)/shard_map/pallas_call | solution.py:37
  2.0 0.5 %collective-permute-start = (bf16[784,128]{1,0:T(8,128)(2,1)S(1)}, bf16[784,128]{1,0:T(8,128)(2,1)S(1)}, u32[]{:S(2)}, u32[]{:S(2)}) collective-permute-start(bf16[784,128]{1,0:T(8,128)(2,1)S(1)} %get-tuple-element.65.refs_0_), channel_id=1, source_target_pairs={{0,1},{1,0},{2,3},{3,2},{4,5},{5,4},{6,7},{7,6},{8,9},{9,8},{10,11... | collective-permute-start | bytes 602120 | tf_op jit(solution)/shard_map/ppermute | solution.py:624
  2.5 0.8 %shard_map.138 = (bf16[4,1024,128]{2,1,0:T(8,128)(2,1)S(1)}, f32[4,16,128]{2,1,0:T(8,128)S(1)}) custom-call(bf16[2,512,128]{2,1,0:T(8,128)(2,1)S(1)} %get-tuple-element.66.refs_0_, s32[1,8,512]{2,1,0:T(8,128)S(1)} %get-tuple-element.67.refs_1_, s32[1,512]{1,0:T(1,128)S(1)} %get-tuple-element.68.refs_2_, s32[1,512]{1,0:T(1,128)S(1)} %get-tuple-element.69.refs_3_, ...), custom_call_target="tpu_custom_call" | custom-call | flops 5242880 | bytes 2097152 | tf_op jit(solution)/shard_map/pallas_call | solution.py:37
  3.3 0.2 collective-permute-done.refs_1_
  3.6 1.2 %shard_map.139 = (bf16[128,256]{1,0:T(8,128)(2,1)S(1)}, bf16[256,256]{1,0:T(8,128)(2,1)S(1)}, bf16[256,512]{1,0:T(8,128)(2,1)S(1)}, f32[1,1152]{1,0:T(1,128)S(1)...) custom-call(bf16[784,128]{1,0:T(8,128)(2,1)S(1)} %get-tuple-element., ...), custom_call_target="tpu_custom_call" | custom-call | flops 469762048 | bytes 2621440 | tf_op jit(solution)/shard_map/pallas_call | solution.py:37
  4.8 3.9 %collective-permute-start.1 = (bf16[392,128]{1,0:T(8,128)(2,1)S(1)}, bf16[392,128]{1,0:T(8,128)(2,1)S(1)}, u32[]{:S(2)}, u32[]{:S(2)}) collective-permute-start(bf16[392,128]{1,0:T(8,128)(2,1)S(1)} %get-tuple-element.77), channel_id=1, source_target_pairs={{0,6},{2,4},{4,2},{6,0},{8,14},{10,12},{12,10},{14,8},{16,22},{18,... | collective-permute-start | bytes 301064 | tf_op jit(solution)/shard_map/ppermute | solution.py:577
  8.7 1.7 %shard_map.141 = (bf16[2,1024,256]{2,1,0:T(8,128)(2,1)S(1)}, bf16[2,1024,256]{2,1,0:T(8,128)(2,1)S(1)}, f32[2,1024,384]{2,1,0:T(8,128)S(1)}, f32[2,3,8,128]{3,2,...) custom-call(bf16[128,256]{1,0:T(8,128)(2,1)S(1)} %get-tuple-element.73.in_ref, ...), custom_call_target="tpu_custom_call" | custom-call | flops 939524096 | bytes 5242880 | tf_op jit(solution)/shard_map/pallas_call | solution.py:37
  10.4 0.6 %collective-permute-start.2 = (bf16[392,128]{1,0:T(8,128)(2,1)S(1)}, bf16[392,128]{1,0:T(8,128)(2,1)S(1)}, u32[]{:S(2)}, u32[]{:S(2)}) collective-permute-start(bf16[392,128]{1,0:T(8,128)(2,1)S(1)} %get-tuple-element.79), channel_id=1, source_target_pairs={{0,2},{2,0},{4,6},{6,4},{8,10},{10,8},{12,14},{14,12},{16,18},{18,... | collective-permute-start | bytes 301064 | tf_op jit(solution)/shard_map/ppermute | solution.py:577
  11.0 0.0 collective-permute-start.3
  11.0 0.8 %collective-permute-done.1.refs_0_.refs_3_ = bf16[392,128]{1,0:T(8,128)(2,1)S(1)} collective-permute-done((bf16[392,128]{1,0:T(8,128)(2,1)S(1)}, bf16[392,128]{1,0:T(8,128)(2,1)S(1)}, u32[]{:S(2)}, u32[]{:S(2)}) %collective-permute-start.1) | collective-permute-done | bytes 100384 | tf_op jit(solution)/shard_map/ppermute | solution.py:577
  11.8 1.1 %shard_map.140 = (bf16[1,1024,256]{2,1,0:T(8,128)(2,1)S(1)}, bf16[1,1024,256]{2,1,0:T(8,128)(2,1)S(1)}, f32[1,1024,384]{2,1,0:T(8,128)S(1)}, f32[1,3,8,128]{3,2,1,0:T(8,128)S(1)}, bf16[392,128]{1,0:T(8,128)(2,1)S(1)}) custom-call(bf16[128,256]{1,0:T(8,128)(2,1)S(1)} %get-tuple-element.73.in_ref, bf16[256,256]{1,0:T(8,128)(2,1)S(1)} %get-tuple-element.74.mid_ref.refs_5_, ...), custom_call_target="tpu_custom_call" | custom-call | flops 469762048 | bytes 2621440 | tf_op jit(solution)/shard_map/pallas_call | solution.py:37
  12.9 2.1 %collective-permute-done.2.refs_1_ = bf16[392,128]{1,0:T(8,128)(2,1)S(1)} collective-permute-done((bf16[392,128]{1,0:T(8,128)(2,1)S(1)}, bf16[392,128]{1,0:T(8,128)(2,1)S(1)}, u32[]{:S(2)}, u32[]{:S(2)}) %collective-permute-start.2) | collective-permute-done | bytes 100384 | tf_op jit(solution)/shard_map/ppermute | solution.py:577
  15.1 0.5 %collective-permute-done.3.refs_2_ = bf16[392,128]{1,0:T(8,128)(2,1)S(1)} collective-permute-done((bf16[392,128]{1,0:T(8,128)(2,1)S(1)}, bf16[392,128]{1,0:T(8,128)(2,1)S(1)}, u32[]{:S(2)}, u32[]{:S(2)}) %collective-permute-start.3) | collective-permute-done | bytes 100384 | tf_op jit(solution)/shard_map/ppermute | solution.py:577
  15.6 0.3 shard_map.142.refs_0_.refs_4_
  15.9 1.6 %collective-permute-start.4 = (bf16[392,128]{1,0:T(8,128)(2,1)S(1)}, bf16[392,128]{1,0:T(8,128)(2,1)S(1)}, u32[]{:S(2)}, u32[]{:S(2)}) collective-permute-start(bf16[392,128]{1,0:T(8,128)(2,1)S(1)} %shard_map.142.refs_0_.refs_4_), channel_id=1, source_target_pairs={{0,8},{2,10},{4,12},{6,14},{8,0},{10,2},{12,4},{14,6},{16,24},{18,... | collective-permute-start | bytes 301064 | tf_op jit(solution)/shard_map/ppermute | solution.py:577
  17.6 2.0 %shard_map.143 = (f32[3,1,64,256]{3,2,1,0:T(8,128)S(1)}, f32[3,1,128,256]{3,2,1,0:T(8,128)S(1)}, f32[3,1,128,384]{3,2,1,0:T(8,128)S(1)}, f32[3,1,576]{2,1,0:T(1,...) custom-call(f32[3,1,64,256]{3,2,1,0:T(8,128)} %refs_0_.3, ...), custom_call_target="tpu_custom_call" | custom-call | flops 469762048 | bytes 5242880 | tf_op jit(solution)/shard_map/pallas_call | solution.py:37
  19.5 1.1 %collective-permute-done.4.refs_1_.refs_5_ = bf16[392,128]{1,0:T(8,128)(2,1)S(1)} collective-permute-done((bf16[392,128]{1,0:T(8,128)(2,1)S(1)}, bf16[392,128]{1,0:T(8,128)(2,1)S(1)}, u32[]{:S(2)}, u32[]{:S(2)}) %collective-permute-start.4) | collective-permute-done | bytes 100384 | tf_op jit(solution)/shard_map/ppermute | solution.py:577
  20.6 0.3 shard_map.144.refs_6_
  20.9 2.7 %collective-permute-start.5 = (bf16[392,128]{1,0:T(8,128)(2,1)S(1)}, bf16[392,128]{1,0:T(8,128)(2,1)S(1)}, u32[]{:S(2)}, u32[]{:S(2)}) collective-permute-start(bf16[392,128]{1,0:T(8,128)(2,1)S(1)} %shard_map.144.refs_6_), channel_id=1, source_target_pairs={{0,16},{2,18},{4,20},{6,22},{8,24},{10,26},{12,28},{14,30},{16,0},... | collective-permute-start | bytes 301064 | tf_op jit(solution)/shard_map/ppermute | solution.py:577
  23.6 1.6 %shard_map.145 = (bf16[2,272,1024]{2,1,0:T(8,128)(2,1)S(1)}, bf16[2,272,1024]{2,1,0:T(8,128)(2,1)S(1)}, f32[2,1024,384]{2,1,0:T(8,128)S(1)}, bf16[1,272,1024]{2,...) custom-call(bf16[2,1024,256]{2,1,0:T(8,128)(2,1)S(1)} %get-tuple-element.87.refs_0_.refs_1_.refs_9_, ...), custom_call_target="tpu_custom_call" | custom-call | flops 1409286144 | bytes 15728640 | tf_op jit(solution)/shard_map/pallas_call | solution.py:37
  25.2 1.3 %collective-permute-done.5.refs_7_ = bf16[392,128]{1,0:T(8,128)(2,1)S(1)} collective-permute-done((bf16[392,128]{1,0:T(8,128)(2,1)S(1)}, bf16[392,128]{1,0:T(8,128)(2,1)S(1)}, u32[]{:S(2)}, u32[]{:S(2)}) %collective-permute-start.5) | collective-permute-done | bytes 100384 | tf_op jit(solution)/shard_map/ppermute | solution.py:577
  26.5 0.5 %shard_map.146 = (bf16[392,128]{1,0:T(8,128)(2,1)S(1)}, bf16[392,128]{1,0:T(8,128)(2,1)S(1)}, bf16[392,128]{1,0:T(8,128)(2,1)S(1)}, bf16[392,128]{1,0:T(8,128)(2,1)S(1)}) custom-call(bf16[392,128]{1,0:T(8,128)(2,1)S(1)} %get-tuple-element.78.refs_0_, bf16[392,128]{1,0:T(8,128)(2,1)S(1)} %collective-permute-done.2.refs_1_, ...), custom_call_target="tpu_custom_call" | custom-call | flops 1000000 | bytes 1000000 | tf_op jit(solution)/shard_map/pallas_call | solution.py:37
  27.0 1.6 %collective-permute-start.8 = (bf16[392,128]{1,0:T(8,128)(2,1)S(1)}, bf16[392,128]{1,0:T(8,128)(2,1)S(1)}, u32[]{:S(2)}, u32[]{:S(2)}) collective-permute-start(bf16[392,128]{1,0:T(8,128)(2,1)S(1)} %get-tuple-element.105), channel_id=1, source_target_pairs={{0,2},{2,0},{4,6},{6,4},{8,10},{10,8},{12,14},{14,12},{16,18},{18,... | collective-permute-start | bytes 301064 | tf_op jit(solution)/shard_map/ppermute | solution.py:577
  28.6 0.5 %collective-permute-start.6 = (bf16[392,128]{1,0:T(8,128)(2,1)S(1)}, bf16[392,128]{1,0:T(8,128)(2,1)S(1)}, u32[]{:S(2)}, u32[]{:S(2)}) collective-permute-start(bf16[392,128]{1,0:T(8,128)(2,1)S(1)} %get-tuple-element.96), channel_id=1, source_target_pairs={{0,4},{2,6},{4,0},{6,2},{8,12},{10,14},{12,8},{14,10},{16,20},{18,... | collective-permute-start | bytes 301064 | tf_op jit(solution)/shard_map/ppermute | solution.py:577
  29.1 1.5 %collective-permute-start.7 = (bf16[392,128]{1,0:T(8,128)(2,1)S(1)}, bf16[392,128]{1,0:T(8,128)(2,1)S(1)}, u32[]{:S(2)}, u32[]{:S(2)}) collective-permute-start(bf16[392,128]{1,0:T(8,128)(2,1)S(1)} %get-tuple-element.97), channel_id=1, source_target_pairs={{0,6},{2,4},{4,2},{6,0},{8,14},{10,12},{12,10},{14,8},{16,22},{18,... | collective-permute-start | bytes 301064 | tf_op jit(solution)/shard_map/ppermute | solution.py:577
  30.6 1.5 %shard_map.147 = (f32[144,256]{1,0:T(8,128)S(1)}, f32[272,256]{1,0:T(8,128)S(1)}, f32[272,512]{1,0:T(8,128)S(1)}, f32[1,128]{1,0:T(1,128)S(1)}) custom-call(bf16[392,128]{1,0:T(8,128)(2,1)S(1)} %get-tuple-element.106.refs_0_, bf16[1,1024,256]{2,1,0:T(8,128)(2,1)S(1)} %get-tuple-element.91.refs_4_.refs_1_, ...), custom_call_target="tpu_custom_call" | custom-call | flops 939524096 | bytes 2621440 | tf_op jit(solution)/shard_map/pallas_call | solution.py:37
  32.1 0.0 collective-permute-done.8.refs_0_
  32.1 1.6 %shard_map.148 = (f32[144,256]{1,0:T(8,128)S(1)}, f32[272,256]{1,0:T(8,128)S(1)}, f32[272,512]{1,0:T(8,128)S(1)}, f32[1,128]{1,0:T(1,128)S(1)}) custom-call(bf16[392,128]{1,0:T(8,128)(2,1)S(1)} %collective-permute-done.8.refs_0_, bf16[2,1024,256]{2,1,0:T(8,128)(2,1)S(1)} %get-tuple-element.87.refs_0_.refs_1_.refs_9_, ...), custom_call_target="tpu_custom_call" | custom-call | flops 939524096 | bytes 2621440 | tf_op jit(solution)/shard_map/pallas_call | solution.py:37
  33.7 0.0 collective-permute-done.6.refs_0_
  33.7 0.9 %collective-permute-done.7.refs_1_ = bf16[392,128]{1,0:T(8,128)(2,1)S(1)} collective-permute-done((bf16[392,128]{1,0:T(8,128)(2,1)S(1)}, bf16[392,128]{1,0:T(8,128)(2,1)S(1)}, u32[]{:S(2)}, u32[]{:S(2)}) %collective-permute-start.7) | collective-permute-done | bytes 100384 | tf_op jit(solution)/shard_map/ppermute | solution.py:577
  34.6 2.7 %shard_map.149 = (f32[1,512]{1,0:T(1,128)S(1)}, f32[784,128]{1,0:T(8,128)S(1)}, f32[784,128]{1,0:T(8,128)S(1)}) custom-call(bf16[392,128]{1,0:T(8,128)(2,1)S(1)} %collective-permute-done.6.refs_0_, bf16[392,128]{1,0:T(8,128)(2,1)S(1)} %collective-permute-done.7.refs_1_, bf16[1,1024,256]{2,1,0:T(8,128)(2,1)S(1)} %get-tuple-element.81.refs_7_.refs_2_, ...), custom_call_target="tpu_custom_call" | custom-call | flops 1879048192 | bytes 5242880 | tf_op jit(solution)/shard_map/pallas_call | solution.py:37
  37.3 0.0 collective-permute-start.9
  37.4 1.7 %collective-permute-done.9.refs_1_ = f32[784,128]{1,0:T(8,128)S(1)} collective-permute-done((f32[784,128]{1,0:T(8,128)S(1)}, f32[784,128]{1,0:T(8,128)S(1)}, u32[]{:S(2)}, u32[]{:S(2)}) %collective-permute-start.9) | collective-permute-done | bytes 401440 | tf_op jit(solution)/shard_map/ppermute | solution.py:793
  39.1 1.2 %shard_map.150 = (f32[3,1,64,256]{3,2,1,0:T(8,128)}, f32[3,1,128,256]{3,2,1,0:T(8,128)}, f32[3,1,128,384]{3,2,1,0:T(8,128)}, f32[3,1,576]{2,1,0:T(1,128)}, f32[1,512]{1,0:T(1,128)}) custom-call(f32[784,128]{1,0:T(8,128)S(1)} %get-tuple-element.118.refs_0_, f32[784,128]{1,0:T(8,128)S(1)} %collective-permute-done.9.refs_1_, ...), custom_call_target="tpu_custom_call" | custom-call | flops 1000000 | bytes 1000000 | tf_op jit(solution)/shard_map/pallas_call | solution.py:37
Async XLA Ops:
  2.0 1.6 %collective-permute-start = (bf16[784,128]{1,0:T(8,128)(2,1)S(1)}, bf16[784,128]{1,0:T(8,128)(2,1)S(1)}, u32[]{:S(2)}, u32[]{:S(2)}) collective-permute-start(bf16[784,128]{1,0:T(8,128)(2,1)S(1)} %get-tuple-element.65.refs_0_), channel_id=1, source_target_pairs={{0,1},{1,0},{2,3},{3,2},{4,5},{5,4},{6,7},{7,6},{8,9},{9,8},{10,11... | collective-permute-start | bytes 602120 | tf_op jit(solution)/shard_map/ppermute | solution.py:624
  4.8 7.0 %collective-permute-start.1 = (bf16[392,128]{1,0:T(8,128)(2,1)S(1)}, bf16[392,128]{1,0:T(8,128)(2,1)S(1)}, u32[]{:S(2)}, u32[]{:S(2)}) collective-permute-start(bf16[392,128]{1,0:T(8,128)(2,1)S(1)} %get-tuple-element.77), channel_id=1, source_target_pairs={{0,6},{2,4},{4,2},{6,0},{8,14},{10,12},{12,10},{14,8},{16,22},{18,... | collective-permute-start | bytes 301064 | tf_op jit(solution)/shard_map/ppermute | solution.py:577
  10.4 4.7 %collective-permute-start.2 = (bf16[392,128]{1,0:T(8,128)(2,1)S(1)}, bf16[392,128]{1,0:T(8,128)(2,1)S(1)}, u32[]{:S(2)}, u32[]{:S(2)}) collective-permute-start(bf16[392,128]{1,0:T(8,128)(2,1)S(1)} %get-tuple-element.79), channel_id=1, source_target_pairs={{0,2},{2,0},{4,6},{6,4},{8,10},{10,8},{12,14},{14,12},{16,18},{18,... | collective-permute-start | bytes 301064 | tf_op jit(solution)/shard_map/ppermute | solution.py:577
  11.0 4.6 %collective-permute-start.3 = (bf16[392,128]{1,0:T(8,128)(2,1)S(1)}, bf16[392,128]{1,0:T(8,128)(2,1)S(1)}, u32[]{:S(2)}, u32[]{:S(2)}) collective-permute-start(bf16[392,128]{1,0:T(8,128)(2,1)S(1)} %get-tuple-element.80), channel_id=1, source_target_pairs={{0,4},{2,6},{4,0},{6,2},{8,12},{10,14},{12,8},{14,10},{16,20},{18,... | collective-permute-start | bytes 301064 | tf_op jit(solution)/shard_map/ppermute | solution.py:577
  15.9 4.7 %collective-permute-start.4 = (bf16[392,128]{1,0:T(8,128)(2,1)S(1)}, bf16[392,128]{1,0:T(8,128)(2,1)S(1)}, u32[]{:S(2)}, u32[]{:S(2)}) collective-permute-start(bf16[392,128]{1,0:T(8,128)(2,1)S(1)} %shard_map.142.refs_0_.refs_4_), channel_id=1, source_target_pairs={{0,8},{2,10},{4,12},{6,14},{8,0},{10,2},{12,4},{14,6},{16,24},{18,... | collective-permute-start | bytes 301064 | tf_op jit(solution)/shard_map/ppermute | solution.py:577
  20.9 5.6 %collective-permute-start.5 = (bf16[392,128]{1,0:T(8,128)(2,1)S(1)}, bf16[392,128]{1,0:T(8,128)(2,1)S(1)}, u32[]{:S(2)}, u32[]{:S(2)}) collective-permute-start(bf16[392,128]{1,0:T(8,128)(2,1)S(1)} %shard_map.144.refs_6_), channel_id=1, source_target_pairs={{0,16},{2,18},{4,20},{6,22},{8,24},{10,26},{12,28},{14,30},{16,0},... | collective-permute-start | bytes 301064 | tf_op jit(solution)/shard_map/ppermute | solution.py:577
  27.0 5.1 %collective-permute-start.8 = (bf16[392,128]{1,0:T(8,128)(2,1)S(1)}, bf16[392,128]{1,0:T(8,128)(2,1)S(1)}, u32[]{:S(2)}, u32[]{:S(2)}) collective-permute-start(bf16[392,128]{1,0:T(8,128)(2,1)S(1)} %get-tuple-element.105), channel_id=1, source_target_pairs={{0,2},{2,0},{4,6},{6,4},{8,10},{10,8},{12,14},{14,12},{16,18},{18,... | collective-permute-start | bytes 301064 | tf_op jit(solution)/shard_map/ppermute | solution.py:577
  28.6 5.1 %collective-permute-start.6 = (bf16[392,128]{1,0:T(8,128)(2,1)S(1)}, bf16[392,128]{1,0:T(8,128)(2,1)S(1)}, u32[]{:S(2)}, u32[]{:S(2)}) collective-permute-start(bf16[392,128]{1,0:T(8,128)(2,1)S(1)} %get-tuple-element.96), channel_id=1, source_target_pairs={{0,4},{2,6},{4,0},{6,2},{8,12},{10,14},{12,8},{14,10},{16,20},{18,... | collective-permute-start | bytes 301064 | tf_op jit(solution)/shard_map/ppermute | solution.py:577
  29.1 5.5 %collective-permute-start.7 = (bf16[392,128]{1,0:T(8,128)(2,1)S(1)}, bf16[392,128]{1,0:T(8,128)(2,1)S(1)}, u32[]{:S(2)}, u32[]{:S(2)}) collective-permute-start(bf16[392,128]{1,0:T(8,128)(2,1)S(1)} %get-tuple-element.97), channel_id=1, source_target_pairs={{0,6},{2,4},{4,2},{6,0},{8,14},{10,12},{12,10},{14,8},{16,22},{18,... | collective-permute-start | bytes 301064 | tf_op jit(solution)/shard_map/ppermute | solution.py:577
  37.3 1.8 %collective-permute-start.9 = (f32[784,128]{1,0:T(8,128)S(1)}, f32[784,128]{1,0:T(8,128)S(1)}, u32[]{:S(2)}, u32[]{:S(2)}) collective-permute-start(f32[784,128]{1,0:T(8,128)S(1)} %get-tuple-element.119), channel_id=1, source_target_pairs={{0,1},{1,0},{2,3},{3,2},{4,5},{5,4},{6,7},{7,6},{8,9},{9,8},{10,11... | collective-permute-start | bytes 1204232 | tf_op jit(solution)/shard_map/ppermute | solution.py:793

commit v7 on v6

--- a/solution.py
+++ b/solution.py
@@ -544,8 +544,8 @@
     def update(stacked, gradient):
         first_moment = beta_one * stacked[1] + (1.0 - beta_one) * gradient
         second = beta_two * stacked[2] + (1.0 - beta_two) * gradient * gradient
-        step = first_moment / first_fix / (jnp.sqrt(second / second_fix) + epsilon)
-        return (stacked[0] - learn_rate * step, first_moment, second)
+        step = first_moment / (jnp.sqrt(second * (1.0 / second_fix)) + epsilon)
+        return (stacked[0] - (learn_rate / first_fix) * step, first_moment, second)
 
     def gathered(spot, rows):
         total = grad_refs[0][spot : spot + rows, :]
@@ -753,7 +753,7 @@
     )
     earlier, depths, before = ((), [], ())
     place = {k: (n, slots.index(k)) for n, slots in enumerate(groups) for k in slots}
-    steps = [(0,), (1,), tuple(range(2, quad))]
+    steps = [(0,), (2, 1), (3,)]
     for slots in steps:
         last = slots == steps[-1]
         if last:

time: 40.5 us -> 39.5 us (0.975)
  waiting for transfers between devices: 8.75 us -> 7.85 us
    ppermute x8, waiting for transfers between devices: 6.79 us -> 5.89 us  [swap(): lax.ppermute(value, 'region', [(i, i ^ distance) for i in range(size)])]
  transfers between devices with their start and end apart: 10 -> 10, of which waited for: 8 -> 7; matrix products, arithmetic and copies ran while one was open for 0% -> 0% of each run, Pallas kernels for 26% -> 29%
where the time goes in v7:
time: 39.5 us; the launch traced here: 39.3 us
  Pallas kernels  17.8 us (45%)
  starting transfers between devices  12.9 us (33%)
  waiting for transfers between devices  7.85 us (20%)
  between operations  0.74 us (2%)
    pallas_call x14, Pallas kernels, call(): pl.pallas_call(body, out_shape=out_shape, in_specs=specs or [spec] * len(...  17.8 us
    ppermute x8, starting transfers between devices, swap(): lax.ppermute(value, 'region', [(i, i ^ distance) for i in range(size)])  12.4 us
    ppermute x8, waiting for transfers between devices, swap(): lax.ppermute(value, 'region', [(i, i ^ distance) for i in range(size)])  5.89 us
    ppermute x1, waiting for transfers between devices, per_device(): parts = (grads[0], lax.ppermute(grads[1], 'rays', [(0, 1), (1, 0)]))  1.72 us
  transfers between devices with their start and end apart: 10, of which 7 were waited for; matrix products, arithmetic and copies ran while one was open for 0% of the time, Pallas kernels for 29%

profile of v7, /device:TPU:0, one launch (start us, length us, event | category | flops | bytes accessed | tf_op | source)
XLA Modules:
  0.0 39.3 jit_solution(7504470990597931799)
XLA Ops:
  0.6 1.3 %shard_map.137 = (bf16[784,128]{1,0:T(8,128)(2,1)S(1)}, bf16[2,512,128]{2,1,0:T(8,128)(2,1)S(1)}, s32[1,8,512]{2,1,0:T(8,128)S(1)}, s32[1,512]{1,0:T(1,128)S(1)}...) custom-call(f32[3,1,64,256]{3,2,1,0:T(8,128)} %refs_0_.3, f32[3,1,128,256]{3,2,1,0:T(8,128)} %refs_1_.3, ...), custom_call_target="tpu_custom_call" | custom-call | flops 1000000 | bytes 1000000 | tf_op jit(solution)/shard_map/pallas_call | solution.py:37
  2.0 0.5 %collective-permute-start = (bf16[784,128]{1,0:T(8,128)(2,1)S(1)}, bf16[784,128]{1,0:T(8,128)(2,1)S(1)}, u32[]{:S(2)}, u32[]{:S(2)}) collective-permute-start(bf16[784,128]{1,0:T(8,128)(2,1)S(1)} %get-tuple-element.65.refs_0_), channel_id=1, source_target_pairs={{0,1},{1,0},{2,3},{3,2},{4,5},{5,4},{6,7},{7,6},{8,9},{9,8},{10,11... | collective-permute-start | bytes 602120 | tf_op jit(solution)/shard_map/ppermute | solution.py:624
  2.5 0.8 %shard_map.138 = (bf16[4,1024,128]{2,1,0:T(8,128)(2,1)S(1)}, f32[4,16,128]{2,1,0:T(8,128)S(1)}) custom-call(bf16[2,512,128]{2,1,0:T(8,128)(2,1)S(1)} %get-tuple-element.66.refs_0_, s32[1,8,512]{2,1,0:T(8,128)S(1)} %get-tuple-element.67.refs_1_, s32[1,512]{1,0:T(1,128)S(1)} %get-tuple-element.68.refs_2_, s32[1,512]{1,0:T(1,128)S(1)} %get-tuple-element.69.refs_3_, ...), custom_call_target="tpu_custom_call" | custom-call | flops 5242880 | bytes 2097152 | tf_op jit(solution)/shard_map/pallas_call | solution.py:37
  3.3 0.2 collective-permute-done.refs_1_
  3.6 1.2 %shard_map.139 = (bf16[128,256]{1,0:T(8,128)(2,1)S(1)}, bf16[256,256]{1,0:T(8,128)(2,1)S(1)}, bf16[256,512]{1,0:T(8,128)(2,1)S(1)}, f32[1,1152]{1,0:T(1,128)S(1)...) custom-call(bf16[784,128]{1,0:T(8,128)(2,1)S(1)} %get-tuple-element., ...), custom_call_target="tpu_custom_call" | custom-call | flops 469762048 | bytes 2621440 | tf_op jit(solution)/shard_map/pallas_call | solution.py:37
  4.8 3.9 %collective-permute-start.1 = (bf16[392,128]{1,0:T(8,128)(2,1)S(1)}, bf16[392,128]{1,0:T(8,128)(2,1)S(1)}, u32[]{:S(2)}, u32[]{:S(2)}) collective-permute-start(bf16[392,128]{1,0:T(8,128)(2,1)S(1)} %get-tuple-element.77), channel_id=1, source_target_pairs={{0,6},{2,4},{4,2},{6,0},{8,14},{10,12},{12,10},{14,8},{16,22},{18,... | collective-permute-start | bytes 301064 | tf_op jit(solution)/shard_map/ppermute | solution.py:577
  8.7 1.7 %shard_map.141 = (bf16[2,1024,256]{2,1,0:T(8,128)(2,1)S(1)}, bf16[2,1024,256]{2,1,0:T(8,128)(2,1)S(1)}, f32[2,1024,384]{2,1,0:T(8,128)S(1)}, f32[2,3,8,128]{3,2,...) custom-call(bf16[128,256]{1,0:T(8,128)(2,1)S(1)} %get-tuple-element.73.in_ref, ...), custom_call_target="tpu_custom_call" | custom-call | flops 939524096 | bytes 5242880 | tf_op jit(solution)/shard_map/pallas_call | solution.py:37
  10.4 0.6 %collective-permute-start.2 = (bf16[392,128]{1,0:T(8,128)(2,1)S(1)}, bf16[392,128]{1,0:T(8,128)(2,1)S(1)}, u32[]{:S(2)}, u32[]{:S(2)}) collective-permute-start(bf16[392,128]{1,0:T(8,128)(2,1)S(1)} %get-tuple-element.79), channel_id=1, source_target_pairs={{0,2},{2,0},{4,6},{6,4},{8,10},{10,8},{12,14},{14,12},{16,18},{18,... | collective-permute-start | bytes 301064 | tf_op jit(solution)/shard_map/ppermute | solution.py:577
  11.0 0.0 collective-permute-start.3
  11.0 0.8 %collective-permute-done.1.refs_0_.refs_3_ = bf16[392,128]{1,0:T(8,128)(2,1)S(1)} collective-permute-done((bf16[392,128]{1,0:T(8,128)(2,1)S(1)}, bf16[392,128]{1,0:T(8,128)(2,1)S(1)}, u32[]{:S(2)}, u32[]{:S(2)}) %collective-permute-start.1) | collective-permute-done | bytes 100384 | tf_op jit(solution)/shard_map/ppermute | solution.py:577
  11.8 1.1 %shard_map.140 = (bf16[1,1024,256]{2,1,0:T(8,128)(2,1)S(1)}, bf16[1,1024,256]{2,1,0:T(8,128)(2,1)S(1)}, f32[1,1024,384]{2,1,0:T(8,128)S(1)}, f32[1,3,8,128]{3,2,1,0:T(8,128)S(1)}, bf16[392,128]{1,0:T(8,128)(2,1)S(1)}) custom-call(bf16[128,256]{1,0:T(8,128)(2,1)S(1)} %get-tuple-element.73.in_ref, bf16[256,256]{1,0:T(8,128)(2,1)S(1)} %get-tuple-element.74.mid_ref.refs_5_, ...), custom_call_target="tpu_custom_call" | custom-call | flops 469762048 | bytes 2621440 | tf_op jit(solution)/shard_map/pallas_call | solution.py:37
  12.9 2.1 %collective-permute-done.2.refs_1_ = bf16[392,128]{1,0:T(8,128)(2,1)S(1)} collective-permute-done((bf16[392,128]{1,0:T(8,128)(2,1)S(1)}, bf16[392,128]{1,0:T(8,128)(2,1)S(1)}, u32[]{:S(2)}, u32[]{:S(2)}) %collective-permute-start.2) | collective-permute-done | bytes 100384 | tf_op jit(solution)/shard_map/ppermute | solution.py:577
  15.1 0.5 %collective-permute-done.3.refs_2_ = bf16[392,128]{1,0:T(8,128)(2,1)S(1)} collective-permute-done((bf16[392,128]{1,0:T(8,128)(2,1)S(1)}, bf16[392,128]{1,0:T(8,128)(2,1)S(1)}, u32[]{:S(2)}, u32[]{:S(2)}) %collective-permute-start.3) | collective-permute-done | bytes 100384 | tf_op jit(solution)/shard_map/ppermute | solution.py:577
  15.6 0.3 shard_map.142.refs_0_.refs_4_
  15.9 1.6 %collective-permute-start.4 = (bf16[392,128]{1,0:T(8,128)(2,1)S(1)}, bf16[392,128]{1,0:T(8,128)(2,1)S(1)}, u32[]{:S(2)}, u32[]{:S(2)}) collective-permute-start(bf16[392,128]{1,0:T(8,128)(2,1)S(1)} %shard_map.142.refs_0_.refs_4_), channel_id=1, source_target_pairs={{0,8},{2,10},{4,12},{6,14},{8,0},{10,2},{12,4},{14,6},{16,24},{18,... | collective-permute-start | bytes 301064 | tf_op jit(solution)/shard_map/ppermute | solution.py:577
  17.6 2.0 %shard_map.143 = (f32[3,1,64,256]{3,2,1,0:T(8,128)S(1)}, f32[3,1,128,256]{3,2,1,0:T(8,128)S(1)}, f32[3,1,128,384]{3,2,1,0:T(8,128)S(1)}, f32[3,1,576]{2,1,0:T(1,...) custom-call(f32[3,1,64,256]{3,2,1,0:T(8,128)} %refs_0_.3, ...), custom_call_target="tpu_custom_call" | custom-call | flops 469762048 | bytes 5242880 | tf_op jit(solution)/shard_map/pallas_call | solution.py:37
  19.5 1.1 %collective-permute-done.4.refs_1_.refs_5_ = bf16[392,128]{1,0:T(8,128)(2,1)S(1)} collective-permute-done((bf16[392,128]{1,0:T(8,128)(2,1)S(1)}, bf16[392,128]{1,0:T(8,128)(2,1)S(1)}, u32[]{:S(2)}, u32[]{:S(2)}) %collective-permute-start.4) | collective-permute-done | bytes 100384 | tf_op jit(solution)/shard_map/ppermute | solution.py:577
  20.6 0.3 shard_map.144.refs_6_
  20.9 2.7 %collective-permute-start.5 = (bf16[392,128]{1,0:T(8,128)(2,1)S(1)}, bf16[392,128]{1,0:T(8,128)(2,1)S(1)}, u32[]{:S(2)}, u32[]{:S(2)}) collective-permute-start(bf16[392,128]{1,0:T(8,128)(2,1)S(1)} %shard_map.144.refs_6_), channel_id=1, source_target_pairs={{0,16},{2,18},{4,20},{6,22},{8,24},{10,26},{12,28},{14,30},{16,0},... | collective-permute-start | bytes 301064 | tf_op jit(solution)/shard_map/ppermute | solution.py:577
  23.6 1.6 %shard_map.145 = (bf16[2,272,1024]{2,1,0:T(8,128)(2,1)S(1)}, bf16[2,272,1024]{2,1,0:T(8,128)(2,1)S(1)}, f32[2,1024,384]{2,1,0:T(8,128)S(1)}, bf16[1,272,1024]{2,...) custom-call(bf16[2,1024,256]{2,1,0:T(8,128)(2,1)S(1)} %get-tuple-element.87.refs_0_.refs_2_, ...), custom_call_target="tpu_custom_call" | custom-call | flops 1409286144 | bytes 15728640 | tf_op jit(solution)/shard_map/pallas_call | solution.py:37
  25.2 1.3 %collective-permute-done.5.refs_7_ = bf16[392,128]{1,0:T(8,128)(2,1)S(1)} collective-permute-done((bf16[392,128]{1,0:T(8,128)(2,1)S(1)}, bf16[392,128]{1,0:T(8,128)(2,1)S(1)}, u32[]{:S(2)}, u32[]{:S(2)}) %collective-permute-start.5) | collective-permute-done | bytes 100384 | tf_op jit(solution)/shard_map/ppermute | solution.py:577
  26.5 0.5 %shard_map.146 = (bf16[392,128]{1,0:T(8,128)(2,1)S(1)}, bf16[392,128]{1,0:T(8,128)(2,1)S(1)}, bf16[392,128]{1,0:T(8,128)(2,1)S(1)}, bf16[392,128]{1,0:T(8,128)(2,1)S(1)}) custom-call(bf16[392,128]{1,0:T(8,128)(2,1)S(1)} %get-tuple-element.78.refs_0_, bf16[392,128]{1,0:T(8,128)(2,1)S(1)} %collective-permute-done.2.refs_1_, ...), custom_call_target="tpu_custom_call" | custom-call | flops 1000000 | bytes 1000000 | tf_op jit(solution)/shard_map/pallas_call | solution.py:37
  27.0 0.2 collective-permute-start.7
  27.2 1.8 %collective-permute-start.8 = (bf16[392,128]{1,0:T(8,128)(2,1)S(1)}, bf16[392,128]{1,0:T(8,128)(2,1)S(1)}, u32[]{:S(2)}, u32[]{:S(2)}) collective-permute-start(bf16[392,128]{1,0:T(8,128)(2,1)S(1)} %get-tuple-element.103), channel_id=1, source_target_pairs={{0,2},{2,0},{4,6},{6,4},{8,10},{10,8},{12,14},{14,12},{16,18},{18,... | collective-permute-start | bytes 301064 | tf_op jit(solution)/shard_map/ppermute | solution.py:577
  29.1 1.5 %collective-permute-start.6 = (bf16[392,128]{1,0:T(8,128)(2,1)S(1)}, bf16[392,128]{1,0:T(8,128)(2,1)S(1)}, u32[]{:S(2)}, u32[]{:S(2)}) collective-permute-start(bf16[392,128]{1,0:T(8,128)(2,1)S(1)} %get-tuple-element.96), channel_id=1, source_target_pairs={{0,6},{2,4},{4,2},{6,0},{8,14},{10,12},{12,10},{14,8},{16,22},{18,... | collective-permute-start | bytes 301064 | tf_op jit(solution)/shard_map/ppermute | solution.py:577
  30.6 1.5 %shard_map.147 = (f32[144,256]{1,0:T(8,128)S(1)}, f32[272,256]{1,0:T(8,128)S(1)}, f32[272,512]{1,0:T(8,128)S(1)}, f32[1,128]{1,0:T(1,128)S(1)}) custom-call(bf16[392,128]{1,0:T(8,128)(2,1)S(1)} %get-tuple-element.106.refs_0_, bf16[1,1024,256]{2,1,0:T(8,128)(2,1)S(1)} %get-tuple-element.91.refs_4_.refs_1_, ...), custom_call_target="tpu_custom_call" | custom-call | flops 939524096 | bytes 2621440 | tf_op jit(solution)/shard_map/pallas_call | solution.py:37
  32.1 0.0 collective-permute-done.7.refs_0_
  32.1 0.0 collective-permute-done.8.refs_1_
  32.1 2.6 %shard_map.148 = (f32[144,256]{1,0:T(8,128)S(1)}, f32[272,256]{1,0:T(8,128)S(1)}, f32[272,512]{1,0:T(8,128)S(1)}, f32[2,128]{1,0:T(2,128)S(1)}) custom-call(bf16[392,128]{1,0:T(8,128)(2,1)S(1)} %collective-permute-done.7.refs_0_, bf16[392,128]{1,0:T(8,128)(2,1)S(1)} %collective-permute-done.8.refs_1_, ...), custom_call_target="tpu_custom_call" | custom-call | flops 1879048192 | bytes 5242880 | tf_op jit(solution)/shard_map/pallas_call | solution.py:37
  34.8 0.0 collective-permute-done.6.refs_0_
  34.8 1.7 %shard_map.149 = (f32[1,512]{1,0:T(1,128)S(1)}, f32[784,128]{1,0:T(8,128)S(1)}, f32[784,128]{1,0:T(8,128)S(1)}) custom-call(bf16[392,128]{1,0:T(8,128)(2,1)S(1)} %collective-permute-done.6.refs_0_, bf16[1,1024,256]{2,1,0:T(8,128)(2,1)S(1)} %get-tuple-element.81.refs_7_.refs_1_, bf16[1,1024,256]{2,1,0:T(8,128)(2,1)S(1)} %get-tuple-element.82.refs_8_.refs_2_, ...), custom_call_target="tpu_custom_call" | custom-call | flops 939524096 | bytes 2621440 | tf_op jit(solution)/shard_map/pallas_call | solution.py:37
  36.4 0.0 collective-permute-start.9
  36.5 1.7 %collective-permute-done.9.refs_1_ = f32[784,128]{1,0:T(8,128)S(1)} collective-permute-done((f32[784,128]{1,0:T(8,128)S(1)}, f32[784,128]{1,0:T(8,128)S(1)}, u32[]{:S(2)}, u32[]{:S(2)}) %collective-permute-start.9) | collective-permute-done | bytes 401440 | tf_op jit(solution)/shard_map/ppermute | solution.py:793
  38.2 1.1 %shard_map.150 = (f32[3,1,64,256]{3,2,1,0:T(8,128)}, f32[3,1,128,256]{3,2,1,0:T(8,128)}, f32[3,1,128,384]{3,2,1,0:T(8,128)}, f32[3,1,576]{2,1,0:T(1,128)}, f32[1,512]{1,0:T(1,128)}) custom-call(f32[784,128]{1,0:T(8,128)S(1)} %get-tuple-element.118.refs_0_, f32[784,128]{1,0:T(8,128)S(1)} %collective-permute-done.9.refs_1_, ...), custom_call_target="tpu_custom_call" | custom-call | flops 1000000 | bytes 1000000 | tf_op jit(solution)/shard_map/pallas_call | solution.py:37
Async XLA Ops:
  2.0 1.6 %collective-permute-start = (bf16[784,128]{1,0:T(8,128)(2,1)S(1)}, bf16[784,128]{1,0:T(8,128)(2,1)S(1)}, u32[]{:S(2)}, u32[]{:S(2)}) collective-permute-start(bf16[784,128]{1,0:T(8,128)(2,1)S(1)} %get-tuple-element.65.refs_0_), channel_id=1, source_target_pairs={{0,1},{1,0},{2,3},{3,2},{4,5},{5,4},{6,7},{7,6},{8,9},{9,8},{10,11... | collective-permute-start | bytes 602120 | tf_op jit(solution)/shard_map/ppermute | solution.py:624
  4.8 7.0 %collective-permute-start.1 = (bf16[392,128]{1,0:T(8,128)(2,1)S(1)}, bf16[392,128]{1,0:T(8,128)(2,1)S(1)}, u32[]{:S(2)}, u32[]{:S(2)}) collective-permute-start(bf16[392,128]{1,0:T(8,128)(2,1)S(1)} %get-tuple-element.77), channel_id=1, source_target_pairs={{0,6},{2,4},{4,2},{6,0},{8,14},{10,12},{12,10},{14,8},{16,22},{18,... | collective-permute-start | bytes 301064 | tf_op jit(solution)/shard_map/ppermute | solution.py:577
  10.4 4.7 %collective-permute-start.2 = (bf16[392,128]{1,0:T(8,128)(2,1)S(1)}, bf16[392,128]{1,0:T(8,128)(2,1)S(1)}, u32[]{:S(2)}, u32[]{:S(2)}) collective-permute-start(bf16[392,128]{1,0:T(8,128)(2,1)S(1)} %get-tuple-element.79), channel_id=1, source_target_pairs={{0,2},{2,0},{4,6},{6,4},{8,10},{10,8},{12,14},{14,12},{16,18},{18,... | collective-permute-start | bytes 301064 | tf_op jit(solution)/shard_map/ppermute | solution.py:577
  11.0 4.6 %collective-permute-start.3 = (bf16[392,128]{1,0:T(8,128)(2,1)S(1)}, bf16[392,128]{1,0:T(8,128)(2,1)S(1)}, u32[]{:S(2)}, u32[]{:S(2)}) collective-permute-start(bf16[392,128]{1,0:T(8,128)(2,1)S(1)} %get-tuple-element.80), channel_id=1, source_target_pairs={{0,4},{2,6},{4,0},{6,2},{8,12},{10,14},{12,8},{14,10},{16,20},{18,... | collective-permute-start | bytes 301064 | tf_op jit(solution)/shard_map/ppermute | solution.py:577
  15.9 4.7 %collective-permute-start.4 = (bf16[392,128]{1,0:T(8,128)(2,1)S(1)}, bf16[392,128]{1,0:T(8,128)(2,1)S(1)}, u32[]{:S(2)}, u32[]{:S(2)}) collective-permute-start(bf16[392,128]{1,0:T(8,128)(2,1)S(1)} %shard_map.142.refs_0_.refs_4_), channel_id=1, source_target_pairs={{0,8},{2,10},{4,12},{6,14},{8,0},{10,2},{12,4},{14,6},{16,24},{18,... | collective-permute-start | bytes 301064 | tf_op jit(solution)/shard_map/ppermute | solution.py:577
  20.9 5.6 %collective-permute-start.5 = (bf16[392,128]{1,0:T(8,128)(2,1)S(1)}, bf16[392,128]{1,0:T(8,128)(2,1)S(1)}, u32[]{:S(2)}, u32[]{:S(2)}) collective-permute-start(bf16[392,128]{1,0:T(8,128)(2,1)S(1)} %shard_map.144.refs_6_), channel_id=1, source_target_pairs={{0,16},{2,18},{4,20},{6,22},{8,24},{10,26},{12,28},{14,30},{16,0},... | collective-permute-start | bytes 301064 | tf_op jit(solution)/shard_map/ppermute | solution.py:577
  27.0 5.1 %collective-permute-start.7 = (bf16[392,128]{1,0:T(8,128)(2,1)S(1)}, bf16[392,128]{1,0:T(8,128)(2,1)S(1)}, u32[]{:S(2)}, u32[]{:S(2)}) collective-permute-start(bf16[392,128]{1,0:T(8,128)(2,1)S(1)} %get-tuple-element.102), channel_id=1, source_target_pairs={{0,4},{2,6},{4,0},{6,2},{8,12},{10,14},{12,8},{14,10},{16,20},{18,... | collective-permute-start | bytes 301064 | tf_op jit(solution)/shard_map/ppermute | solution.py:577
  27.2 4.9 %collective-permute-start.8 = (bf16[392,128]{1,0:T(8,128)(2,1)S(1)}, bf16[392,128]{1,0:T(8,128)(2,1)S(1)}, u32[]{:S(2)}, u32[]{:S(2)}) collective-permute-start(bf16[392,128]{1,0:T(8,128)(2,1)S(1)} %get-tuple-element.103), channel_id=1, source_target_pairs={{0,2},{2,0},{4,6},{6,4},{8,10},{10,8},{12,14},{14,12},{16,18},{18,... | collective-permute-start | bytes 301064 | tf_op jit(solution)/shard_map/ppermute | solution.py:577
  29.1 5.7 %collective-permute-start.6 = (bf16[392,128]{1,0:T(8,128)(2,1)S(1)}, bf16[392,128]{1,0:T(8,128)(2,1)S(1)}, u32[]{:S(2)}, u32[]{:S(2)}) collective-permute-start(bf16[392,128]{1,0:T(8,128)(2,1)S(1)} %get-tuple-element.96), channel_id=1, source_target_pairs={{0,6},{2,4},{4,2},{6,0},{8,14},{10,12},{12,10},{14,8},{16,22},{18,... | collective-permute-start | bytes 301064 | tf_op jit(solution)/shard_map/ppermute | solution.py:577
  36.4 1.8 %collective-permute-start.9 = (f32[784,128]{1,0:T(8,128)S(1)}, f32[784,128]{1,0:T(8,128)S(1)}, u32[]{:S(2)}, u32[]{:S(2)}) collective-permute-start(f32[784,128]{1,0:T(8,128)S(1)} %get-tuple-element.119), channel_id=1, source_target_pairs={{0,1},{1,0},{2,3},{3,2},{4,5},{5,4},{6,7},{7,6},{8,9},{9,8},{10,11... | collective-permute-start | bytes 1204232 | tf_op jit(solution)/shard_map/ppermute | solution.py:793

commit v8 on v7

--- a/solution.py
+++ b/solution.py
@@ -514,9 +514,11 @@
     vec = jnp.concatenate([first_sum, second_sum, density_sum, head_sum[:, :feat]], 1)
     total = vec.shape[1]
 
-    def write(s, ref):
+    def write(s, ref, rest=None):
         spot = 0
-        for (rows, width), value in zip(shapes, values):
+        for n, ((rows, width), value) in enumerate(zip(shapes, values)):
+            if n == 2 and rest is not None:
+                ref, spot = (rest, 0)
             for cut in blocks(width):
                 ref[spot : spot + rows, :] = value[rows * s : rows * (s + 1), cut]
                 spot += rows
@@ -533,11 +535,13 @@
         @pl.when(mine == s)
         def _():
             write(s, outs[0])
-            write(1 - s, outs[1])
+            write(1 - s, outs[1], outs[2])
 
 
 def adam_body(*refs, shards):
-    grad_refs, (depth_ref, *refs) = (refs[:shards], refs[shards:])
+    count = 3 if shards == 2 else shards
+    grad_refs, (depth_ref, *refs) = (refs[:count], refs[count:])
+    split = grad_refs[1].shape[0]
     state_refs, out_refs, depth_out = (refs[:4], refs[4:8], refs[8])
     depth_out[...] = depth_ref[...]
 
@@ -549,6 +553,9 @@
 
     def gathered(spot, rows):
         total = grad_refs[0][spot : spot + rows, :]
+        if shards == 2:
+            ref, first = (grad_refs[1], spot) if spot < split else (grad_refs[2], spot - split)
+            return total + ref[first : first + rows, :]
         for ref in grad_refs[1:]:
             total = total + ref[spot : spot + rows, :]
         return total
@@ -758,7 +765,11 @@
         last = slots == steps[-1]
         if last:
             share = pltpu.VMEM((pack_rows, LANES), f32)
-            out_shape = (pltpu.VMEM((1, ray_count), f32), share, share)
+            near_rows = sum(rows * (width // LANES) for rows, width in shapes[:2])
+            sent_shapes = [
+                pltpu.VMEM((n, LANES), f32) for n in (near_rows, pack_rows - near_rows)
+            ]
+            out_shape = (pltpu.VMEM((1, ray_count), f32), share, *sent_shapes)
             if not pair:
                 out_shape = (out_shape[0], shaped((shards, pack_rows, LANES), f32))
         else:
@@ -790,7 +801,8 @@
             depths.append(out[3])
     depth_grad, *grads = out
     if pair:
-        parts = (grads[0], lax.ppermute(grads[1], "rays", [(0, 1), (1, 0)]))
+        parts = [grads[0]]
+        parts += [lax.ppermute(value, "rays", [(0, 1), (1, 0)]) for value in grads[1:]]
     else:
         exchanged = lax.all_to_all(grads[0], "rays", 0, 0)
         parts = tuple(exchanged[s] for s in range(shards))

time: 39.5 us -> 39.5 us (level)
  starting transfers between devices: 12.9 us -> 13.4 us
  waiting for transfers between devices: 7.85 us -> 7.36 us
    ppermute x1 -> x2, starting transfers between devices: 0.02 us -> 0.52 us  [per_device(): lax.ppermute(value, 'rays', [(0, 1), (1, 0)])]
    ppermute x1 -> x2, waiting for transfers between devices: 1.72 us -> 1.23 us  [per_device(): lax.ppermute(value, 'rays', [(0, 1), (1, 0)])]
  transfers between devices with their start and end apart: 10 -> 11, of which waited for: 7 -> 7; matrix products, arithmetic and copies ran while one was open for 0% -> 0% of each run, Pallas kernels for 29% -> 29%
where the time goes in v8:
time: 39.5 us; the launch traced here: 39.3 us
  Pallas kernels  17.8 us (45%)
  starting transfers between devices  13.4 us (34%)
  waiting for transfers between devices  7.36 us (19%)
  between operations  0.74 us (2%)
    pallas_call x14, Pallas kernels, call(): pl.pallas_call(body, out_shape=out_shape, in_specs=specs or [spec] * len(...  17.8 us
    ppermute x8, starting transfers between devices, swap(): lax.ppermute(value, 'region', [(i, i ^ distance) for i in range(size)])  12.4 us
    ppermute x8, waiting for transfers between devices, swap(): lax.ppermute(value, 'region', [(i, i ^ distance) for i in range(size)])  5.89 us
    ppermute x2, waiting for transfers between devices, per_device(): lax.ppermute(value, 'rays', [(0, 1), (1, 0)])  1.23 us
  transfers between devices with their start and end apart: 11, of which 7 were waited for; matrix products, arithmetic and copies ran while one was open for 0% of the time, Pallas kernels for 29%

profile of v8, /device:TPU:0, one launch (start us, length us, event | category | flops | bytes accessed | tf_op | source)
XLA Modules:
  0.0 39.3 jit_solution(7241607233857776988)
XLA Ops:
  0.6 1.3 %shard_map.137 = (bf16[784,128]{1,0:T(8,128)(2,1)S(1)}, bf16[2,512,128]{2,1,0:T(8,128)(2,1)S(1)}, s32[1,8,512]{2,1,0:T(8,128)S(1)}, s32[1,512]{1,0:T(1,128)S(1)}...) custom-call(f32[3,1,64,256]{3,2,1,0:T(8,128)} %refs_0_.3, f32[3,1,128,256]{3,2,1,0:T(8,128)} %refs_1_.3, ...), custom_call_target="tpu_custom_call" | custom-call | flops 1000000 | bytes 1000000 | tf_op jit(solution)/shard_map/pallas_call | solution.py:37
  2.0 0.5 %collective-permute-start = (bf16[784,128]{1,0:T(8,128)(2,1)S(1)}, bf16[784,128]{1,0:T(8,128)(2,1)S(1)}, u32[]{:S(2)}, u32[]{:S(2)}) collective-permute-start(bf16[784,128]{1,0:T(8,128)(2,1)S(1)} %get-tuple-element.66.refs_0_), channel_id=1, source_target_pairs={{0,1},{1,0},{2,3},{3,2},{4,5},{5,4},{6,7},{7,6},{8,9},{9,8},{10,11... | collective-permute-start | bytes 602120 | tf_op jit(solution)/shard_map/ppermute | solution.py:631
  2.5 0.8 %shard_map.138 = (bf16[4,1024,128]{2,1,0:T(8,128)(2,1)S(1)}, f32[4,16,128]{2,1,0:T(8,128)S(1)}) custom-call(bf16[2,512,128]{2,1,0:T(8,128)(2,1)S(1)} %get-tuple-element.67.refs_0_, s32[1,8,512]{2,1,0:T(8,128)S(1)} %get-tuple-element.68.refs_1_, s32[1,512]{1,0:T(1,128)S(1)} %get-tuple-element.69.refs_2_, s32[1,512]{1,0:T(1,128)S(1)} %get-tuple-element.70.refs_3_, ...), custom_call_target="tpu_custom_call" | custom-call | flops 5242880 | bytes 2097152 | tf_op jit(solution)/shard_map/pallas_call | solution.py:37
  3.3 0.2 collective-permute-done.refs_1_
  3.6 1.2 %shard_map.139 = (bf16[128,256]{1,0:T(8,128)(2,1)S(1)}, bf16[256,256]{1,0:T(8,128)(2,1)S(1)}, bf16[256,512]{1,0:T(8,128)(2,1)S(1)}, f32[1,1152]{1,0:T(1,128)S(1)...) custom-call(bf16[784,128]{1,0:T(8,128)(2,1)S(1)} %get-tuple-element., ...), custom_call_target="tpu_custom_call" | custom-call | flops 469762048 | bytes 2621440 | tf_op jit(solution)/shard_map/pallas_call | solution.py:37
  4.8 3.9 %collective-permute-start.1 = (bf16[392,128]{1,0:T(8,128)(2,1)S(1)}, bf16[392,128]{1,0:T(8,128)(2,1)S(1)}, u32[]{:S(2)}, u32[]{:S(2)}) collective-permute-start(bf16[392,128]{1,0:T(8,128)(2,1)S(1)} %get-tuple-element.78), channel_id=1, source_target_pairs={{0,6},{2,4},{4,2},{6,0},{8,14},{10,12},{12,10},{14,8},{16,22},{18,... | collective-permute-start | bytes 301064 | tf_op jit(solution)/shard_map/ppermute | solution.py:584
  8.7 1.7 %shard_map.141 = (bf16[2,1024,256]{2,1,0:T(8,128)(2,1)S(1)}, bf16[2,1024,256]{2,1,0:T(8,128)(2,1)S(1)}, f32[2,1024,384]{2,1,0:T(8,128)S(1)}, f32[2,3,8,128]{3,2,...) custom-call(bf16[128,256]{1,0:T(8,128)(2,1)S(1)} %get-tuple-element.74.in_ref, ...), custom_call_target="tpu_custom_call" | custom-call | flops 939524096 | bytes 5242880 | tf_op jit(solution)/shard_map/pallas_call | solution.py:37
  10.4 0.6 %collective-permute-start.2 = (bf16[392,128]{1,0:T(8,128)(2,1)S(1)}, bf16[392,128]{1,0:T(8,128)(2,1)S(1)}, u32[]{:S(2)}, u32[]{:S(2)}) collective-permute-start(bf16[392,128]{1,0:T(8,128)(2,1)S(1)} %get-tuple-element.80), channel_id=1, source_target_pairs={{0,2},{2,0},{4,6},{6,4},{8,10},{10,8},{12,14},{14,12},{16,18},{18,... | collective-permute-start | bytes 301064 | tf_op jit(solution)/shard_map/ppermute | solution.py:584
  11.0 0.0 collective-permute-start.3
  11.0 0.8 %collective-permute-done.1.refs_0_.refs_3_ = bf16[392,128]{1,0:T(8,128)(2,1)S(1)} collective-permute-done((bf16[392,128]{1,0:T(8,128)(2,1)S(1)}, bf16[392,128]{1,0:T(8,128)(2,1)S(1)}, u32[]{:S(2)}, u32[]{:S(2)}) %collective-permute-start.1) | collective-permute-done | bytes 100384 | tf_op jit(solution)/shard_map/ppermute | solution.py:584
  11.8 1.1 %shard_map.140 = (bf16[1,1024,256]{2,1,0:T(8,128)(2,1)S(1)}, bf16[1,1024,256]{2,1,0:T(8,128)(2,1)S(1)}, f32[1,1024,384]{2,1,0:T(8,128)S(1)}, f32[1,3,8,128]{3,2,1,0:T(8,128)S(1)}, bf16[392,128]{1,0:T(8,128)(2,1)S(1)}) custom-call(bf16[128,256]{1,0:T(8,128)(2,1)S(1)} %get-tuple-element.74.in_ref, bf16[256,256]{1,0:T(8,128)(2,1)S(1)} %get-tuple-element.75.mid_ref.refs_5_, ...), custom_call_target="tpu_custom_call" | custom-call | flops 469762048 | bytes 2621440 | tf_op jit(solution)/shard_map/pallas_call | solution.py:37
  12.9 2.1 %collective-permute-done.2.refs_1_ = bf16[392,128]{1,0:T(8,128)(2,1)S(1)} collective-permute-done((bf16[392,128]{1,0:T(8,128)(2,1)S(1)}, bf16[392,128]{1,0:T(8,128)(2,1)S(1)}, u32[]{:S(2)}, u32[]{:S(2)}) %collective-permute-start.2) | collective-permute-done | bytes 100384 | tf_op jit(solution)/shard_map/ppermute | solution.py:584
  15.1 0.5 %collective-permute-done.3.refs_2_ = bf16[392,128]{1,0:T(8,128)(2,1)S(1)} collective-permute-done((bf16[392,128]{1,0:T(8,128)(2,1)S(1)}, bf16[392,128]{1,0:T(8,128)(2,1)S(1)}, u32[]{:S(2)}, u32[]{:S(2)}) %collective-permute-start.3) | collective-permute-done | bytes 100384 | tf_op jit(solution)/shard_map/ppermute | solution.py:584
  15.6 0.3 shard_map.142.refs_0_.refs_4_
  15.9 1.6 %collective-permute-start.4 = (bf16[392,128]{1,0:T(8,128)(2,1)S(1)}, bf16[392,128]{1,0:T(8,128)(2,1)S(1)}, u32[]{:S(2)}, u32[]{:S(2)}) collective-permute-start(bf16[392,128]{1,0:T(8,128)(2,1)S(1)} %shard_map.142.refs_0_.refs_4_), channel_id=1, source_target_pairs={{0,8},{2,10},{4,12},{6,14},{8,0},{10,2},{12,4},{14,6},{16,24},{18,... | collective-permute-start | bytes 301064 | tf_op jit(solution)/shard_map/ppermute | solution.py:584
  17.6 2.0 %shard_map.143 = (f32[3,1,64,256]{3,2,1,0:T(8,128)S(1)}, f32[3,1,128,256]{3,2,1,0:T(8,128)S(1)}, f32[3,1,128,384]{3,2,1,0:T(8,128)S(1)}, f32[3,1,576]{2,1,0:T(1,...) custom-call(f32[3,1,64,256]{3,2,1,0:T(8,128)} %refs_0_.3, ...), custom_call_target="tpu_custom_call" | custom-call | flops 469762048 | bytes 5242880 | tf_op jit(solution)/shard_map/pallas_call | solution.py:37
  19.5 1.1 %collective-permute-done.4.refs_1_.refs_5_ = bf16[392,128]{1,0:T(8,128)(2,1)S(1)} collective-permute-done((bf16[392,128]{1,0:T(8,128)(2,1)S(1)}, bf16[392,128]{1,0:T(8,128)(2,1)S(1)}, u32[]{:S(2)}, u32[]{:S(2)}) %collective-permute-start.4) | collective-permute-done | bytes 100384 | tf_op jit(solution)/shard_map/ppermute | solution.py:584
  20.6 0.3 shard_map.144.refs_6_
  20.9 2.7 %collective-permute-start.5 = (bf16[392,128]{1,0:T(8,128)(2,1)S(1)}, bf16[392,128]{1,0:T(8,128)(2,1)S(1)}, u32[]{:S(2)}, u32[]{:S(2)}) collective-permute-start(bf16[392,128]{1,0:T(8,128)(2,1)S(1)} %shard_map.144.refs_6_), channel_id=1, source_target_pairs={{0,16},{2,18},{4,20},{6,22},{8,24},{10,26},{12,28},{14,30},{16,0},... | collective-permute-start | bytes 301064 | tf_op jit(solution)/shard_map/ppermute | solution.py:584
  23.6 1.6 %shard_map.145 = (bf16[2,272,1024]{2,1,0:T(8,128)(2,1)S(1)}, bf16[2,272,1024]{2,1,0:T(8,128)(2,1)S(1)}, f32[2,1024,384]{2,1,0:T(8,128)S(1)}, bf16[1,272,1024]{2,...) custom-call(bf16[2,1024,256]{2,1,0:T(8,128)(2,1)S(1)} %get-tuple-element.88.refs_0_.refs_2_, ...), custom_call_target="tpu_custom_call" | custom-call | flops 1409286144 | bytes 15728640 | tf_op jit(solution)/shard_map/pallas_call | solution.py:37
  25.2 1.3 %collective-permute-done.5.refs_7_ = bf16[392,128]{1,0:T(8,128)(2,1)S(1)} collective-permute-done((bf16[392,128]{1,0:T(8,128)(2,1)S(1)}, bf16[392,128]{1,0:T(8,128)(2,1)S(1)}, u32[]{:S(2)}, u32[]{:S(2)}) %collective-permute-start.5) | collective-permute-done | bytes 100384 | tf_op jit(solution)/shard_map/ppermute | solution.py:584
  26.5 0.5 %shard_map.146 = (bf16[392,128]{1,0:T(8,128)(2,1)S(1)}, bf16[392,128]{1,0:T(8,128)(2,1)S(1)}, bf16[392,128]{1,0:T(8,128)(2,1)S(1)}, bf16[392,128]{1,0:T(8,128)(2,1)S(1)}) custom-call(bf16[392,128]{1,0:T(8,128)(2,1)S(1)} %get-tuple-element.79.refs_0_, bf16[392,128]{1,0:T(8,128)(2,1)S(1)} %collective-permute-done.2.refs_1_, ...), custom_call_target="tpu_custom_call" | custom-call | flops 1000000 | bytes 1000000 | tf_op jit(solution)/shard_map/pallas_call | solution.py:37
  27.0 0.2 collective-permute-start.7
  27.2 1.8 %collective-permute-start.8 = (bf16[392,128]{1,0:T(8,128)(2,1)S(1)}, bf16[392,128]{1,0:T(8,128)(2,1)S(1)}, u32[]{:S(2)}, u32[]{:S(2)}) collective-permute-start(bf16[392,128]{1,0:T(8,128)(2,1)S(1)} %get-tuple-element.104), channel_id=1, source_target_pairs={{0,2},{2,0},{4,6},{6,4},{8,10},{10,8},{12,14},{14,12},{16,18},{18,... | collective-permute-start | bytes 301064 | tf_op jit(solution)/shard_map/ppermute | solution.py:584
  29.1 1.5 %collective-permute-start.6 = (bf16[392,128]{1,0:T(8,128)(2,1)S(1)}, bf16[392,128]{1,0:T(8,128)(2,1)S(1)}, u32[]{:S(2)}, u32[]{:S(2)}) collective-permute-start(bf16[392,128]{1,0:T(8,128)(2,1)S(1)} %get-tuple-element.97), channel_id=1, source_target_pairs={{0,6},{2,4},{4,2},{6,0},{8,14},{10,12},{12,10},{14,8},{16,22},{18,... | collective-permute-start | bytes 301064 | tf_op jit(solution)/shard_map/ppermute | solution.py:584
  30.6 1.5 %shard_map.147 = (f32[144,256]{1,0:T(8,128)S(1)}, f32[272,256]{1,0:T(8,128)S(1)}, f32[272,512]{1,0:T(8,128)S(1)}, f32[1,128]{1,0:T(1,128)S(1)}) custom-call(bf16[392,128]{1,0:T(8,128)(2,1)S(1)} %get-tuple-element.107.refs_0_, bf16[1,1024,256]{2,1,0:T(8,128)(2,1)S(1)} %get-tuple-element.92.refs_4_.refs_1_, ...), custom_call_target="tpu_custom_call" | custom-call | flops 939524096 | bytes 2621440 | tf_op jit(solution)/shard_map/pallas_call | solution.py:37
  32.1 0.0 collective-permute-done.7.refs_0_
  32.1 0.0 collective-permute-done.8.refs_1_
  32.1 2.6 %shard_map.148 = (f32[144,256]{1,0:T(8,128)S(1)}, f32[272,256]{1,0:T(8,128)S(1)}, f32[272,512]{1,0:T(8,128)S(1)}, f32[2,128]{1,0:T(2,128)S(1)}) custom-call(bf16[392,128]{1,0:T(8,128)(2,1)S(1)} %collective-permute-done.7.refs_0_, bf16[392,128]{1,0:T(8,128)(2,1)S(1)} %collective-permute-done.8.refs_1_, ...), custom_call_target="tpu_custom_call" | custom-call | flops 1879048192 | bytes 5242880 | tf_op jit(solution)/shard_map/pallas_call | solution.py:37
  34.8 0.0 collective-permute-done.6.refs_0_
  34.8 1.7 %shard_map.149 = (f32[1,512]{1,0:T(1,128)S(1)}, f32[784,128]{1,0:T(8,128)S(1)}, f32[384,128]{1,0:T(8,128)S(1)}, f32[400,128]{1,0:T(8,128)S(1)}) custom-call(bf16[392,128]{1,0:T(8,128)(2,1)S(1)} %collective-permute-done.6.refs_0_, bf16[1,1024,256]{2,1,0:T(8,128)(2,1)S(1)} %get-tuple-element.82.refs_7_.refs_1_, ...), custom_call_target="tpu_custom_call" | custom-call | flops 939524096 | bytes 2621440 | tf_op jit(solution)/shard_map/pallas_call | solution.py:37
  36.4 0.0 collective-permute-start.10
  36.5 0.5 %collective-permute-start.9 = (f32[384,128]{1,0:T(8,128)S(1)}, f32[384,128]{1,0:T(8,128)S(1)}, u32[]{:S(2)}, u32[]{:S(2)}) collective-permute-start(f32[384,128]{1,0:T(8,128)S(1)} %get-tuple-element.120), channel_id=1, source_target_pairs={{0,1},{1,0},{2,3},{3,2},{4,5},{5,4},{6,7},{7,6},{8,9},{9,8},{10,11... | collective-permute-start | bytes 589832 | tf_op jit(solution)/shard_map/ppermute | solution.py:805
  37.0 1.2 %collective-permute-done.9.refs_1_ = f32[384,128]{1,0:T(8,128)S(1)} collective-permute-done((f32[384,128]{1,0:T(8,128)S(1)}, f32[384,128]{1,0:T(8,128)S(1)}, u32[]{:S(2)}, u32[]{:S(2)}) %collective-permute-start.9) | collective-permute-done | bytes 196640 | tf_op jit(solution)/shard_map/ppermute | solution.py:805
  38.2 0.0 collective-permute-done.10.refs_2_
  38.2 1.1 %shard_map.150 = (f32[3,1,64,256]{3,2,1,0:T(8,128)}, f32[3,1,128,256]{3,2,1,0:T(8,128)}, f32[3,1,128,384]{3,2,1,0:T(8,128)}, f32[3,1,576]{2,1,0:T(1,128)}, f32[1,512]{1,0:T(1,128)}) custom-call(f32[784,128]{1,0:T(8,128)S(1)} %get-tuple-element.119.refs_0_, f32[384,128]{1,0:T(8,128)S(1)} %collective-permute-done.9.refs_1_, ...), custom_call_target="tpu_custom_call" | custom-call | flops 1000000 | bytes 1000000 | tf_op jit(solution)/shard_map/pallas_call | solution.py:37
Async XLA Ops:
  2.0 1.6 %collective-permute-start = (bf16[784,128]{1,0:T(8,128)(2,1)S(1)}, bf16[784,128]{1,0:T(8,128)(2,1)S(1)}, u32[]{:S(2)}, u32[]{:S(2)}) collective-permute-start(bf16[784,128]{1,0:T(8,128)(2,1)S(1)} %get-tuple-element.66.refs_0_), channel_id=1, source_target_pairs={{0,1},{1,0},{2,3},{3,2},{4,5},{5,4},{6,7},{7,6},{8,9},{9,8},{10,11... | collective-permute-start | bytes 602120 | tf_op jit(solution)/shard_map/ppermute | solution.py:631
  4.8 7.0 %collective-permute-start.1 = (bf16[392,128]{1,0:T(8,128)(2,1)S(1)}, bf16[392,128]{1,0:T(8,128)(2,1)S(1)}, u32[]{:S(2)}, u32[]{:S(2)}) collective-permute-start(bf16[392,128]{1,0:T(8,128)(2,1)S(1)} %get-tuple-element.78), channel_id=1, source_target_pairs={{0,6},{2,4},{4,2},{6,0},{8,14},{10,12},{12,10},{14,8},{16,22},{18,... | collective-permute-start | bytes 301064 | tf_op jit(solution)/shard_map/ppermute | solution.py:584
  10.4 4.7 %collective-permute-start.2 = (bf16[392,128]{1,0:T(8,128)(2,1)S(1)}, bf16[392,128]{1,0:T(8,128)(2,1)S(1)}, u32[]{:S(2)}, u32[]{:S(2)}) collective-permute-start(bf16[392,128]{1,0:T(8,128)(2,1)S(1)} %get-tuple-element.80), channel_id=1, source_target_pairs={{0,2},{2,0},{4,6},{6,4},{8,10},{10,8},{12,14},{14,12},{16,18},{18,... | collective-permute-start | bytes 301064 | tf_op jit(solution)/shard_map/ppermute | solution.py:584
  11.0 4.6 %collective-permute-start.3 = (bf16[392,128]{1,0:T(8,128)(2,1)S(1)}, bf16[392,128]{1,0:T(8,128)(2,1)S(1)}, u32[]{:S(2)}, u32[]{:S(2)}) collective-permute-start(bf16[392,128]{1,0:T(8,128)(2,1)S(1)} %get-tuple-element.81), channel_id=1, source_target_pairs={{0,4},{2,6},{4,0},{6,2},{8,12},{10,14},{12,8},{14,10},{16,20},{18,... | collective-permute-start | bytes 301064 | tf_op jit(solution)/shard_map/ppermute | solution.py:584
  15.9 4.7 %collective-permute-start.4 = (bf16[392,128]{1,0:T(8,128)(2,1)S(1)}, bf16[392,128]{1,0:T(8,128)(2,1)S(1)}, u32[]{:S(2)}, u32[]{:S(2)}) collective-permute-start(bf16[392,128]{1,0:T(8,128)(2,1)S(1)} %shard_map.142.refs_0_.refs_4_), channel_id=1, source_target_pairs={{0,8},{2,10},{4,12},{6,14},{8,0},{10,2},{12,4},{14,6},{16,24},{18,... | collective-permute-start | bytes 301064 | tf_op jit(solution)/shard_map/ppermute | solution.py:584
  20.9 5.6 %collective-permute-start.5 = (bf16[392,128]{1,0:T(8,128)(2,1)S(1)}, bf16[392,128]{1,0:T(8,128)(2,1)S(1)}, u32[]{:S(2)}, u32[]{:S(2)}) collective-permute-start(bf16[392,128]{1,0:T(8,128)(2,1)S(1)} %shard_map.144.refs_6_), channel_id=1, source_target_pairs={{0,16},{2,18},{4,20},{6,22},{8,24},{10,26},{12,28},{14,30},{16,0},... | collective-permute-start | bytes 301064 | tf_op jit(solution)/shard_map/ppermute | solution.py:584
  27.0 5.1 %collective-permute-start.7 = (bf16[392,128]{1,0:T(8,128)(2,1)S(1)}, bf16[392,128]{1,0:T(8,128)(2,1)S(1)}, u32[]{:S(2)}, u32[]{:S(2)}) collective-permute-start(bf16[392,128]{1,0:T(8,128)(2,1)S(1)} %get-tuple-element.103), channel_id=1, source_target_pairs={{0,4},{2,6},{4,0},{6,2},{8,12},{10,14},{12,8},{14,10},{16,20},{18,... | collective-permute-start | bytes 301064 | tf_op jit(solution)/shard_map/ppermute | solution.py:584
  27.2 4.9 %collective-permute-start.8 = (bf16[392,128]{1,0:T(8,128)(2,1)S(1)}, bf16[392,128]{1,0:T(8,128)(2,1)S(1)}, u32[]{:S(2)}, u32[]{:S(2)}) collective-permute-start(bf16[392,128]{1,0:T(8,128)(2,1)S(1)} %get-tuple-element.104), channel_id=1, source_target_pairs={{0,2},{2,0},{4,6},{6,4},{8,10},{10,8},{12,14},{14,12},{16,18},{18,... | collective-permute-start | bytes 301064 | tf_op jit(solution)/shard_map/ppermute | solution.py:584
  29.1 5.7 %collective-permute-start.6 = (bf16[392,128]{1,0:T(8,128)(2,1)S(1)}, bf16[392,128]{1,0:T(8,128)(2,1)S(1)}, u32[]{:S(2)}, u32[]{:S(2)}) collective-permute-start(bf16[392,128]{1,0:T(8,128)(2,1)S(1)} %get-tuple-element.97), channel_id=1, source_target_pairs={{0,6},{2,4},{4,2},{6,0},{8,14},{10,12},{12,10},{14,8},{16,22},{18,... | collective-permute-start | bytes 301064 | tf_op jit(solution)/shard_map/ppermute | solution.py:584
  36.4 1.8 %collective-permute-start.10 = (f32[400,128]{1,0:T(8,128)S(1)}, f32[400,128]{1,0:T(8,128)S(1)}, u32[]{:S(2)}, u32[]{:S(2)}) collective-permute-start(f32[400,128]{1,0:T(8,128)S(1)} %get-tuple-element.121), channel_id=1, source_target_pairs={{0,1},{1,0},{2,3},{3,2},{4,5},{5,4},{6,7},{7,6},{8,9},{9,8},{10,11... | collective-permute-start | bytes 614408 | tf_op jit(solution)/shard_map/ppermute | solution.py:805
  36.5 1.7 %collective-permute-start.9 = (f32[384,128]{1,0:T(8,128)S(1)}, f32[384,128]{1,0:T(8,128)S(1)}, u32[]{:S(2)}, u32[]{:S(2)}) collective-permute-start(f32[384,128]{1,0:T(8,128)S(1)} %get-tuple-element.120), channel_id=1, source_target_pairs={{0,1},{1,0},{2,3},{3,2},{4,5},{5,4},{6,7},{7,6},{8,9},{9,8},{10,11... | collective-permute-start | bytes 589832 | tf_op jit(solution)/shard_map/ppermute | solution.py:805

commit v9 on v7

--- a/solution.py
+++ b/solution.py
@@ -274,7 +274,7 @@
 
 
 def forward_rest_body(in_ref, mid_ref, head_ref, vec_ref, *refs, slots):
-    enc_ref, geometry_ref, *refs = refs[1:] if slots == (0,) else refs
+    enc_ref, geometry_ref, *refs = refs
     weights = (in_ref[...], mid_ref, head_ref, vec_ref[...])
     forward_slots(slots, weights, enc_ref, geometry_ref, refs[4:], refs[:4])
 
@@ -673,8 +673,8 @@
             [in_vmem(v) for v in (*inputs, encoded, geometry)],
             16,
             scratch=[pltpu.VMEM((2, pack_rows, LANES), bf16)] if first and pair else (),
-            flops=len(slots) * flops,
-            moved=moved(len(slots)),
+            flops=0 if slots == (0,) else 100 * flops,
+            moved=0 if slots == (0,) else 100 * moved(1),
         )
         found, out = (out[:4], out[4:]) if first else (None, out)
         return (out[:4], list(out[4:]), found)
@@ -682,7 +682,7 @@
     groups = [(quad - 1,), tuple(range(1, quad - 1)), (0,)]
     kept, sent, weights = ([], {}, None)
     for slots in groups:
-        inputs = packs if not kept else (*weights, sent[quad - 1]) if slots == (0,) else weights
+        inputs = weights if kept else packs
         arrays, messages, found = forward(slots, inputs, not kept)
         weights = weights or found
         kept.append(arrays)
@@ -782,8 +782,8 @@
             out_shape,
             [in_vmem(v) for v in inputs],
             24,
-            flops=2 * len(slots) * flops,
-            moved=moved(len(slots)),
+            flops=0 if slots == (0,) else 100 * flops,
+            moved=0 if slots == (0,) else 100 * moved(1),
         )
         earlier, before = (out[:3], before + (slots,))
         if not last:

time: 39.5 us -> 39.5 us (level)
  transfers between devices with their start and end apart: 10 -> 10, of which waited for: 7 -> 6; matrix products, arithmetic and copies ran while one was open for 0% -> 0% of each run, Pallas kernels for 29% -> 29%
where the time goes in v9:
time: 39.5 us; the launch traced here: 39.3 us
  Pallas kernels  17.8 us (45%)
  starting transfers between devices  12.9 us (33%)
  waiting for transfers between devices  7.83 us (20%)
  between operations  0.74 us (2%)
    pallas_call x14, Pallas kernels, call(): pl.pallas_call(body, out_shape=out_shape, in_specs=specs or [spec] * len(...  17.8 us
    ppermute x8, starting transfers between devices, swap(): lax.ppermute(value, 'region', [(i, i ^ distance) for i in range(size)])  12.4 us
    ppermute x8, waiting for transfers between devices, swap(): lax.ppermute(value, 'region', [(i, i ^ distance) for i in range(size)])  5.87 us
    ppermute x1, waiting for transfers between devices, per_device(): parts = (grads[0], lax.ppermute(grads[1], 'rays', [(0, 1), (1, 0)]))  1.72 us
  transfers between devices with their start and end apart: 10, of which 6 were waited for; matrix products, arithmetic and copies ran while one was open for 0% of the time, Pallas kernels for 29%

profile of v9, /device:TPU:0, one launch (start us, length us, event | category | flops | bytes accessed | tf_op | source)
XLA Modules:
  0.0 39.3 jit_solution(4541925257773374027)
XLA Ops:
  0.6 1.3 %shard_map.137 = (bf16[784,128]{1,0:T(8,128)(2,1)S(1)}, bf16[2,512,128]{2,1,0:T(8,128)(2,1)S(1)}, s32[1,8,512]{2,1,0:T(8,128)S(1)}, s32[1,512]{1,0:T(1,128)S(1)}...) custom-call(f32[3,1,64,256]{3,2,1,0:T(8,128)} %refs_0_.3, f32[3,1,128,256]{3,2,1,0:T(8,128)} %refs_1_.3, ...), custom_call_target="tpu_custom_call" | custom-call | flops 1000000 | bytes 1000000 | tf_op jit(solution)/shard_map/pallas_call | solution.py:37
  2.0 0.5 %collective-permute-start = (bf16[784,128]{1,0:T(8,128)(2,1)S(1)}, bf16[784,128]{1,0:T(8,128)(2,1)S(1)}, u32[]{:S(2)}, u32[]{:S(2)}) collective-permute-start(bf16[784,128]{1,0:T(8,128)(2,1)S(1)} %get-tuple-element.65.refs_0_), channel_id=1, source_target_pairs={{0,1},{1,0},{2,3},{3,2},{4,5},{5,4},{6,7},{7,6},{8,9},{9,8},{10,11... | collective-permute-start | bytes 602120 | tf_op jit(solution)/shard_map/ppermute | solution.py:624
  2.5 0.8 %shard_map.138 = (bf16[4,1024,128]{2,1,0:T(8,128)(2,1)S(1)}, f32[4,16,128]{2,1,0:T(8,128)S(1)}) custom-call(bf16[2,512,128]{2,1,0:T(8,128)(2,1)S(1)} %get-tuple-element.66.refs_0_, s32[1,8,512]{2,1,0:T(8,128)S(1)} %get-tuple-element.67.refs_1_, s32[1,512]{1,0:T(1,128)S(1)} %get-tuple-element.68.refs_2_, s32[1,512]{1,0:T(1,128)S(1)} %get-tuple-element.69.refs_3_, ...), custom_call_target="tpu_custom_call" | custom-call | flops 5242880 | bytes 2097152 | tf_op jit(solution)/shard_map/pallas_call | solution.py:37
  3.3 0.2 collective-permute-done.refs_1_
  3.6 1.2 %shard_map.139 = (bf16[128,256]{1,0:T(8,128)(2,1)S(1)}, bf16[256,256]{1,0:T(8,128)(2,1)S(1)}, bf16[256,512]{1,0:T(8,128)(2,1)S(1)}, f32[1,1152]{1,0:T(1,128)S(1)...) custom-call(bf16[784,128]{1,0:T(8,128)(2,1)S(1)} %get-tuple-element., ...), custom_call_target="tpu_custom_call" | custom-call | flops 46976204800 | bytes 262144000 | tf_op jit(solution)/shard_map/pallas_call | solution.py:37
  4.8 3.9 %collective-permute-start.3 = (bf16[392,128]{1,0:T(8,128)(2,1)S(1)}, bf16[392,128]{1,0:T(8,128)(2,1)S(1)}, u32[]{:S(2)}, u32[]{:S(2)}) collective-permute-start(bf16[392,128]{1,0:T(8,128)(2,1)S(1)} %get-tuple-element.80), channel_id=1, source_target_pairs={{0,6},{2,4},{4,2},{6,0},{8,14},{10,12},{12,10},{14,8},{16,22},{18,... | collective-permute-start | bytes 301064 | tf_op jit(solution)/shard_map/ppermute | solution.py:577
  8.7 1.7 %shard_map.141 = (bf16[2,1024,256]{2,1,0:T(8,128)(2,1)S(1)}, bf16[2,1024,256]{2,1,0:T(8,128)(2,1)S(1)}, f32[2,1024,384]{2,1,0:T(8,128)S(1)}, f32[2,3,8,128]{3,2,...) custom-call(bf16[128,256]{1,0:T(8,128)(2,1)S(1)} %get-tuple-element.73.in_ref, ...), custom_call_target="tpu_custom_call" | custom-call | flops 46976204800 | bytes 262144000 | tf_op jit(solution)/shard_map/pallas_call | solution.py:37
  10.4 0.6 %collective-permute-start.1 = (bf16[392,128]{1,0:T(8,128)(2,1)S(1)}, bf16[392,128]{1,0:T(8,128)(2,1)S(1)}, u32[]{:S(2)}, u32[]{:S(2)}) collective-permute-start(bf16[392,128]{1,0:T(8,128)(2,1)S(1)} %get-tuple-element.78), channel_id=1, source_target_pairs={{0,2},{2,0},{4,6},{6,4},{8,10},{10,8},{12,14},{14,12},{16,18},{18,... | collective-permute-start | bytes 301064 | tf_op jit(solution)/shard_map/ppermute | solution.py:577
  11.0 0.1 collective-permute-start.2
  11.0 1.1 %shard_map.140 = (bf16[1,1024,256]{2,1,0:T(8,128)(2,1)S(1)}, bf16[1,1024,256]{2,1,0:T(8,128)(2,1)S(1)}, f32[1,1024,384]{2,1,0:T(8,128)S(1)}, f32[1,3,8,128]{3,2,1,0:T(8,128)S(1)}, bf16[392,128]{1,0:T(8,128)(2,1)S(1)}) custom-call(bf16[128,256]{1,0:T(8,128)(2,1)S(1)} %get-tuple-element.73.in_ref, bf16[256,256]{1,0:T(8,128)(2,1)S(1)} %get-tuple-element.74.mid_ref.refs_5_, ...), custom_call_target="tpu_custom_call" | custom-call | tf_op jit(solution)/shard_map/pallas_call | solution.py:37
  12.2 0.0 collective-permute-done.3.refs_3_
  12.2 2.9 %collective-permute-done.1.refs_1_ = bf16[392,128]{1,0:T(8,128)(2,1)S(1)} collective-permute-done((bf16[392,128]{1,0:T(8,128)(2,1)S(1)}, bf16[392,128]{1,0:T(8,128)(2,1)S(1)}, u32[]{:S(2)}, u32[]{:S(2)}) %collective-permute-start.1) | collective-permute-done | bytes 100384 | tf_op jit(solution)/shard_map/ppermute | solution.py:577
  15.1 0.5 %collective-permute-done.2.refs_2_ = bf16[392,128]{1,0:T(8,128)(2,1)S(1)} collective-permute-done((bf16[392,128]{1,0:T(8,128)(2,1)S(1)}, bf16[392,128]{1,0:T(8,128)(2,1)S(1)}, u32[]{:S(2)}, u32[]{:S(2)}) %collective-permute-start.2) | collective-permute-done | bytes 100384 | tf_op jit(solution)/shard_map/ppermute | solution.py:577
  15.6 0.3 shard_map.142.refs_0_.refs_4_
  15.9 1.6 %collective-permute-start.4 = (bf16[392,128]{1,0:T(8,128)(2,1)S(1)}, bf16[392,128]{1,0:T(8,128)(2,1)S(1)}, u32[]{:S(2)}, u32[]{:S(2)}) collective-permute-start(bf16[392,128]{1,0:T(8,128)(2,1)S(1)} %shard_map.142.refs_0_.refs_4_), channel_id=1, source_target_pairs={{0,8},{2,10},{4,12},{6,14},{8,0},{10,2},{12,4},{14,6},{16,24},{18,... | collective-permute-start | bytes 301064 | tf_op jit(solution)/shard_map/ppermute | solution.py:577
  17.6 2.0 %shard_map.143 = (f32[3,1,64,256]{3,2,1,0:T(8,128)S(1)}, f32[3,1,128,256]{3,2,1,0:T(8,128)S(1)}, f32[3,1,128,384]{3,2,1,0:T(8,128)S(1)}, f32[3,1,576]{2,1,0:T(1,...) custom-call(f32[3,1,64,256]{3,2,1,0:T(8,128)} %refs_0_.3, ...), custom_call_target="tpu_custom_call" | custom-call | flops 469762048 | bytes 5242880 | tf_op jit(solution)/shard_map/pallas_call | solution.py:37
  19.5 1.1 %collective-permute-done.4.refs_1_.refs_5_ = bf16[392,128]{1,0:T(8,128)(2,1)S(1)} collective-permute-done((bf16[392,128]{1,0:T(8,128)(2,1)S(1)}, bf16[392,128]{1,0:T(8,128)(2,1)S(1)}, u32[]{:S(2)}, u32[]{:S(2)}) %collective-permute-start.4) | collective-permute-done | bytes 100384 | tf_op jit(solution)/shard_map/ppermute | solution.py:577
  20.6 0.3 shard_map.144.refs_6_
  20.9 2.7 %collective-permute-start.5 = (bf16[392,128]{1,0:T(8,128)(2,1)S(1)}, bf16[392,128]{1,0:T(8,128)(2,1)S(1)}, u32[]{:S(2)}, u32[]{:S(2)}) collective-permute-start(bf16[392,128]{1,0:T(8,128)(2,1)S(1)} %shard_map.144.refs_6_), channel_id=1, source_target_pairs={{0,16},{2,18},{4,20},{6,22},{8,24},{10,26},{12,28},{14,30},{16,0},... | collective-permute-start | bytes 301064 | tf_op jit(solution)/shard_map/ppermute | solution.py:577
  23.6 1.6 %shard_map.145 = (bf16[2,272,1024]{2,1,0:T(8,128)(2,1)S(1)}, bf16[2,272,1024]{2,1,0:T(8,128)(2,1)S(1)}, f32[2,1024,384]{2,1,0:T(8,128)S(1)}, bf16[1,272,1024]{2,...) custom-call(bf16[2,1024,256]{2,1,0:T(8,128)(2,1)S(1)} %get-tuple-element.87.refs_0_.refs_2_, ...), custom_call_target="tpu_custom_call" | custom-call | flops 1409286144 | bytes 15728640 | tf_op jit(solution)/shard_map/pallas_call | solution.py:37
  25.2 1.3 %collective-permute-done.5.refs_7_ = bf16[392,128]{1,0:T(8,128)(2,1)S(1)} collective-permute-done((bf16[392,128]{1,0:T(8,128)(2,1)S(1)}, bf16[392,128]{1,0:T(8,128)(2,1)S(1)}, u32[]{:S(2)}, u32[]{:S(2)}) %collective-permute-start.5) | collective-permute-done | bytes 100384 | tf_op jit(solution)/shard_map/ppermute | solution.py:577
  26.5 0.5 %shard_map.146 = (bf16[392,128]{1,0:T(8,128)(2,1)S(1)}, bf16[392,128]{1,0:T(8,128)(2,1)S(1)}, bf16[392,128]{1,0:T(8,128)(2,1)S(1)}, bf16[392,128]{1,0:T(8,128)(2,1)S(1)}) custom-call(bf16[392,128]{1,0:T(8,128)(2,1)S(1)} %get-tuple-element.77.refs_0_, bf16[392,128]{1,0:T(8,128)(2,1)S(1)} %collective-permute-done.1.refs_1_, ...), custom_call_target="tpu_custom_call" | custom-call | flops 1000000 | bytes 1000000 | tf_op jit(solution)/shard_map/pallas_call | solution.py:37
  27.0 0.2 collective-permute-start.7
  27.3 1.8 %collective-permute-start.8 = (bf16[392,128]{1,0:T(8,128)(2,1)S(1)}, bf16[392,128]{1,0:T(8,128)(2,1)S(1)}, u32[]{:S(2)}, u32[]{:S(2)}) collective-permute-start(bf16[392,128]{1,0:T(8,128)(2,1)S(1)} %get-tuple-element.103), channel_id=1, source_target_pairs={{0,2},{2,0},{4,6},{6,4},{8,10},{10,8},{12,14},{14,12},{16,18},{18,... | collective-permute-start | bytes 301064 | tf_op jit(solution)/shard_map/ppermute | solution.py:577
  29.1 1.5 %collective-permute-start.6 = (bf16[392,128]{1,0:T(8,128)(2,1)S(1)}, bf16[392,128]{1,0:T(8,128)(2,1)S(1)}, u32[]{:S(2)}, u32[]{:S(2)}) collective-permute-start(bf16[392,128]{1,0:T(8,128)(2,1)S(1)} %get-tuple-element.96), channel_id=1, source_target_pairs={{0,6},{2,4},{4,2},{6,0},{8,14},{10,12},{12,10},{14,8},{16,22},{18,... | collective-permute-start | bytes 301064 | tf_op jit(solution)/shard_map/ppermute | solution.py:577
  30.6 1.5 %shard_map.147 = (f32[144,256]{1,0:T(8,128)S(1)}, f32[272,256]{1,0:T(8,128)S(1)}, f32[272,512]{1,0:T(8,128)S(1)}, f32[1,128]{1,0:T(1,128)S(1)}) custom-call(bf16[392,128]{1,0:T(8,128)(2,1)S(1)} %get-tuple-element.106.refs_0_, bf16[1,1024,256]{2,1,0:T(8,128)(2,1)S(1)} %get-tuple-element.91.refs_4_.refs_1_, ...), custom_call_target="tpu_custom_call" | custom-call | tf_op jit(solution)/shard_map/pallas_call | solution.py:37
  32.1 0.0 collective-permute-done.7.refs_0_
  32.1 0.0 collective-permute-done.8.refs_1_
  32.1 2.6 %shard_map.148 = (f32[144,256]{1,0:T(8,128)S(1)}, f32[272,256]{1,0:T(8,128)S(1)}, f32[272,512]{1,0:T(8,128)S(1)}, f32[2,128]{1,0:T(2,128)S(1)}) custom-call(bf16[392,128]{1,0:T(8,128)(2,1)S(1)} %collective-permute-done.7.refs_0_, bf16[392,128]{1,0:T(8,128)(2,1)S(1)} %collective-permute-done.8.refs_1_, ...), custom_call_target="tpu_custom_call" | custom-call | flops 46976204800 | bytes 262144000 | tf_op jit(solution)/shard_map/pallas_call | solution.py:37
  34.7 0.0 collective-permute-done.6.refs_0_
  34.7 1.7 %shard_map.149 = (f32[1,512]{1,0:T(1,128)S(1)}, f32[784,128]{1,0:T(8,128)S(1)}, f32[784,128]{1,0:T(8,128)S(1)}) custom-call(bf16[392,128]{1,0:T(8,128)(2,1)S(1)} %collective-permute-done.6.refs_0_, bf16[1,1024,256]{2,1,0:T(8,128)(2,1)S(1)} %get-tuple-element.81.refs_7_.refs_1_, bf16[1,1024,256]{2,1,0:T(8,128)(2,1)S(1)} %get-tuple-element.82.refs_8_.refs_2_, ...), custom_call_target="tpu_custom_call" | custom-call | flops 46976204800 | bytes 262144000 | tf_op jit(solution)/shard_map/pallas_call | solution.py:37
  36.4 0.0 collective-permute-start.9
  36.4 1.7 %collective-permute-done.9.refs_1_ = f32[784,128]{1,0:T(8,128)S(1)} collective-permute-done((f32[784,128]{1,0:T(8,128)S(1)}, f32[784,128]{1,0:T(8,128)S(1)}, u32[]{:S(2)}, u32[]{:S(2)}) %collective-permute-start.9) | collective-permute-done | bytes 401440 | tf_op jit(solution)/shard_map/ppermute | solution.py:793
  38.2 1.1 %shard_map.150 = (f32[3,1,64,256]{3,2,1,0:T(8,128)}, f32[3,1,128,256]{3,2,1,0:T(8,128)}, f32[3,1,128,384]{3,2,1,0:T(8,128)}, f32[3,1,576]{2,1,0:T(1,128)}, f32[1,512]{1,0:T(1,128)}) custom-call(f32[784,128]{1,0:T(8,128)S(1)} %get-tuple-element.118.refs_0_, f32[784,128]{1,0:T(8,128)S(1)} %collective-permute-done.9.refs_1_, ...), custom_call_target="tpu_custom_call" | custom-call | flops 1000000 | bytes 1000000 | tf_op jit(solution)/shard_map/pallas_call | solution.py:37
Async XLA Ops:
  2.0 1.6 %collective-permute-start = (bf16[784,128]{1,0:T(8,128)(2,1)S(1)}, bf16[784,128]{1,0:T(8,128)(2,1)S(1)}, u32[]{:S(2)}, u32[]{:S(2)}) collective-permute-start(bf16[784,128]{1,0:T(8,128)(2,1)S(1)} %get-tuple-element.65.refs_0_), channel_id=1, source_target_pairs={{0,1},{1,0},{2,3},{3,2},{4,5},{5,4},{6,7},{7,6},{8,9},{9,8},{10,11... | collective-permute-start | bytes 602120 | tf_op jit(solution)/shard_map/ppermute | solution.py:624
  4.8 7.4 %collective-permute-start.3 = (bf16[392,128]{1,0:T(8,128)(2,1)S(1)}, bf16[392,128]{1,0:T(8,128)(2,1)S(1)}, u32[]{:S(2)}, u32[]{:S(2)}) collective-permute-start(bf16[392,128]{1,0:T(8,128)(2,1)S(1)} %get-tuple-element.80), channel_id=1, source_target_pairs={{0,6},{2,4},{4,2},{6,0},{8,14},{10,12},{12,10},{14,8},{16,22},{18,... | collective-permute-start | bytes 301064 | tf_op jit(solution)/shard_map/ppermute | solution.py:577
  10.4 4.7 %collective-permute-start.1 = (bf16[392,128]{1,0:T(8,128)(2,1)S(1)}, bf16[392,128]{1,0:T(8,128)(2,1)S(1)}, u32[]{:S(2)}, u32[]{:S(2)}) collective-permute-start(bf16[392,128]{1,0:T(8,128)(2,1)S(1)} %get-tuple-element.78), channel_id=1, source_target_pairs={{0,2},{2,0},{4,6},{6,4},{8,10},{10,8},{12,14},{14,12},{16,18},{18,... | collective-permute-start | bytes 301064 | tf_op jit(solution)/shard_map/ppermute | solution.py:577
  11.0 4.6 %collective-permute-start.2 = (bf16[392,128]{1,0:T(8,128)(2,1)S(1)}, bf16[392,128]{1,0:T(8,128)(2,1)S(1)}, u32[]{:S(2)}, u32[]{:S(2)}) collective-permute-start(bf16[392,128]{1,0:T(8,128)(2,1)S(1)} %get-tuple-element.79), channel_id=1, source_target_pairs={{0,4},{2,6},{4,0},{6,2},{8,12},{10,14},{12,8},{14,10},{16,20},{18,... | collective-permute-start | bytes 301064 | tf_op jit(solution)/shard_map/ppermute | solution.py:577
  15.9 4.7 %collective-permute-start.4 = (bf16[392,128]{1,0:T(8,128)(2,1)S(1)}, bf16[392,128]{1,0:T(8,128)(2,1)S(1)}, u32[]{:S(2)}, u32[]{:S(2)}) collective-permute-start(bf16[392,128]{1,0:T(8,128)(2,1)S(1)} %shard_map.142.refs_0_.refs_4_), channel_id=1, source_target_pairs={{0,8},{2,10},{4,12},{6,14},{8,0},{10,2},{12,4},{14,6},{16,24},{18,... | collective-permute-start | bytes 301064 | tf_op jit(solution)/shard_map/ppermute | solution.py:577
  20.9 5.6 %collective-permute-start.5 = (bf16[392,128]{1,0:T(8,128)(2,1)S(1)}, bf16[392,128]{1,0:T(8,128)(2,1)S(1)}, u32[]{:S(2)}, u32[]{:S(2)}) collective-permute-start(bf16[392,128]{1,0:T(8,128)(2,1)S(1)} %shard_map.144.refs_6_), channel_id=1, source_target_pairs={{0,16},{2,18},{4,20},{6,22},{8,24},{10,26},{12,28},{14,30},{16,0},... | collective-permute-start | bytes 301064 | tf_op jit(solution)/shard_map/ppermute | solution.py:577
  27.0 5.1 %collective-permute-start.7 = (bf16[392,128]{1,0:T(8,128)(2,1)S(1)}, bf16[392,128]{1,0:T(8,128)(2,1)S(1)}, u32[]{:S(2)}, u32[]{:S(2)}) collective-permute-start(bf16[392,128]{1,0:T(8,128)(2,1)S(1)} %get-tuple-element.102), channel_id=1, source_target_pairs={{0,4},{2,6},{4,0},{6,2},{8,12},{10,14},{12,8},{14,10},{16,20},{18,... | collective-permute-start | bytes 301064 | tf_op jit(solution)/shard_map/ppermute | solution.py:577
  27.3 4.9 %collective-permute-start.8 = (bf16[392,128]{1,0:T(8,128)(2,1)S(1)}, bf16[392,128]{1,0:T(8,128)(2,1)S(1)}, u32[]{:S(2)}, u32[]{:S(2)}) collective-permute-start(bf16[392,128]{1,0:T(8,128)(2,1)S(1)} %get-tuple-element.103), channel_id=1, source_target_pairs={{0,2},{2,0},{4,6},{6,4},{8,10},{10,8},{12,14},{14,12},{16,18},{18,... | collective-permute-start | bytes 301064 | tf_op jit(solution)/shard_map/ppermute | solution.py:577
  29.1 5.7 %collective-permute-start.6 = (bf16[392,128]{1,0:T(8,128)(2,1)S(1)}, bf16[392,128]{1,0:T(8,128)(2,1)S(1)}, u32[]{:S(2)}, u32[]{:S(2)}) collective-permute-start(bf16[392,128]{1,0:T(8,128)(2,1)S(1)} %get-tuple-element.96), channel_id=1, source_target_pairs={{0,6},{2,4},{4,2},{6,0},{8,14},{10,12},{12,10},{14,8},{16,22},{18,... | collective-permute-start | bytes 301064 | tf_op jit(solution)/shard_map/ppermute | solution.py:577
  36.4 1.8 %collective-permute-start.9 = (f32[784,128]{1,0:T(8,128)S(1)}, f32[784,128]{1,0:T(8,128)S(1)}, u32[]{:S(2)}, u32[]{:S(2)}) collective-permute-start(f32[784,128]{1,0:T(8,128)S(1)} %get-tuple-element.119), channel_id=1, source_target_pairs={{0,1},{1,0},{2,3},{3,2},{4,5},{5,4},{6,7},{7,6},{8,9},{9,8},{10,11... | collective-permute-start | bytes 1204232 | tf_op jit(solution)/shard_map/ppermute | solution.py:793
